TPU v7x, 256 devices: a whole 4x4x8 slice. The times are simulated.
256 devices in a mesh: group: 8 (over x, core), band: 32 (over z, y).
Axes of the slice: x: 4, y: 4, z: 8, core: 2. Of those that a mesh axis runs over, the one named last changes fastest.
Arguments:
- base_latents: bfloat16 [2048, 32, 16, 128], P(('group', 'band')), may hold values from -41 to 41
- clip_lengths: int32 [8, 4], replicated, may hold values from 17 to 81, as said below
- clip_group: int32 [8, 4], replicated, may hold values from 0 to 7, as said below
- conv_weight: bfloat16 [3, 3, 128, 128], replicated, may hold values from -0.1875 to 0.1875
- w_qkv: bfloat16 [128, 384], replicated, may hold values from -0.5 to 0.5
- query_gain: float32 [128], replicated, may hold values from 0.5 to 90
- w_out: bfloat16 [128, 128], replicated, may hold values from -1.5 to 1.5
- w_up: bfloat16 [128, 512], replicated, may hold values from -0.5 to 0.5
- w_down: bfloat16 [512, 128], replicated, may hold values from -0.25 to 0.25
Outputs:
- refined: bfloat16 [8, 768, 32, 16, 128], P('group', 'band')
Inputs may be any that keep to these rules, and one draw needn't show every extreme that they name: `clip_lengths`: row p lists the frame counts of base pool p's clips in the order of its frames; every row sums to 256 and holds one clip of exactly 81 frames. `clip_group`: the groups in one row are distinct, and one SR group receives a 81-frame clip from every pool.
All inputs are finite; a program needn't handle non-finite values.
Results may differ from a plain program's by a relative error of at most 0.013.
The roundings to bfloat16 on the way count: a program that leaves them out, or rounds other values in their place, can miss the bound.
Values may be sent and summed in bfloat16 or wider, within the bound.
No kernel may reach another device: no remote copies, remote signals or barrier semaphores. Data moves between devices by JAX's collectives and lax.ppermute only.
A program may use at most 64 MiB of HBM per device.

v0:
```python
import jax
import jax.numpy as jnp
from jax import lax
from jax.sharding import PartitionSpec as P

HEADS = 8
HEAD_DIM = 16
LMAX = 81


EPS = 1e-06


def rms_scale(values, reduce_axis):
    return values * lax.rsqrt(jnp.mean(values * values, axis=reduce_axis, keepdims=True) + EPS)


def head_layout(tensor, frames, pixels):
    return (
        tensor.reshape(frames, pixels, HEADS, HEAD_DIM)
        .transpose(0, 3, 1, 2)
        .reshape(frames, HEAD_DIM, pixels * HEADS)
    )


def channel_layout(tensor, frames, pixels):
    return (
        tensor.reshape(frames, HEAD_DIM, pixels, HEADS)
        .transpose(0, 2, 3, 1)
        .reshape(frames, pixels, HEADS * HEAD_DIM)
    )


def attend(queries, key_rows, values, allowed):
    scores = jnp.einsum(
        "adm,bdm->abm", queries, key_rows, preferred_element_type=jnp.float32
    ) * HEAD_DIM ** (-0.5)
    scores = jnp.where(allowed[:, :, None], scores, -1e30)
    row_top = jnp.max(scores, axis=1, keepdims=True)
    weights = jnp.exp(scores - row_top)
    weights = (weights / jnp.sum(weights, axis=1, keepdims=True)).astype(jnp.bfloat16)
    return jnp.einsum("abm,bdm->adm", weights, values, preferred_element_type=jnp.float32).astype(
        jnp.bfloat16
    )


def refine(slab, allowed, weight_set):
    w_qkv, query_gain, w_out, w_up, w_down = weight_set
    frames, pixels, channels = slab.shape
    slab_wide = slab.astype(jnp.float32).reshape(-1, channels)
    normed = rms_scale(slab_wide, -1).astype(jnp.bfloat16)
    projected = jnp.dot(normed, w_qkv, preferred_element_type=jnp.float32).astype(jnp.bfloat16)
    projected = projected.reshape(frames, pixels, 3 * channels)
    gain_map = jnp.tile(query_gain.reshape(HEADS, HEAD_DIM).T, (1, pixels))
    queries = (
        rms_scale(head_layout(projected[:, :, :channels], frames, pixels).astype(jnp.float32), 1)
        * gain_map
    )
    queries = queries.astype(jnp.bfloat16)
    key_heads = rms_scale(
        head_layout(projected[:, :, channels : 2 * channels], frames, pixels).astype(jnp.float32), 1
    )
    key_heads = key_heads.astype(jnp.bfloat16)
    value_heads = head_layout(projected[:, :, 2 * channels :], frames, pixels)
    mixed = attend(queries, key_heads, value_heads, allowed)
    mixed = channel_layout(mixed, frames, pixels).reshape(-1, channels)
    middle = (slab_wide + jnp.dot(mixed, w_out, preferred_element_type=jnp.float32)).astype(
        jnp.bfloat16
    )
    mlp_input = rms_scale(middle.astype(jnp.float32), -1).astype(jnp.bfloat16)
    lifted = jax.nn.silu(jnp.dot(mlp_input, w_up, preferred_element_type=jnp.float32)).astype(
        jnp.bfloat16
    )
    result = middle.astype(jnp.float32) + jnp.dot(
        lifted, w_down, preferred_element_type=jnp.float32
    )
    return result.astype(jnp.bfloat16).reshape(frames, pixels, channels)


def body(
    base_latents, clip_lengths, clip_group, conv_weight, w_qkv, query_gain, w_out, w_up, w_down
):
    groups = lax.axis_size("group")
    bands = lax.axis_size("band")
    frames_dev, tile_rows, tile_cols, channels = base_latents.shape
    latent_wide = base_latents.astype(jnp.float32)
    normed = jax.nn.silu(rms_scale(latent_wide, -1)).astype(jnp.bfloat16)
    convolved = lax.conv_general_dilated(
        normed,
        conv_weight,
        (1, 1),
        "SAME",
        dimension_numbers=("NHWC", "HWIO", "NHWC"),
        preferred_element_type=jnp.float32,
    )
    hidden = (latent_wide + convolved).astype(jnp.bfloat16)
    pencil = lax.all_to_all(hidden, "band", split_axis=1, concat_axis=0, tiled=True)
    pool_frames = pencil.shape[0]
    band_rows = pencil.shape[1]
    pencil = pencil.reshape(pool_frames, band_rows * tile_cols, channels)
    weight_set = (w_qkv, query_gain, w_out, w_up, w_down)
    slot_pad = bands * -(-LMAX // bands)
    pad_index = jnp.arange(slot_pad, dtype=jnp.int32)
    slot_index = jnp.arange(LMAX, dtype=jnp.int32)
    source_pool = lax.axis_index("group")
    lengths = lax.dynamic_index_in_dim(clip_lengths, source_pool, 0, keepdims=False)
    targets = lax.dynamic_index_in_dim(clip_group, source_pool, 0, keepdims=False)
    starts = jnp.cumsum(lengths) - lengths
    matched = targets[None, :] == jnp.arange(groups, dtype=jnp.int32)[:, None]
    seg_start = jnp.sum(jnp.where(matched, starts[None, :], 0), axis=1)
    seg_len = jnp.sum(jnp.where(matched, lengths[None, :], 0), axis=1)
    sent_live = pad_index[:, None] < seg_len[None, :]
    picked_rows = jnp.where(sent_live, seg_start[None, :] + pad_index[:, None], 0).reshape(-1)
    my_group = lax.axis_index("group")
    owned = clip_group == my_group
    got_len = jnp.sum(jnp.where(owned, clip_lengths, 0), axis=1)
    got_live = slot_index[None, :] < got_len[:, None]
    chosen = jnp.take(pencil, picked_rows, axis=0).reshape(slot_pad, groups, -1, channels)
    by_source = jnp.moveaxis(
        lax.all_to_all(
            jnp.where(sent_live[:, :, None, None], chosen, jnp.zeros((), pencil.dtype)),
            "group",
            split_axis=1,
            concat_axis=1,
            tiled=True,
        ),
        1,
        0,
    )[:, :LMAX]

    def per_source(paired):
        rows_in, live_slots = paired
        allowed = jnp.broadcast_to(live_slots[None, :], (LMAX, LMAX))
        result = refine(rows_in, allowed, weight_set)
        return jnp.where(live_slots[:, None, None], result, jnp.zeros((), jnp.bfloat16))

    results = lax.map(per_source, (by_source, got_live))
    tail = jnp.zeros((groups, slot_pad - LMAX) + results.shape[2:], jnp.bfloat16)
    arrived = jnp.moveaxis(jnp.concatenate([results, tail], axis=1), 0, 1)
    returned = lax.all_to_all(arrived, "band", split_axis=0, concat_axis=2, tiled=True)
    slot_band = returned.shape[0] * returned.shape[1]
    return returned.reshape(slot_band, band_rows * bands, tile_cols, channels)[None]


def solution(mesh):
    placed = (P(("group", "band"), None, None, None), P(), P(), P(), P(), P(), P(), P(), P())
    return jax.shard_map(
        body,
        mesh=mesh,
        in_specs=placed,
        out_specs=P("group", "band", None, None, None),
        check_vma=False,
    )
```

profile of v0, /device:TPU:1, one launch (start us, length us, event | category | flops | bytes accessed | tf_op | source)
XLA Modules:
  0.0 379.6 jit_solution(9760430145220689998)
XLA Ops:
  2.1 5.5 %fusion.29 = bf16[8,32,16,128]{3,0,2,1:T(8,128)(2,1)} fusion(bf16[3,3,128,128]{3,2,1,0:T(8,128)(2,1)S(1)} %copy-done, f32[8,32,16]{0,2,1:T(8,128)S(1)} %add_rsqrt_fusion.2, bf16[8,32,16,128]{3,2,1,0:T(8,128)(2,1)} %param.11), kind=kOutput, calls=%fused_computation.57 | convolution fusion | flops 1138753536 | bytes 2408448 | tf_op jit(solution)/shard_map/conv_general_dilated | solution.py:88
  7.6 12.0 %all-to-all-start = ((bf16[8,32,16,128]{3,0,2,1:T(8,128)(2,1)}), bf16[8,32,16,128]{3,0,2,1:T(8,128)(2,1)S(1)}, u32[]{:S(2)}, u32[]{:S(2)}) async-start(bf16[8,32,16,128]{3,0,2,1:T(8,128)(2,1)} %fusion.29), calls=%async_computation | async-start | bytes 2097152 | tf_op jit(solution)/shard_map/all_to_all | solution.py:97
  20.3 25.5 %all-to-all-done = bf16[8,32,16,128]{3,0,2,1:T(8,128)(2,1)S(1)} async-done(((bf16[8,32,16,128]{3,0,2,1:T(8,128)(2,1)}), bf16[8,32,16,128]{3,0,2,1:T(8,128)(2,1)S(1)}, u32[]{:S(2)}, u32[]{:S(2)}) %all-to-all-start) | async-done | bytes 1048608 | tf_op jit(solution)/shard_map/all_to_all | solution.py:97
  49.6 5.5 %select_select_fusion = bf16[96,8,16,128]{3,2,1,0:T(8,128)(2,1)S(1)} fusion(bf16[96,8,16,128]{3,2,1,0:T(8,128)(2,1)} %bitcast.130, pred[96,8]{1,0:T(8,128)(4,1)S(1)} %get-tuple-element.94, pred[96,8]{1,0:T(8,128)(4,1)S(1)} %get-tuple-element.93), kind=kLoop, calls=%fused_computation.46 | loop fusion | flops 3145728 | bytes 6292992 | tf_op jit(solution)/shard_map/jit(_where)/select_n | solution.py:121
  57.3 7.1 %all-to-all-start.1 = ((bf16[96,8,16,128]{3,2,0,1:T(8,128)(2,1)}), bf16[96,8,16,128]{3,2,0,1:T(8,128)(2,1)S(1)}, u32[]{:S(2)}, u32[]{:S(2)}) async-start(bf16[96,8,16,128]{3,2,0,1:T(8,128)(2,1)} %copy.32), calls=%async_computation.1 | async-start | bytes 6291456 | tf_op jit(solution)/shard_map/all_to_all | solution.py:120
  64.5 37.5 %all-to-all-done.1 = bf16[96,8,16,128]{3,2,0,1:T(8,128)(2,1)S(1)} async-done(((bf16[96,8,16,128]{3,2,0,1:T(8,128)(2,1)}), bf16[96,8,16,128]{3,2,0,1:T(8,128)(2,1)S(1)}, u32[]{:S(2)}, u32[]{:S(2)}) %all-to-all-start.1) | async-done | bytes 3145760 | tf_op jit(solution)/shard_map/all_to_all | solution.py:120
  105.9 192.4 %while.10 = (s32[]{:T(128)}, bf16[8,81,16,128]{3,2,0,1:T(8,128)(2,1)}, pred[8,81]{1,0:T(8,128)(4,1)S(1)}, bf16[8,81,16,128]{3,2,1,0:T(8,128)(2,1)S(1)}, bf16[128...) while((s32[]{:T(128)}, ...), condition=%wide.region_12.13_spmd, body=%wide.region_5.12_spmd.sunk | while | flops 577375872 | bytes 45419632 | solution.py:137
  109.3 4.5 %fusion.68 = (f32[81,128]{0,1:T(8,128)S(1)}, f32[81,81,128]{0,1,2:T(8,128)}) fusion(pred[81]{0:T(512)(128)(4,1)S(1)} %dynamic-slice_bitcast_fusion.2, f32[81,16,128]{0,1,2:T(8,128)S(1)} %bitcast.124, f32[81,128]{0,1:T(8,128)S(1)} %get-tuple-element.164, f32[81,16,128]{0,1,2:T(8,128)S(1)} %bitcast.125, f32[16,128]{0,1:T(8,128)S(1)} %broadcast_bitcast_fusion.2, ...), kind=kOutput, calls=%fused_computation.80.clone.1 | convolution fusion | flops 31062608 | bytes 4819025 | tf_op jit(solution)/shard_map/while/body/eval_jaxpr/sub | solution.py:40
  114.1 4.4 %fusion.69 = bf16[128,16,81]{2,1,0:T(8,128)(2,1)} fusion(bf16[81,16,128]{0,1,2:T(8,128)(2,1)S(1)} %bitcast.128, f32[81,81,128]{0,1,2:T(8,128)} %get-tuple-element.166, f32[81,128]{0,1:T(8,128)S(1)} %get-tuple-element.167), kind=kOutput, calls=%fused_computation.19.clone.1 | convolution fusion | flops 28719360 | bytes 4064256 | tf_op jit(solution)/shard_map/while/body/eval_jaxpr/abm,bdm->adm/dot_general | solution.py:42
  133.4 4.5 %fusion.68 = (f32[81,128]{0,1:T(8,128)S(1)}, f32[81,81,128]{0,1,2:T(8,128)}) fusion(pred[81]{0:T(512)(128)(4,1)S(1)} %dynamic-slice_bitcast_fusion.2, f32[81,16,128]{0,1,2:T(8,128)S(1)} %bitcast.124, f32[81,128]{0,1:T(8,128)S(1)} %get-tuple-element.164, f32[81,16,128]{0,1,2:T(8,128)S(1)} %bitcast.125, f32[16,128]{0,1:T(8,128)S(1)} %broadcast_bitcast_fusion.2, ...), kind=kOutput, calls=%fused_computation.80.clone.1 | convolution fusion | flops 31062608 | bytes 4819025 | tf_op jit(solution)/shard_map/while/body/eval_jaxpr/sub | solution.py:40
  138.2 4.4 %fusion.69 = bf16[128,16,81]{2,1,0:T(8,128)(2,1)} fusion(bf16[81,16,128]{0,1,2:T(8,128)(2,1)S(1)} %bitcast.128, f32[81,81,128]{0,1,2:T(8,128)} %get-tuple-element.166, f32[81,128]{0,1:T(8,128)S(1)} %get-tuple-element.167), kind=kOutput, calls=%fused_computation.19.clone.1 | convolution fusion | flops 28719360 | bytes 4064256 | tf_op jit(solution)/shard_map/while/body/eval_jaxpr/abm,bdm->adm/dot_general | solution.py:42
  157.4 4.5 %fusion.68 = (f32[81,128]{0,1:T(8,128)S(1)}, f32[81,81,128]{0,1,2:T(8,128)}) fusion(pred[81]{0:T(512)(128)(4,1)S(1)} %dynamic-slice_bitcast_fusion.2, f32[81,16,128]{0,1,2:T(8,128)S(1)} %bitcast.124, f32[81,128]{0,1:T(8,128)S(1)} %get-tuple-element.164, f32[81,16,128]{0,1,2:T(8,128)S(1)} %bitcast.125, f32[16,128]{0,1:T(8,128)S(1)} %broadcast_bitcast_fusion.2, ...), kind=kOutput, calls=%fused_computation.80.clone.1 | convolution fusion | flops 31062608 | bytes 4819025 | tf_op jit(solution)/shard_map/while/body/eval_jaxpr/sub | solution.py:40
  162.3 4.4 %fusion.69 = bf16[128,16,81]{2,1,0:T(8,128)(2,1)} fusion(bf16[81,16,128]{0,1,2:T(8,128)(2,1)S(1)} %bitcast.128, f32[81,81,128]{0,1,2:T(8,128)} %get-tuple-element.166, f32[81,128]{0,1:T(8,128)S(1)} %get-tuple-element.167), kind=kOutput, calls=%fused_computation.19.clone.1 | convolution fusion | flops 28719360 | bytes 4064256 | tf_op jit(solution)/shard_map/while/body/eval_jaxpr/abm,bdm->adm/dot_general | solution.py:42
  181.5 4.5 %fusion.68 = (f32[81,128]{0,1:T(8,128)S(1)}, f32[81,81,128]{0,1,2:T(8,128)}) fusion(pred[81]{0:T(512)(128)(4,1)S(1)} %dynamic-slice_bitcast_fusion.2, f32[81,16,128]{0,1,2:T(8,128)S(1)} %bitcast.124, f32[81,128]{0,1:T(8,128)S(1)} %get-tuple-element.164, f32[81,16,128]{0,1,2:T(8,128)S(1)} %bitcast.125, f32[16,128]{0,1:T(8,128)S(1)} %broadcast_bitcast_fusion.2, ...), kind=kOutput, calls=%fused_computation.80.clone.1 | convolution fusion | flops 31062608 | bytes 4819025 | tf_op jit(solution)/shard_map/while/body/eval_jaxpr/sub | solution.py:40
  186.3 4.4 %fusion.69 = bf16[128,16,81]{2,1,0:T(8,128)(2,1)} fusion(bf16[81,16,128]{0,1,2:T(8,128)(2,1)S(1)} %bitcast.128, f32[81,81,128]{0,1,2:T(8,128)} %get-tuple-element.166, f32[81,128]{0,1:T(8,128)S(1)} %get-tuple-element.167), kind=kOutput, calls=%fused_computation.19.clone.1 | convolution fusion | flops 28719360 | bytes 4064256 | tf_op jit(solution)/shard_map/while/body/eval_jaxpr/abm,bdm->adm/dot_general | solution.py:42
  205.5 4.5 %fusion.68 = (f32[81,128]{0,1:T(8,128)S(1)}, f32[81,81,128]{0,1,2:T(8,128)}) fusion(pred[81]{0:T(512)(128)(4,1)S(1)} %dynamic-slice_bitcast_fusion.2, f32[81,16,128]{0,1,2:T(8,128)S(1)} %bitcast.124, f32[81,128]{0,1:T(8,128)S(1)} %get-tuple-element.164, f32[81,16,128]{0,1,2:T(8,128)S(1)} %bitcast.125, f32[16,128]{0,1:T(8,128)S(1)} %broadcast_bitcast_fusion.2, ...), kind=kOutput, calls=%fused_computation.80.clone.1 | convolution fusion | flops 31062608 | bytes 4819025 | tf_op jit(solution)/shard_map/while/body/eval_jaxpr/sub | solution.py:40
  210.4 4.4 %fusion.69 = bf16[128,16,81]{2,1,0:T(8,128)(2,1)} fusion(bf16[81,16,128]{0,1,2:T(8,128)(2,1)S(1)} %bitcast.128, f32[81,81,128]{0,1,2:T(8,128)} %get-tuple-element.166, f32[81,128]{0,1:T(8,128)S(1)} %get-tuple-element.167), kind=kOutput, calls=%fused_computation.19.clone.1 | convolution fusion | flops 28719360 | bytes 4064256 | tf_op jit(solution)/shard_map/while/body/eval_jaxpr/abm,bdm->adm/dot_general | solution.py:42
  229.6 4.5 %fusion.68 = (f32[81,128]{0,1:T(8,128)S(1)}, f32[81,81,128]{0,1,2:T(8,128)}) fusion(pred[81]{0:T(512)(128)(4,1)S(1)} %dynamic-slice_bitcast_fusion.2, f32[81,16,128]{0,1,2:T(8,128)S(1)} %bitcast.124, f32[81,128]{0,1:T(8,128)S(1)} %get-tuple-element.164, f32[81,16,128]{0,1,2:T(8,128)S(1)} %bitcast.125, f32[16,128]{0,1:T(8,128)S(1)} %broadcast_bitcast_fusion.2, ...), kind=kOutput, calls=%fused_computation.80.clone.1 | convolution fusion | flops 31062608 | bytes 4819025 | tf_op jit(solution)/shard_map/while/body/eval_jaxpr/sub | solution.py:40
  234.4 4.4 %fusion.69 = bf16[128,16,81]{2,1,0:T(8,128)(2,1)} fusion(bf16[81,16,128]{0,1,2:T(8,128)(2,1)S(1)} %bitcast.128, f32[81,81,128]{0,1,2:T(8,128)} %get-tuple-element.166, f32[81,128]{0,1:T(8,128)S(1)} %get-tuple-element.167), kind=kOutput, calls=%fused_computation.19.clone.1 | convolution fusion | flops 28719360 | bytes 4064256 | tf_op jit(solution)/shard_map/while/body/eval_jaxpr/abm,bdm->adm/dot_general | solution.py:42
  253.6 4.5 %fusion.68 = (f32[81,128]{0,1:T(8,128)S(1)}, f32[81,81,128]{0,1,2:T(8,128)}) fusion(pred[81]{0:T(512)(128)(4,1)S(1)} %dynamic-slice_bitcast_fusion.2, f32[81,16,128]{0,1,2:T(8,128)S(1)} %bitcast.124, f32[81,128]{0,1:T(8,128)S(1)} %get-tuple-element.164, f32[81,16,128]{0,1,2:T(8,128)S(1)} %bitcast.125, f32[16,128]{0,1:T(8,128)S(1)} %broadcast_bitcast_fusion.2, ...), kind=kOutput, calls=%fused_computation.80.clone.1 | convolution fusion | flops 31062608 | bytes 4819025 | tf_op jit(solution)/shard_map/while/body/eval_jaxpr/sub | solution.py:40
  258.5 4.4 %fusion.69 = bf16[128,16,81]{2,1,0:T(8,128)(2,1)} fusion(bf16[81,16,128]{0,1,2:T(8,128)(2,1)S(1)} %bitcast.128, f32[81,81,128]{0,1,2:T(8,128)} %get-tuple-element.166, f32[81,128]{0,1:T(8,128)S(1)} %get-tuple-element.167), kind=kOutput, calls=%fused_computation.19.clone.1 | convolution fusion | flops 28719360 | bytes 4064256 | tf_op jit(solution)/shard_map/while/body/eval_jaxpr/abm,bdm->adm/dot_general | solution.py:42
  277.6 4.5 %fusion.68 = (f32[81,128]{0,1:T(8,128)S(1)}, f32[81,81,128]{0,1,2:T(8,128)}) fusion(pred[81]{0:T(512)(128)(4,1)S(1)} %dynamic-slice_bitcast_fusion.2, f32[81,16,128]{0,1,2:T(8,128)S(1)} %bitcast.124, f32[81,128]{0,1:T(8,128)S(1)} %get-tuple-element.164, f32[81,16,128]{0,1,2:T(8,128)S(1)} %bitcast.125, f32[16,128]{0,1:T(8,128)S(1)} %broadcast_bitcast_fusion.2, ...), kind=kOutput, calls=%fused_computation.80.clone.1 | convolution fusion | flops 31062608 | bytes 4819025 | tf_op jit(solution)/shard_map/while/body/eval_jaxpr/sub | solution.py:40
  282.5 4.4 %fusion.69 = bf16[128,16,81]{2,1,0:T(8,128)(2,1)} fusion(bf16[81,16,128]{0,1,2:T(8,128)(2,1)S(1)} %bitcast.128, f32[81,81,128]{0,1,2:T(8,128)} %get-tuple-element.166, f32[81,128]{0,1:T(8,128)S(1)} %get-tuple-element.167), kind=kOutput, calls=%fused_computation.19.clone.1 | convolution fusion | flops 28719360 | bytes 4064256 | tf_op jit(solution)/shard_map/while/body/eval_jaxpr/abm,bdm->adm/dot_general | solution.py:42
  301.1 76.0 %all_to_all.35 = bf16[96,8,16,128]{3,2,1,0:T(8,128)(2,1)S(1)} all-to-all(bf16[96,8,16,128]{3,2,1,0:T(8,128)(2,1)S(1)} %pad_bitcast_fusion), channel_id=1, replica_groups=mesh['group'=8,'band'=32] {'band'}, dimensions={0} | all-to-all | bytes 6291456 | tf_op jit(solution)/shard_map/all_to_all | solution.py:140
  (258 shorter events, 138.2 us)
Async XLA Ops:
  0.0 2.1 copy-start
  2.1 17.5 %copy-start.7 = (s32[8,4]{0,1:T(4,128)S(1)}, s32[8,4]{0,1:T(4,128)}, u32[]{:S(2)}) copy-start(s32[8,4]{0,1:T(4,128)} %param.12) | copy-start | bytes 388
  2.1 17.5 %copy-start.8 = (s32[8,4]{0,1:T(4,128)S(1)}, s32[8,4]{0,1:T(4,128)}, u32[]{:S(2)}) copy-start(s32[8,4]{0,1:T(4,128)} %param.13) | copy-start | bytes 388
  7.6 38.3 %all-to-all-start = ((bf16[8,32,16,128]{3,0,2,1:T(8,128)(2,1)}), bf16[8,32,16,128]{3,0,2,1:T(8,128)(2,1)S(1)}, u32[]{:S(2)}, u32[]{:S(2)}) async-start(bf16[8,32,16,128]{3,0,2,1:T(8,128)(2,1)} %fusion.29), calls=%async_computation | async-start | bytes 2097152 | tf_op jit(solution)/shard_map/all_to_all | solution.py:97
  57.3 44.7 %all-to-all-start.1 = ((bf16[96,8,16,128]{3,2,0,1:T(8,128)(2,1)}), bf16[96,8,16,128]{3,2,0,1:T(8,128)(2,1)S(1)}, u32[]{:S(2)}, u32[]{:S(2)}) async-start(bf16[96,8,16,128]{3,2,0,1:T(8,128)(2,1)} %copy.32), calls=%async_computation.1 | async-start | bytes 6291456 | tf_op jit(solution)/shard_map/all_to_all | solution.py:120
  102.0 1.7 copy-start.3
  103.7 2.3 copy-start.4
  103.7 2.3 copy-start.5
  103.7 2.3 copy-start.6
  105.9 1.5 copy-start.1
  126.4 3.6 copy-start.2
  130.0 1.5 copy-start.1
  150.5 3.6 copy-start.2
  154.1 1.5 copy-start.1
  174.5 3.6 copy-start.2
  178.1 1.5 copy-start.1
  198.6 3.6 copy-start.2
  202.2 1.5 copy-start.1
  222.6 3.6 copy-start.2
  226.2 1.5 copy-start.1
  246.7 3.6 copy-start.2
  270.7 3.6 copy-start.2
  274.3 1.5 copy-start.1
  294.8 3.6 copy-start.2
  (1 other events, 1.5 us)
where the time goes:
time: 383 us; the launch traced here: 380 us
  matrix products  111 us (29%)
  blocking collectives  76 us (20%)
  local copies, waits for them, and re-layouts  75.8 us (20%)
  waiting for transfers between devices  63 us (16%)
  other arithmetic  33.5 us (9%)
  starting transfers between devices  19.2 us (5%)
    all_to_all x1, blocking collectives, body(): lax.all_to_all(arrived, 'band', split_axis=0, concat_axis=2, tiled=True)  76 us
    all_to_all x1, waiting for transfers between devices, body(): lax.all_to_all(jnp.where(sent_live[:, :, None, None], chosen, jnp.zeros((...  37.5 us
    sub x8, matrix products, attend(): weights = jnp.exp(scores - row_top)  35.7 us
    dot_general x8, matrix products, attend(): jnp.einsum('abm,bdm->adm', weights, values, preferred_element_type=jnp.fl...  35.5 us
    reshape x8, local copies, waits for them, and re-layouts, channel_layout(): tensor.reshape(frames, HEAD_DIM, pixels, HEADS).transpose(0, 2, 3, 1)  31.3 us
    all_to_all x1, waiting for transfers between devices, body(): lax.all_to_all(hidden, 'band', split_axis=1, concat_axis=0, tiled=True)  25.5 us
    dot_general x8, matrix products, refine(): jnp.dot(lifted, w_down, preferred_element_type=jnp.float32)  21.3 us
    reshape x8, local copies, waits for them, and re-layouts, refine(): mixed = channel_layout(mixed, frames, pixels).reshape(-1, channels)  13.7 us
  transfers between devices with their start and end apart: 2, of which 2 were waited for; matrix products, arithmetic and copies ran while one was open for 0% of the time, Pallas kernels for 0%

commit v1 on v0

v1 whole, which is shorter than its diff:
```python
import functools

import jax
import jax.numpy as jnp
from jax import lax
from jax.experimental import pallas as pl
from jax.experimental.pallas import tpu as pltpu
from jax.sharding import PartitionSpec as P

HEADS = 8
HEAD_DIM = 16
LMAX = 81
EPS = 1e-6
C = 128
POOL = 256
REACH = 80
HALF = 128
KEYS = 208
FAR = -1e30
LOG2E = 1.4426950408889634
BF = jnp.bfloat16
F32 = jnp.float32


def square_parts(v):
    sq = v * v
    hi = sq.astype(BF)
    lo = (sq - hi.astype(F32)).astype(BF)
    return hi, lo


def attention_kernel(
    slots, starts, lens, x_ref, wk_ref, wqv_ref, gain_ref, wout_ref, wup_ref, wdown_ref, onehot_ref, far_ref,
    blockones_ref, out_ref, kaug, qbig, vaug, mixt, rows
):
    bands, flat, _ = x_ref.shape
    per_band = POOL // bands
    px = flat // per_band
    n2 = 2 * POOL
    kaug[:, C:] = onehot_ref[...]
    qbig[:C, :] = jnp.zeros((C, HEADS * n2), BF)
    qbig[C:, :] = far_ref[...]
    for pair in range(HEADS // 2):
        vaug[pair * 48 + 32 : pair * 48 + 48, :] = jnp.ones((16, n2), BF)

    def pixel_pair(pp, carry):
        both = x_ref[:, pl.ds(pl.multiple_of(pp * 16, 16), 16), :].astype(F32)
        xa = both[:, :per_band].reshape(POOL, C)
        xb = both[:, per_band:].reshape(POOL, C)
        x = jnp.concatenate([xa, xb], axis=0)
        n = (x * lax.rsqrt(jnp.mean(x * x, axis=-1, keepdims=True) + EPS)).astype(BF)
        k = jnp.dot(n, wk_ref[...], preferred_element_type=F32).astype(BF).astype(F32)
        ss = jnp.dot(
            jnp.concatenate(square_parts(k), axis=1), blockones_ref[...], preferred_element_type=F32
        )
        kaug[:, :C] = (k * lax.rsqrt(ss * (1.0 / HEAD_DIM) + EPS)).astype(BF)
        qv = lax.dot_general(
            wqv_ref[...], n, (((1,), (1,)), ((), ())), preferred_element_type=F32
        ).astype(BF)
        q = qv[:C].astype(F32).reshape(HEADS, HEAD_DIM, n2)
        qs = jnp.sum(q * q, axis=1, keepdims=True)
        q = (q * lax.rsqrt(qs * (1.0 / HEAD_DIM) + EPS)).reshape(C, n2) * gain_ref[...]
        q = q.astype(BF)
        for h in range(HEADS):
            head = slice(h * HEAD_DIM, (h + 1) * HEAD_DIM)
            for ib in range(4):
                lane = (ib * HEADS + h) * HALF
                qbig[head, lane : lane + HALF] = q[head, ib * HALF : (ib + 1) * HALF]
            pair, odd = h // 2, h % 2
            vaug[pair * 48 + odd * 16 : pair * 48 + odd * 16 + 16, :] = qv[C + h * HEAD_DIM : C + (h + 1) * HEAD_DIM]
        for i in range(2):
            for b in range(2):
                key0 = i * POOL + b * (POOL - KEYS)
                for pair in range(HEADS // 2):
                    lane = ((2 * i + b) * HEADS + 2 * pair) * HALF
                    s = jnp.dot(
                        kaug[key0 : key0 + KEYS, :],
                        qbig[:, lane : lane + 2 * HALF],
                        preferred_element_type=F32,
                    )
                    top = jnp.max(s, axis=0, keepdims=True)
                    e = jnp.exp2((s - top) * (LOG2E / 4)).astype(BF)
                    blank = jnp.zeros((POOL - KEYS, 2 * HALF), BF)
                    e = jnp.concatenate([e, blank] if b == 0 else [blank, e], axis=0)
                    o = jnp.dot(
                        vaug[pair * 48 : pair * 48 + 48, i * POOL : (i + 1) * POOL], e, preferred_element_type=F32
                    )
                    r = 1.0 / o[32:33]
                    lanes = slice(i * POOL + b * HALF, i * POOL + (b + 1) * HALF)
                    for odd in range(2):
                        part = o[odd * 16 : odd * 16 + 16, odd * HALF : (odd + 1) * HALF]
                        part = part * r[:, odd * HALF : (odd + 1) * HALF]
                        head = (2 * pair + odd) * HEAD_DIM
                        mixt[head : head + HEAD_DIM, lanes] = part.astype(BF)
        m = x + lax.dot_general(
            mixt[...], wout_ref[...], (((0,), (0,)), ((), ())), preferred_element_type=F32
        )
        m = m.astype(BF).astype(F32)
        n = (m * lax.rsqrt(jnp.mean(m * m, axis=-1, keepdims=True) + EPS)).astype(BF)
        up = jnp.dot(n, wup_ref[...], preferred_element_type=F32) * 0.5
        up = (up + up * jnp.tanh(up)).astype(BF)
        res = m + jnp.dot(up, wdown_ref[...], preferred_element_type=F32)
        for i in range(2):
            rows[pl.ds(2 * pp + i, POOL, stride=px), :] = res[i * POOL : (i + 1) * POOL]
        return carry

    lax.fori_loop(0, px // 2, pixel_pair, 0)

    clips = out_ref.shape[1] // slots

    def hand_out(b, carry):
        parts = []
        for c in range(clips):
            for jj in range(slots):
                j = b * slots + jj
                frame = jnp.minimum(starts[c] + j, POOL - 1)
                part = rows[pl.ds(pl.multiple_of(frame * px, px), px), :]
                parts.append(jnp.where(j < lens[c], part, 0.0))
        out_ref[b] = jnp.stack(parts, axis=0).astype(BF)
        return carry

    lax.fori_loop(0, bands, hand_out, 0)


def attention(x, starts, lens, w_qkv, query_gain, w_out, w_up, w_down, slots):
    bands, flat, _ = x.shape
    px = flat // (POOL // bands)
    n2 = 2 * POOL
    clips = starts.shape[0]
    frame = jnp.arange(POOL, dtype=jnp.int32)
    clip_of = jnp.sum((frame[:, None] >= starts[None, :]).astype(jnp.int32), axis=1) - 1
    lane = jnp.arange(C, dtype=jnp.int32)
    onehot = (clip_of[:, None] == lane[None, :]).astype(BF)
    onehot = jnp.concatenate([onehot, onehot], axis=0)
    apart = jnp.where((lane[:, None] < clips) & (lane[:, None] != clip_of[None, :]), FAR, 0.0).astype(BF)
    apart = jnp.broadcast_to(apart.reshape(C, 1, 2, 1, HALF), (C, 2, 2, HEADS, HALF)).reshape(C, HEADS * n2)
    blockones = (lane[:, None] // HEAD_DIM == lane[None, :] // HEAD_DIM).astype(BF)
    blockones = jnp.concatenate([blockones, blockones], axis=0)
    wqv = jnp.concatenate([w_qkv[:, :C].T, w_qkv[:, 2 * C :].T], axis=0)
    gain = jnp.broadcast_to(query_gain[:, None], (C, n2))
    vmem = pl.BlockSpec(memory_space=pltpu.VMEM)
    smem = pl.BlockSpec(memory_space=pltpu.SMEM)
    return pl.pallas_call(
        functools.partial(attention_kernel, slots),
        out_shape=jax.ShapeDtypeStruct((bands, clips * slots, px, C), BF),
        in_specs=[smem, smem] + [vmem] * 10,
        out_specs=vmem,
        scratch_shapes=[
            pltpu.VMEM((n2, 2 * C), BF),
            pltpu.VMEM((2 * C, HEADS * n2), BF),
            pltpu.VMEM((HEADS // 2 * 48, n2), BF),
            pltpu.VMEM((C, n2), BF),
            pltpu.VMEM((POOL * px, C), F32),
        ],
        compiler_params=pltpu.CompilerParams(vmem_limit_bytes=48 * 2**20),
        cost_estimate=pl.CostEstimate(
            flops=2 * POOL * px * C * 4000, bytes_accessed=4 * 2**20, transcendentals=POOL * px * HEADS * KEYS
        ),
        name="pool_attention",
    )(starts, lens, x, w_qkv[:, C : 2 * C], wqv, gain, w_out, w_up, w_down, onehot, apart, blockones)


CHUNKS = 2


def rms_scale(values, reduce_axis):
    return values * lax.rsqrt(jnp.mean(values * values, axis=reduce_axis, keepdims=True) + EPS)


def pack_kernel(slots, clip_of_group, y_ref, *out_refs):
    bands, _, px, _ = y_ref.shape
    groups = len(out_refs)
    for g in range(groups):
        c = clip_of_group[g]
        live = c >= 0
        for jj in range(slots):
            part = y_ref[:, jnp.maximum(c, 0) * slots + jj].astype(F32)
            part = jnp.where(live, part, 0.0).reshape(bands * px, C)
            out_refs[g][jj] = part.astype(BF)


def pack(y, clip_of_group, slots):
    groups = clip_of_group.shape[0]
    bands, _, px, _ = y.shape
    vmem = pl.BlockSpec(memory_space=pltpu.VMEM)
    return pl.pallas_call(
        functools.partial(pack_kernel, slots),
        out_shape=[jax.ShapeDtypeStruct((slots, bands * px, C), BF)] * groups,
        in_specs=[pl.BlockSpec(memory_space=pltpu.SMEM), vmem],
        out_specs=[vmem] * groups,
        compiler_params=pltpu.CompilerParams(vmem_limit_bytes=32 * 2**20),
        cost_estimate=pl.CostEstimate(flops=0, bytes_accessed=8 * 2**20, transcendentals=0),
        name="pack_slots",
    )(clip_of_group, y)


def place_kernel(groups, slots, chunks, me_ref, *refs):
    pieces, out_ref, sem = refs[: groups * chunks], refs[-2], refs[-1]
    chunk_px = pieces[0].shape[1]
    copies = []
    for chunk in range(chunks):
        for step in range(groups):
            source = lax.rem(me_ref[0] + groups - step, groups)
            for jj in range(slots):
                copies.append(
                    pltpu.make_async_copy(
                        pieces[chunk * groups + step].at[jj],
                        out_ref.at[jj * groups + source, pl.ds(chunk * chunk_px, chunk_px)],
                        sem.at[len(copies)],
                    )
                )
    for copy in copies:
        copy.start()
    for copy in copies:
        copy.wait()


def place(pieces, me, chunks):
    groups = len(pieces) // chunks
    slots, chunk_px, _ = pieces[0].shape
    vmem = pl.BlockSpec(memory_space=pltpu.VMEM)
    return pl.pallas_call(
        functools.partial(place_kernel, groups, slots, chunks),
        out_shape=jax.ShapeDtypeStruct((slots * groups, chunks * chunk_px, C), BF),
        in_specs=[pl.BlockSpec(memory_space=pltpu.SMEM)] + [vmem] * len(pieces),
        out_specs=pl.BlockSpec(memory_space=pl.ANY),
        scratch_shapes=[pltpu.SemaphoreType.DMA((len(pieces) * slots,))],
        compiler_params=pltpu.CompilerParams(vmem_limit_bytes=32 * 2**20),
        cost_estimate=pl.CostEstimate(flops=0, bytes_accessed=6 * 2**20, transcendentals=0),
        name="place_slots",
    )(me[None], *pieces)


def body(
    base_latents, clip_lengths, clip_group, conv_weight, w_qkv, query_gain, w_out, w_up, w_down
):
    groups = lax.axis_size("group")
    bands = lax.axis_size("band")
    frames_dev, tile_rows, tile_cols, channels = base_latents.shape
    latent_wide = base_latents.astype(jnp.float32)
    normed = jax.nn.silu(rms_scale(latent_wide, -1)).astype(jnp.bfloat16)
    convolved = lax.conv_general_dilated(
        normed,
        conv_weight,
        (1, 1),
        "SAME",
        dimension_numbers=("NHWC", "HWIO", "NHWC"),
        preferred_element_type=jnp.float32,
    )
    hidden = (latent_wide + convolved).astype(jnp.bfloat16)
    pixels = tile_rows * tile_cols
    px = pixels // bands // CHUNKS
    hidden = hidden.reshape(frames_dev, pixels, channels).transpose(1, 0, 2)
    hidden = hidden.reshape(CHUNKS, bands, px * frames_dev, channels)

    me = lax.axis_index("group")
    lengths = lax.dynamic_index_in_dim(clip_lengths, me, 0, keepdims=False)
    targets = lax.dynamic_index_in_dim(clip_group, me, 0, keepdims=False)
    starts = jnp.cumsum(lengths) - lengths
    slots = -(-LMAX // bands)
    aims = lax.rem(me + jnp.arange(groups, dtype=jnp.int32), groups)
    hit = targets[None, :] == aims[:, None]
    clip_of_group = jnp.where(
        jnp.any(hit, axis=1), jnp.argmax(hit, axis=1).astype(jnp.int32), -1
    )

    pieces = []
    for chunk in range(CHUNKS):
        pencil = lax.all_to_all(hidden[chunk], "band", split_axis=0, concat_axis=0, tiled=True)
        refined = attention(pencil, starts, lengths, w_qkv, query_gain, w_out, w_up, w_down, slots)
        arrived = lax.all_to_all(refined, "band", split_axis=0, concat_axis=0, tiled=True)
        packed = pack(arrived, clip_of_group, slots)
        for step in range(groups):
            ring = [(i, (i + step) % groups) for i in range(groups)]
            pieces.append(lax.ppermute(packed[step], "group", ring) if step else packed[step])
    placed = place(pieces, me, CHUNKS)
    return placed.reshape(1, slots * groups, tile_rows, tile_cols, channels)


def solution(mesh):
    placed = (P(("group", "band"), None, None, None), P(), P(), P(), P(), P(), P(), P(), P())
    return jax.shard_map(
        body,
        mesh=mesh,
        in_specs=placed,
        out_specs=P("group", "band", None, None, None),
        check_vma=False,
    )
```

time: 383 us -> 158 us (0.41)
  matrix products: 111 us -> 4.75 us
  blocking collectives: 76 us -> 0 us
  local copies, waits for them, and re-layouts: 75.8 us -> 2.3 us
  starting transfers between devices: 19.2 us -> 67.2 us
  Pallas kernels: 0 us -> 45.8 us
  other arithmetic: 33.5 us -> 3.51 us
  waiting for transfers between devices: 63 us -> 33.7 us
    all_to_all x1 -> x0, blocking collectives: 76 us -> none  [body(): lax.all_to_all(arrived, 'band', split_axis=0, concat_axis=2, tiled=True)]
    dot_general x32 -> x0, matrix products: 69.9 us -> none  [the longest x8 35.5 us: attend(): jnp.einsum('abm,bdm->adm', weights, values, preferred_element_type=jnp.fl...]
    pallas_call x0 -> x5, Pallas kernels: none -> 45.8 us  [the longest x2 41.7 us: attention(): pl.pallas_call(functools.partial(attention_kernel, slots), out_shape=jax....]
    reshape x24 -> x0, local copies, waits for them, and re-layouts: 45.6 us -> none  [the longest x8 31.3 us: channel_layout(): tensor.reshape(frames, HEAD_DIM, pixels, HEADS).transpose(0, 2, 3, 1)]
    all_to_all x2 -> x4, waiting for transfers between devices: 63 us -> 23.3 us  [the longest x2 15.4 us: body(): lax.all_to_all(hidden[chunk], 'band', split_axis=0, concat_axis=0, tiled=...]
    sub x8 -> x0, matrix products: 35.7 us -> none  [attend(): weights = jnp.exp(scores - row_top)]
    ppermute x0 -> x14, starting transfers between devices: none -> 31.6 us  [body(): lax.ppermute(packed[step], 'group', ring)]
    all_to_all x2 -> x4, starting transfers between devices: 19.2 us -> 35.6 us  [the longest x2 18.4 us: body(): lax.all_to_all(refined, 'band', split_axis=0, concat_axis=0, tiled=True)]
  transfers between devices with their start and end apart: 2 -> 18, of which waited for: 2 -> 6; matrix products, arithmetic and copies ran while one was open for 0% -> 2% of each run, Pallas kernels for 0% -> 28%
where the time goes in v1:
time: 158 us
  starting transfers between devices  67.2 us (43%)
  Pallas kernels  45.8 us (29%)
  waiting for transfers between devices  33.7 us (21%)
  matrix products  4.75 us (3%)
  other arithmetic  3.51 us (2%)
  local copies, waits for them, and re-layouts  2.3 us (1%)
    pallas_call x2, Pallas kernels, attention(): pl.pallas_call(functools.partial(attention_kernel, slots), out_shape=jax....  41.7 us
    ppermute x14, starting transfers between devices, body(): lax.ppermute(packed[step], 'group', ring)  31.6 us
    all_to_all x2, starting transfers between devices, body(): lax.all_to_all(refined, 'band', split_axis=0, concat_axis=0, tiled=True)  18.4 us
    all_to_all x2, starting transfers between devices, body(): lax.all_to_all(hidden[chunk], 'band', split_axis=0, concat_axis=0, tiled=...  17.2 us
    all_to_all x2, waiting for transfers between devices, body(): lax.all_to_all(hidden[chunk], 'band', split_axis=0, concat_axis=0, tiled=...  15.4 us
    ppermute x14, waiting for transfers between devices, body(): lax.ppermute(packed[step], 'group', ring)  10.4 us
    all_to_all x2, waiting for transfers between devices, body(): lax.all_to_all(refined, 'band', split_axis=0, concat_axis=0, tiled=True)  7.83 us
    conv_general_dilated x1, matrix products, body(): lax.conv_general_dilated(normed, conv_weight, (1, 1), 'SAME', dimension_n...  4.75 us
  transfers between devices with their start and end apart: 18, of which 6 were waited for; matrix products, arithmetic and copies ran while one was open for 2% of the time, Pallas kernels for 28%

profile of v1, /device:TPU:1, one launch (start us, length us, event | category | flops | bytes accessed | tf_op | source)
XLA Modules:
  0.0 157.8 jit_solution(14138646354074276435)
XLA Ops:
  0.0 2.0 %fusion.6 = f32[8,32,16]{0,2,1:T(8,128)S(1)} fusion(bf16[8,32,16,128]{3,2,1,0:T(8,128)(2,1)} %param.9), kind=kLoop, calls=%fused_computation.9 | loop fusion | flops 1568768 | bytes 1064960 | tf_op jit(solution)/shard_map/reduce_sum | solution.py:167
  2.1 4.8 %fusion.7 = bf16[8,32,16,128]{3,0,2,1:T(8,128)(2,1)S(1)} fusion(bf16[3,3,128,128]{3,2,1,0:T(8,128)(2,1)S(1)} %copy-done, f32[8,32,16]{0,2,1:T(8,128)S(1)} %add_rsqrt_fusion, bf16[8,32,16,128]{3,2,1,0:T(8,128)(2,1)} %param.9), kind=kOutput, calls=%fused_computation.10 | convolution fusion | flops 1138753536 | bytes 2408448 | tf_op jit(solution)/shard_map/conv_general_dilated | solution.py:242
  7.9 12.0 %all-to-all-start.2 = ((bf16[32,64,128]{2,1,0:T(8,128)(2,1)}), bf16[32,64,128]{2,1,0:T(8,128)(2,1)S(1)}, u32[]{:S(2)}, u32[]{:S(2)}) async-start(bf16[32,64,128]{2,1,0:T(8,128)(2,1)} %bitcast.13), calls=%async_computation.2 | async-start | bytes 1048576 | tf_op jit(solution)/shard_map/all_to_all | solution.py:269
  20.8 15.4 %all-to-all-done.2.x_ref = bf16[32,64,128]{2,1,0:T(8,128)(2,1)S(1)} async-done(((bf16[32,64,128]{2,1,0:T(8,128)(2,1)}), bf16[32,64,128]{2,1,0:T(8,128)(2,1)S(1)}, u32[]{:S(2)}, u32[]{:S(2)}) %all-to-all-start.2) | async-done | bytes 524320 | tf_op jit(solution)/shard_map/all_to_all | solution.py:269
  36.2 5.2 %all-to-all-start = ((bf16[32,64,128]{2,1,0:T(8,128)(2,1)}), bf16[32,64,128]{2,1,0:T(8,128)(2,1)S(1)}, u32[]{:S(2)}, u32[]{:S(2)}) async-start(bf16[32,64,128]{2,1,0:T(8,128)(2,1)} %bitcast.6), calls=%async_computation | async-start | bytes 1048576 | tf_op jit(solution)/shard_map/all_to_all | solution.py:269
  42.8 20.8 %pool_attention.3 = bf16[32,12,8,128]{3,2,1,0:T(8,128)(2,1)} custom-call(s32[4]{0:T(128)S(1)} %bitcast_subtract_fusion.1.starts, s32[4]{0:T(128)S(1)} %bitcast.31, bf16[32,64,128]{2,1,0:T(8,128)(2,1)S(1)} %all-to-all-done.2.x_ref, bf16[128,128]{1,0:T(8,128)(2,1)S(1)} %get-tuple-element.42.wk_ref, bf16[256,128]{1,0:T(8,128)(2,1)S(1)} %pad_maximum_fusion.wqv_ref, ...), custom_call_target="tpu_custom_call" | custom-call | flops 2097152000 | bytes 4194304 | tf_op jit(solution)/shard_map/pool_attention/pallas_call | solution.py:143
  63.6 9.4 %all-to-all-start.3 = ((bf16[32,12,8,128]{3,2,1,0:T(8,128)(2,1)}), bf16[32,12,8,128]{3,2,1,0:T(8,128)(2,1)S(1)}, u32[]{:S(2)}, u32[]{:S(2)}) async-start(bf16[32,12,8,128]{3,2,1,0:T(8,128)(2,1)} %pool_attention.3), calls=%async_computation.3 | async-start | bytes 1572864 | tf_op jit(solution)/shard_map/all_to_all | solution.py:271
  73.0 20.8 %pool_attention.2 = bf16[32,12,8,128]{3,2,1,0:T(8,128)(2,1)} custom-call(s32[4]{0:T(128)S(1)} %bitcast_subtract_fusion.1.starts, s32[4]{0:T(128)S(1)} %bitcast.32, bf16[32,64,128]{2,1,0:T(8,128)(2,1)S(1)} %all-to-all-done.x_ref, bf16[128,128]{1,0:T(8,128)(2,1)S(1)} %get-tuple-element.42.wk_ref, bf16[256,128]{1,0:T(8,128)(2,1)S(1)} %pad_maximum_fusion.wqv_ref, ...), custom_call_target="tpu_custom_call" | custom-call | flops 2097152000 | bytes 4194304 | tf_op jit(solution)/shard_map/pool_attention/pallas_call | solution.py:143
  93.8 9.0 %all-to-all-start.1 = ((bf16[32,12,8,128]{3,2,1,0:T(8,128)(2,1)}), bf16[32,12,8,128]{3,2,1,0:T(8,128)(2,1)S(1)}, u32[]{:S(2)}, u32[]{:S(2)}) async-start(bf16[32,12,8,128]{3,2,1,0:T(8,128)(2,1)} %pool_attention.2), calls=%async_computation.1 | async-start | bytes 1572864 | tf_op jit(solution)/shard_map/all_to_all | solution.py:271
  103.6 1.3 pack_slots.3
  104.9 4.1 %collective-permute-start.7 = (bf16[3,256,128]{2,1,0:T(8,128)(2,1)}, bf16[3,256,128]{2,1,0:T(8,128)(2,1)S(1)}, u32[]{:S(2)}, u32[]{:S(2)}) collective-permute-start(bf16[3,256,128]{2,1,0:T(8,128)(2,1)} %get-tuple-element.32), channel_id=1, source_target_pairs={{0,32},{32,64},{64,96},{96,128},{128,160},{160,192},{192,224},{224... | collective-permute-start | bytes 589832 | tf_op jit(solution)/shard_map/ppermute | solution.py:275
  109.0 1.2 collective-permute-start.8
  110.2 1.5 collective-permute-start.9
  112.3 2.0 %collective-permute-start.11 = (bf16[3,256,128]{2,1,0:T(8,128)(2,1)S(1)}, bf16[3,256,128]{2,1,0:T(8,128)(2,1)S(1)}, u32[]{:S(2)}, u32[]{:S(2)}) collective-permute-start(bf16[3,256,128]{2,1,0:T(8,128)(2,1)S(1)} %get-tuple-element.36), channel_id=1, source_target_pairs={{0,160},{32,192},{64,224},{96,0},{128,32},{160,64},{192,96},{224,1... | collective-permute-start | bytes 589832 | tf_op jit(solution)/shard_map/ppermute | solution.py:275
  114.3 7.8 %all-to-all-done.1.y_ref = bf16[32,12,8,128]{3,2,1,0:T(8,128)(2,1)S(1)} async-done(((bf16[32,12,8,128]{3,2,1,0:T(8,128)(2,1)}), bf16[32,12,8,128]{3,2,1,0:T(8,128)(2,1)S(1)}, u32[]{:S(2)}, u32[]{:S(2)}) %all-to-all-start.1) | async-done | bytes 786464 | tf_op jit(solution)/shard_map/all_to_all | solution.py:271
  122.9 2.6 %collective-permute-start.12 = (bf16[3,256,128]{2,1,0:T(8,128)(2,1)S(1)}, bf16[3,256,128]{2,1,0:T(8,128)(2,1)S(1)}, u32[]{:S(2)}, u32[]{:S(2)}) collective-permute-start(bf16[3,256,128]{2,1,0:T(8,128)(2,1)S(1)} %get-tuple-element.37), channel_id=1, source_target_pairs={{0,192},{32,224},{64,0},{96,32},{128,64},{160,96},{192,128},{224,1... | collective-permute-start | bytes 589832 | tf_op jit(solution)/shard_map/ppermute | solution.py:275
  125.5 5.3 %collective-permute-start.13 = (bf16[3,256,128]{2,1,0:T(8,128)(2,1)S(1)}, bf16[3,256,128]{2,1,0:T(8,128)(2,1)S(1)}, u32[]{:S(2)}, u32[]{:S(2)}) collective-permute-start(bf16[3,256,128]{2,1,0:T(8,128)(2,1)S(1)} %get-tuple-element.38), channel_id=1, source_target_pairs={{0,224},{32,0},{64,32},{96,64},{128,96},{160,128},{192,160},{224,1... | collective-permute-start | bytes 589832 | tf_op jit(solution)/shard_map/ppermute | solution.py:275
  130.9 2.3 %collective-permute-start.2 = (bf16[3,256,128]{2,1,0:T(8,128)(2,1)S(1)}, bf16[3,256,128]{2,1,0:T(8,128)(2,1)S(1)}, u32[]{:S(2)}, u32[]{:S(2)}) collective-permute-start(bf16[3,256,128]{2,1,0:T(8,128)(2,1)S(1)} %get-tuple-element.26), channel_id=1, source_target_pairs={{0,96},{32,128},{64,160},{96,192},{128,224},{160,0},{192,32},{224,... | collective-permute-start | bytes 589832 | tf_op jit(solution)/shard_map/ppermute | solution.py:275
  133.2 1.5 collective-permute-start.3
  135.4 2.7 %collective-permute-start.4 = (bf16[3,256,128]{2,1,0:T(8,128)(2,1)S(1)}, bf16[3,256,128]{2,1,0:T(8,128)(2,1)S(1)}, u32[]{:S(2)}, u32[]{:S(2)}) collective-permute-start(bf16[3,256,128]{2,1,0:T(8,128)(2,1)S(1)} %get-tuple-element.28), channel_id=1, source_target_pairs={{0,160},{32,192},{64,224},{96,0},{128,32},{160,64},{192,96},{224,1... | collective-permute-start | bytes 589832 | tf_op jit(solution)/shard_map/ppermute | solution.py:275
  138.0 7.9 %collective-permute-start.5 = (bf16[3,256,128]{2,1,0:T(8,128)(2,1)S(1)}, bf16[3,256,128]{2,1,0:T(8,128)(2,1)S(1)}, u32[]{:S(2)}, u32[]{:S(2)}) collective-permute-start(bf16[3,256,128]{2,1,0:T(8,128)(2,1)S(1)} %get-tuple-element.29), channel_id=1, source_target_pairs={{0,192},{32,224},{64,0},{96,32},{128,64},{160,96},{192,128},{224,1... | collective-permute-start | bytes 589832 | tf_op jit(solution)/shard_map/ppermute | solution.py:275
  146.0 5.2 %collective-permute-done.2.refs_3_ = bf16[3,256,128]{2,1,0:T(8,128)(2,1)S(1)} collective-permute-done((bf16[3,256,128]{2,1,0:T(8,128)(2,1)S(1)}, bf16[3,256,128]{2,1,0:T(8,128)(2,1)S(1)}, u32[]{:S(2)}, u32[]{:S(2)}) %collective-permute-start.2) | collective-permute-done | bytes 196640 | tf_op jit(solution)/shard_map/ppermute | solution.py:275
  152.2 3.4 %collective-permute-done.6.refs_7_ = bf16[3,256,128]{2,1,0:T(8,128)(2,1)S(1)} collective-permute-done((bf16[3,256,128]{2,1,0:T(8,128)(2,1)S(1)}, bf16[3,256,128]{2,1,0:T(8,128)(2,1)S(1)}, u32[]{:S(2)}, u32[]{:S(2)}) %collective-permute-start.6) | collective-permute-done | bytes 196640 | tf_op jit(solution)/shard_map/ppermute | solution.py:275
  155.6 2.0 %place_slots.1 = bf16[24,512,128]{2,1,0:T(8,128)(2,1)} custom-call(s32[1]{0:T(128)} %bitcast.me_ref, bf16[3,256,128]{2,1,0:T(8,128)(2,1)S(1)} %get-tuple-element.23.refs_0_, bf16[3,256,128]{2,1,0:T(8,128)(2,1)S(1)} %collective-permute-done.refs_1_, bf16[3,256,128]{2,1,0:T(8,128)(2,1)S(1)} %collective-permute-done.1.refs_2_, ...), custom_call_target="tpu_custom_call" | custom-call | bytes 6291456 | tf_op jit(solution)/shard_map/place_slots/pallas_call | solution.py:222
  (62 shorter events, 7.1 us)
Async XLA Ops:
  0.0 2.1 %copy-start = (bf16[3,3,128,128]{3,2,1,0:T(8,128)(2,1)S(1)}, bf16[3,3,128,128]{3,2,1,0:T(8,128)(2,1)}, u32[]{:S(2)}) copy-start(bf16[3,3,128,128]{3,2,1,0:T(8,128)(2,1)} %param.12) | copy-start | bytes 884740
  6.8 13.1 %copy-start.5 = (s32[8,4]{0,1:T(4,128)S(1)}, s32[8,4]{0,1:T(4,128)}, u32[]{:S(2)}) copy-start(s32[8,4]{0,1:T(4,128)} %param.11) | copy-start | bytes 388
  6.8 13.1 %copy-start.6 = (s32[8,4]{0,1:T(4,128)S(1)}, s32[8,4]{0,1:T(4,128)}, u32[]{:S(2)}) copy-start(s32[8,4]{0,1:T(4,128)} %param.10) | copy-start | bytes 388
  6.9 13.9 %copy-start.4 = (bf16[128,384]{1,0:T(8,128)(2,1)S(1)}, bf16[128,384]{1,0:T(8,128)(2,1)}, u32[]{:S(2)}) copy-start(bf16[128,384]{1,0:T(8,128)(2,1)} %param.13) | copy-start | bytes 294916
  7.9 28.3 %all-to-all-start.2 = ((bf16[32,64,128]{2,1,0:T(8,128)(2,1)}), bf16[32,64,128]{2,1,0:T(8,128)(2,1)S(1)}, u32[]{:S(2)}, u32[]{:S(2)}) async-start(bf16[32,64,128]{2,1,0:T(8,128)(2,1)} %bitcast.13), calls=%async_computation.2 | async-start | bytes 1048576 | tf_op jit(solution)/shard_map/all_to_all | solution.py:269
  36.2 27.4 %all-to-all-start = ((bf16[32,64,128]{2,1,0:T(8,128)(2,1)}), bf16[32,64,128]{2,1,0:T(8,128)(2,1)S(1)}, u32[]{:S(2)}, u32[]{:S(2)}) async-start(bf16[32,64,128]{2,1,0:T(8,128)(2,1)} %bitcast.6), calls=%async_computation | async-start | bytes 1048576 | tf_op jit(solution)/shard_map/all_to_all | solution.py:269
  41.5 1.3 copy-start.1
  41.5 1.3 copy-start.2
  63.6 30.2 %all-to-all-start.3 = ((bf16[32,12,8,128]{3,2,1,0:T(8,128)(2,1)}), bf16[32,12,8,128]{3,2,1,0:T(8,128)(2,1)S(1)}, u32[]{:S(2)}, u32[]{:S(2)}) async-start(bf16[32,12,8,128]{3,2,1,0:T(8,128)(2,1)} %pool_attention.3), calls=%async_computation.3 | async-start | bytes 1572864 | tf_op jit(solution)/shard_map/all_to_all | solution.py:271
  93.8 28.3 %all-to-all-start.1 = ((bf16[32,12,8,128]{3,2,1,0:T(8,128)(2,1)}), bf16[32,12,8,128]{3,2,1,0:T(8,128)(2,1)S(1)}, u32[]{:S(2)}, u32[]{:S(2)}) async-start(bf16[32,12,8,128]{3,2,1,0:T(8,128)(2,1)} %pool_attention.2), calls=%async_computation.1 | async-start | bytes 1572864 | tf_op jit(solution)/shard_map/all_to_all | solution.py:271
  104.9 18.0 %collective-permute-start.7 = (bf16[3,256,128]{2,1,0:T(8,128)(2,1)}, bf16[3,256,128]{2,1,0:T(8,128)(2,1)S(1)}, u32[]{:S(2)}, u32[]{:S(2)}) collective-permute-start(bf16[3,256,128]{2,1,0:T(8,128)(2,1)} %get-tuple-element.32), channel_id=1, source_target_pairs={{0,32},{32,64},{64,96},{96,128},{128,160},{160,192},{192,224},{224... | collective-permute-start | bytes 589832 | tf_op jit(solution)/shard_map/ppermute | solution.py:275
  109.0 16.5 %collective-permute-start.8 = (bf16[3,256,128]{2,1,0:T(8,128)(2,1)S(1)}, bf16[3,256,128]{2,1,0:T(8,128)(2,1)S(1)}, u32[]{:S(2)}, u32[]{:S(2)}) collective-permute-start(bf16[3,256,128]{2,1,0:T(8,128)(2,1)S(1)} %get-tuple-element.33), channel_id=1, source_target_pairs={{0,64},{32,96},{64,128},{96,160},{128,192},{160,224},{192,0},{224,... | collective-permute-start | bytes 589832 | tf_op jit(solution)/shard_map/ppermute | solution.py:275
  110.2 20.5 %collective-permute-start.9 = (bf16[3,256,128]{2,1,0:T(8,128)(2,1)S(1)}, bf16[3,256,128]{2,1,0:T(8,128)(2,1)S(1)}, u32[]{:S(2)}, u32[]{:S(2)}) collective-permute-start(bf16[3,256,128]{2,1,0:T(8,128)(2,1)S(1)} %get-tuple-element.34), channel_id=1, source_target_pairs={{0,96},{32,128},{64,160},{96,192},{128,224},{160,0},{192,32},{224,... | collective-permute-start | bytes 589832 | tf_op jit(solution)/shard_map/ppermute | solution.py:275
  111.8 19.0 %collective-permute-start.10 = (bf16[3,256,128]{2,1,0:T(8,128)(2,1)S(1)}, bf16[3,256,128]{2,1,0:T(8,128)(2,1)S(1)}, u32[]{:S(2)}, u32[]{:S(2)}) collective-permute-start(bf16[3,256,128]{2,1,0:T(8,128)(2,1)S(1)} %get-tuple-element.35), channel_id=1, source_target_pairs={{0,128},{32,160},{64,192},{96,224},{128,0},{160,32},{192,64},{224,... | collective-permute-start | bytes 589832 | tf_op jit(solution)/shard_map/ppermute | solution.py:275
  112.3 18.5 %collective-permute-start.11 = (bf16[3,256,128]{2,1,0:T(8,128)(2,1)S(1)}, bf16[3,256,128]{2,1,0:T(8,128)(2,1)S(1)}, u32[]{:S(2)}, u32[]{:S(2)}) collective-permute-start(bf16[3,256,128]{2,1,0:T(8,128)(2,1)S(1)} %get-tuple-element.36), channel_id=1, source_target_pairs={{0,160},{32,192},{64,224},{96,0},{128,32},{160,64},{192,96},{224,1... | collective-permute-start | bytes 589832 | tf_op jit(solution)/shard_map/ppermute | solution.py:275
  122.9 10.2 %collective-permute-start.12 = (bf16[3,256,128]{2,1,0:T(8,128)(2,1)S(1)}, bf16[3,256,128]{2,1,0:T(8,128)(2,1)S(1)}, u32[]{:S(2)}, u32[]{:S(2)}) collective-permute-start(bf16[3,256,128]{2,1,0:T(8,128)(2,1)S(1)} %get-tuple-element.37), channel_id=1, source_target_pairs={{0,192},{32,224},{64,0},{96,32},{128,64},{160,96},{192,128},{224,1... | collective-permute-start | bytes 589832 | tf_op jit(solution)/shard_map/ppermute | solution.py:275
  125.5 9.9 %collective-permute-start.13 = (bf16[3,256,128]{2,1,0:T(8,128)(2,1)S(1)}, bf16[3,256,128]{2,1,0:T(8,128)(2,1)S(1)}, u32[]{:S(2)}, u32[]{:S(2)}) collective-permute-start(bf16[3,256,128]{2,1,0:T(8,128)(2,1)S(1)} %get-tuple-element.38), channel_id=1, source_target_pairs={{0,224},{32,0},{64,32},{96,64},{128,96},{160,128},{192,160},{224,1... | collective-permute-start | bytes 589832 | tf_op jit(solution)/shard_map/ppermute | solution.py:275
  130.8 7.3 %collective-permute-start = (bf16[3,256,128]{2,1,0:T(8,128)(2,1)S(1)}, bf16[3,256,128]{2,1,0:T(8,128)(2,1)S(1)}, u32[]{:S(2)}, u32[]{:S(2)}) collective-permute-start(bf16[3,256,128]{2,1,0:T(8,128)(2,1)S(1)} %get-tuple-element.24), channel_id=1, source_target_pairs={{0,32},{32,64},{64,96},{96,128},{128,160},{160,192},{192,224},{224... | collective-permute-start | bytes 589832 | tf_op jit(solution)/shard_map/ppermute | solution.py:275
  130.8 15.2 %collective-permute-start.1 = (bf16[3,256,128]{2,1,0:T(8,128)(2,1)S(1)}, bf16[3,256,128]{2,1,0:T(8,128)(2,1)S(1)}, u32[]{:S(2)}, u32[]{:S(2)}) collective-permute-start(bf16[3,256,128]{2,1,0:T(8,128)(2,1)S(1)} %get-tuple-element.25), channel_id=1, source_target_pairs={{0,64},{32,96},{64,128},{96,160},{128,192},{160,224},{192,0},{224,... | collective-permute-start | bytes 589832 | tf_op jit(solution)/shard_map/ppermute | solution.py:275
  130.9 20.3 %collective-permute-start.2 = (bf16[3,256,128]{2,1,0:T(8,128)(2,1)S(1)}, bf16[3,256,128]{2,1,0:T(8,128)(2,1)S(1)}, u32[]{:S(2)}, u32[]{:S(2)}) collective-permute-start(bf16[3,256,128]{2,1,0:T(8,128)(2,1)S(1)} %get-tuple-element.26), channel_id=1, source_target_pairs={{0,96},{32,128},{64,160},{96,192},{128,224},{160,0},{192,32},{224,... | collective-permute-start | bytes 589832 | tf_op jit(solution)/shard_map/ppermute | solution.py:275
  133.2 18.0 %collective-permute-start.3 = (bf16[3,256,128]{2,1,0:T(8,128)(2,1)S(1)}, bf16[3,256,128]{2,1,0:T(8,128)(2,1)S(1)}, u32[]{:S(2)}, u32[]{:S(2)}) collective-permute-start(bf16[3,256,128]{2,1,0:T(8,128)(2,1)S(1)} %get-tuple-element.27), channel_id=1, source_target_pairs={{0,128},{32,160},{64,192},{96,224},{128,0},{160,32},{192,64},{224,... | collective-permute-start | bytes 589832 | tf_op jit(solution)/shard_map/ppermute | solution.py:275
  135.4 15.8 %collective-permute-start.4 = (bf16[3,256,128]{2,1,0:T(8,128)(2,1)S(1)}, bf16[3,256,128]{2,1,0:T(8,128)(2,1)S(1)}, u32[]{:S(2)}, u32[]{:S(2)}) collective-permute-start(bf16[3,256,128]{2,1,0:T(8,128)(2,1)S(1)} %get-tuple-element.28), channel_id=1, source_target_pairs={{0,160},{32,192},{64,224},{96,0},{128,32},{160,64},{192,96},{224,1... | collective-permute-start | bytes 589832 | tf_op jit(solution)/shard_map/ppermute | solution.py:275
  138.0 14.2 %collective-permute-start.5 = (bf16[3,256,128]{2,1,0:T(8,128)(2,1)S(1)}, bf16[3,256,128]{2,1,0:T(8,128)(2,1)S(1)}, u32[]{:S(2)}, u32[]{:S(2)}) collective-permute-start(bf16[3,256,128]{2,1,0:T(8,128)(2,1)S(1)} %get-tuple-element.29), channel_id=1, source_target_pairs={{0,192},{32,224},{64,0},{96,32},{128,64},{160,96},{192,128},{224,1... | collective-permute-start | bytes 589832 | tf_op jit(solution)/shard_map/ppermute | solution.py:275
  146.0 9.7 %collective-permute-start.6 = (bf16[3,256,128]{2,1,0:T(8,128)(2,1)S(1)}, bf16[3,256,128]{2,1,0:T(8,128)(2,1)S(1)}, u32[]{:S(2)}, u32[]{:S(2)}) collective-permute-start(bf16[3,256,128]{2,1,0:T(8,128)(2,1)S(1)} %get-tuple-element.30), channel_id=1, source_target_pairs={{0,224},{32,0},{64,32},{96,64},{128,96},{160,128},{192,160},{224,1... | collective-permute-start | bytes 589832 | tf_op jit(solution)/shard_map/ppermute | solution.py:275
  (2 other events, 2.4 us)

commit v2 on v1

v2 whole, which is shorter than its diff:
```python
import functools

import jax
import jax.numpy as jnp
from jax import lax
from jax.experimental import pallas as pl
from jax.experimental.pallas import tpu as pltpu
from jax.sharding import PartitionSpec as P

HEADS = 8
HEAD_DIM = 16
LMAX = 81
EPS = 1e-6
C = 128
POOL = 256
REACH = 80
HALF = 128
KEYS = 208
FAR = -1e30
LOG2E = 1.4426950408889634
BF = jnp.bfloat16
F32 = jnp.float32


def square_parts(v):
    sq = v * v
    hi = sq.astype(BF)
    lo = (sq - hi.astype(F32)).astype(BF)
    return hi, lo


def attention_kernel(
    slots, starts, lens, x_ref, wqv_ref, wk_ref, gain_ref, wout_ref, wup_ref, wdown_ref, onehot_ref, far_ref,
    blockones_ref, out_ref, kaug, qbig, rows
):
    bands, flat, _ = x_ref.shape
    per_band = POOL // bands
    px = flat // per_band
    n2 = 2 * POOL
    lane = lax.broadcasted_iota(jnp.int32, (1, C), 1) // HEAD_DIM
    kaug[C:, :] = onehot_ref[...]
    for h in range(HEADS):
        qbig[h, :, C:] = far_ref[...]

    def pixel_pair(pp, carry):
        both = x_ref[:, pl.ds(pl.multiple_of(pp * 16, 16), 16), :].astype(F32)
        xa = both[:, :per_band].reshape(POOL, C)
        xb = both[:, per_band:].reshape(POOL, C)
        x = jnp.concatenate([xa, xb], axis=0)
        n = (x * lax.rsqrt(jnp.mean(x * x, axis=-1, keepdims=True) + EPS)).astype(BF)
        qv = jnp.dot(n, wqv_ref[...], preferred_element_type=F32).astype(BF)
        q = qv[:, :C].astype(F32)
        ss = jnp.dot(
            jnp.concatenate(square_parts(q), axis=1), blockones_ref[...], preferred_element_type=F32
        )
        q = q * lax.rsqrt(ss * (1.0 / HEAD_DIM) + EPS) * gain_ref[...]
        v = qv[:, C:]
        k = lax.dot_general(
            wk_ref[...], n, (((1,), (1,)), ((), ())), preferred_element_type=F32
        ).astype(BF)
        k = k.astype(F32).reshape(HEADS, HEAD_DIM, n2)
        ks = jnp.sum(k * k, axis=1, keepdims=True)
        kaug[:C, :] = (k * lax.rsqrt(ks * (1.0 / HEAD_DIM) + EPS)).reshape(C, n2).astype(BF)
        for h in range(HEADS):
            qbig[h, :, :C] = jnp.where(lane == h, q, 0.0).astype(BF)
        mixed = []
        for i in range(2):
            own = slice(i * POOL, (i + 1) * POOL)
            scores = jnp.dot(
                qbig[:, own, :].reshape(HEADS * POOL, 2 * C), kaug[:, own], preferred_element_type=F32
            )
            value_ones = jnp.concatenate([v[own], jnp.ones((POOL, C), BF)], axis=1)
            for h in range(HEADS):
                s = scores[h * POOL : (h + 1) * POOL]
                top = jnp.max(s, axis=-1, keepdims=True)
                e = jnp.exp2((s - top) * (LOG2E / 4)).astype(BF)
                o = jnp.dot(e, value_ones, preferred_element_type=F32)
                num = o[:, :C] if h == 0 else jnp.where(lane == h, o[:, :C], num)
                den = o[:, C:] if h == 0 else jnp.where(lane == h, o[:, C:], den)
            mixed.append((num / den).astype(BF))
        m = x + jnp.dot(
            jnp.concatenate(mixed, axis=0), wout_ref[...], preferred_element_type=F32
        )
        m = m.astype(BF).astype(F32)
        n = (m * lax.rsqrt(jnp.mean(m * m, axis=-1, keepdims=True) + EPS)).astype(BF)
        up = jnp.dot(n, wup_ref[...], preferred_element_type=F32) * 0.5
        up = (up + up * jnp.tanh(up)).astype(BF)
        res = m + jnp.dot(up, wdown_ref[...], preferred_element_type=F32)
        for i in range(2):
            rows[pl.ds(2 * pp + i, POOL, stride=px), :] = res[i * POOL : (i + 1) * POOL]
        return carry

    lax.fori_loop(0, px // 2, pixel_pair, 0)

    clips = out_ref.shape[1] // slots

    def hand_out(b, carry):
        parts = []
        for c in range(clips):
            for jj in range(slots):
                j = b * slots + jj
                frame = jnp.minimum(starts[c] + j, POOL - 1)
                part = rows[pl.ds(pl.multiple_of(frame * px, px), px), :]
                parts.append(jnp.where(j < lens[c], part, 0.0))
        out_ref[b] = jnp.stack(parts, axis=0).astype(BF)
        return carry

    lax.fori_loop(0, bands, hand_out, 0)


def attention(x, starts, lens, w_qkv, query_gain, w_out, w_up, w_down, slots):
    bands, flat, _ = x.shape
    px = flat // (POOL // bands)
    n2 = 2 * POOL
    clips = starts.shape[0]
    frame = jnp.arange(POOL, dtype=jnp.int32)
    clip_of = jnp.sum((frame[:, None] >= starts[None, :]).astype(jnp.int32), axis=1) - 1
    lane = jnp.arange(C, dtype=jnp.int32)
    onehot = (lane[:, None] == clip_of[None, :]).astype(BF)
    onehot = jnp.concatenate([onehot, onehot], axis=1)
    apart = jnp.where((lane[None, :] < clips) & (lane[None, :] != clip_of[:, None]), FAR, 0.0).astype(BF)
    apart = jnp.concatenate([apart, apart], axis=0)
    blockones = (lane[:, None] // HEAD_DIM == lane[None, :] // HEAD_DIM).astype(BF)
    blockones = jnp.concatenate([blockones, blockones], axis=0)
    wqv = jnp.concatenate([w_qkv[:, :C], w_qkv[:, 2 * C :]], axis=1)
    gain = query_gain.reshape(1, C)
    vmem = pl.BlockSpec(memory_space=pltpu.VMEM)
    smem = pl.BlockSpec(memory_space=pltpu.SMEM)
    return pl.pallas_call(
        functools.partial(attention_kernel, slots),
        out_shape=jax.ShapeDtypeStruct((bands, clips * slots, px, C), BF),
        in_specs=[smem, smem] + [vmem] * 10,
        out_specs=vmem,
        scratch_shapes=[
            pltpu.VMEM((2 * C, n2), BF),
            pltpu.VMEM((HEADS, n2, 2 * C), BF),
            pltpu.VMEM((POOL * px, C), F32),
        ],
        compiler_params=pltpu.CompilerParams(vmem_limit_bytes=48 * 2**20),
        cost_estimate=pl.CostEstimate(
            flops=2 * POOL * px * C * 4000, bytes_accessed=4 * 2**20, transcendentals=POOL * px * HEADS * KEYS
        ),
        name="pool_attention",
    )(starts, lens, x, wqv, w_qkv[:, C : 2 * C].T, gain, w_out, w_up, w_down, onehot, apart, blockones)


CHUNKS = 2


def rms_scale(values, reduce_axis):
    return values * lax.rsqrt(jnp.mean(values * values, axis=reduce_axis, keepdims=True) + EPS)


def conv_rows(latents, conv_weight, first, count):
    total = latents.shape[1]
    above, below = min(first, 1), min(total - first - count, 1)
    latent_wide = latents[:, first - above : first + count + below].astype(F32)
    normed = jax.nn.silu(rms_scale(latent_wide, -1)).astype(BF)
    convolved = lax.conv_general_dilated(
        normed,
        conv_weight,
        (1, 1),
        ((1 - above, 1 - below), (1, 1)),
        dimension_numbers=("NHWC", "HWIO", "NHWC"),
        preferred_element_type=F32,
    )
    return (latent_wide[:, above : above + count] + convolved).astype(BF)


def pack_kernel(slots, aims_of, clip_ref, y_ref, *out_refs):
    bands, _, px, _ = y_ref.shape
    for out_ref, aims in zip(out_refs, aims_of):
        for at, aim in enumerate(aims):
            c = clip_ref[aim]
            for jj in range(slots):
                part = y_ref[:, jnp.maximum(c, 0) * slots + jj].astype(F32)
                part = jnp.where(c >= 0, part, 0.0).reshape(bands * px, C)
                out_ref[at, jj] = part.astype(BF)


def pack(y, clip_of_aim, slots, aims_of):
    bands, _, px, _ = y.shape
    vmem = pl.BlockSpec(memory_space=pltpu.VMEM)
    return pl.pallas_call(
        functools.partial(pack_kernel, slots, aims_of),
        out_shape=[jax.ShapeDtypeStruct((len(aims), slots, bands * px, C), BF) for aims in aims_of],
        in_specs=[pl.BlockSpec(memory_space=pltpu.SMEM), vmem],
        out_specs=[vmem] * len(aims_of),
        compiler_params=pltpu.CompilerParams(vmem_limit_bytes=32 * 2**20),
        cost_estimate=pl.CostEstimate(flops=0, bytes_accessed=2 * 2**20, transcendentals=0),
        name="pack_slots",
    )(clip_of_aim, y)


def place_kernel(groups, slots, entries, me_ref, *refs):
    pieces, out_ref, sem = refs[:-2], refs[-2], refs[-1]
    chip, core = me_ref[0] // 2, lax.rem(me_ref[0], 2)
    copies = []
    for piece, at, chunk, hop, flip in entries:
        chunk_px = pieces[piece].shape[2]
        source = lax.rem(chip + groups // 2 - hop, groups // 2) * 2 + (1 - core if flip else core)
        for jj in range(slots):
            copies.append(
                pltpu.make_async_copy(
                    pieces[piece].at[at, jj],
                    out_ref.at[jj * groups + source, pl.ds(chunk * chunk_px, chunk_px)],
                    sem.at[len(copies)],
                )
            )
    for copy in copies:
        copy.start()
    for copy in copies:
        copy.wait()


def place(pieces, entries, me, groups, pixels):
    slots = pieces[0].shape[1]
    vmem = pl.BlockSpec(memory_space=pltpu.VMEM)
    return pl.pallas_call(
        functools.partial(place_kernel, groups, slots, entries),
        out_shape=jax.ShapeDtypeStruct((slots * groups, pixels, C), BF),
        in_specs=[pl.BlockSpec(memory_space=pltpu.SMEM)] + [vmem] * len(pieces),
        out_specs=pl.BlockSpec(memory_space=pl.ANY),
        scratch_shapes=[pltpu.SemaphoreType.DMA((len(entries) * slots,))],
        compiler_params=pltpu.CompilerParams(vmem_limit_bytes=32 * 2**20),
        cost_estimate=pl.CostEstimate(flops=0, bytes_accessed=6 * 2**20, transcendentals=0),
        name="place_slots",
    )(me[None], *pieces)


def to_chip(value, hop, flip, groups):
    pairs = [
        (chip * 2 + core, (chip + hop) % (groups // 2) * 2 + (core ^ flip))
        for chip in range(groups // 2)
        for core in range(2)
    ]
    return lax.ppermute(value, "group", pairs) if hop or flip else value


def body(
    base_latents, clip_lengths, clip_group, conv_weight, w_qkv, query_gain, w_out, w_up, w_down
):
    groups = lax.axis_size("group")
    bands = lax.axis_size("band")
    frames_dev, tile_rows, tile_cols, channels = base_latents.shape
    pixels = tile_rows * tile_cols
    px = pixels // bands // CHUNKS
    chunk_rows = tile_rows // CHUNKS

    me = lax.axis_index("group")
    lengths = lax.dynamic_index_in_dim(clip_lengths, me, 0, keepdims=False)
    targets = lax.dynamic_index_in_dim(clip_group, me, 0, keepdims=False)
    starts = jnp.cumsum(lengths) - lengths
    slots = -(-LMAX // bands)
    chips = groups // 2
    aim_list = [(hop, flip) for hop in range(chips) for flip in range(2)]
    aims = jnp.stack(
        [lax.rem(me // 2 + hop, chips) * 2 + lax.rem(me + flip, 2) for hop, flip in aim_list]
    )
    hit = targets[None, :] == aims[:, None]
    clip_index = jnp.arange(targets.shape[0], dtype=jnp.int32)
    clip_of_aim = jnp.max(jnp.where(hit, clip_index[None, :], -1), axis=1)

    pieces, entries = [], []
    for chunk in range(CHUNKS):
        hidden = conv_rows(base_latents, conv_weight, chunk * chunk_rows, chunk_rows)
        hidden = hidden.reshape(frames_dev, chunk_rows * tile_cols, channels).transpose(1, 0, 2)
        hidden = hidden.reshape(bands, px * frames_dev, channels)
        pencil = lax.all_to_all(hidden, "band", split_axis=0, concat_axis=0, tiled=True)
        refined = attention(pencil, starts, lengths, w_qkv, query_gain, w_out, w_up, w_down, slots)
        arrived = lax.all_to_all(refined, "band", split_axis=0, concat_axis=0, tiled=True)
        if chunk < CHUNKS - 1:
            packed = pack(
                arrived, clip_of_aim, slots, [[2 * hop, 2 * hop + 1] for hop in range(chips)]
            )
            landed = [to_chip(slab, hop, 0, groups) for hop, slab in enumerate(packed)]
            swapped = to_chip(jnp.stack([slab[1] for slab in landed]), 0, 1, groups)
            for hop, slab in enumerate(landed):
                entries += [(len(pieces), 0, chunk, hop, 0), (chips, hop, chunk, hop, 1)]
                pieces.append(slab)
            pieces.append(swapped)
        else:
            packed = pack(arrived, clip_of_aim, slots, [[i] for i in range(groups)])
            for (hop, flip), slab in zip(aim_list, packed):
                entries.append((len(pieces), 0, chunk, hop, flip))
                pieces.append(to_chip(slab, hop, flip, groups))
    placed = place(pieces, entries, me, groups, pixels)
    return placed.reshape(1, slots * groups, tile_rows, tile_cols, channels)


def solution(mesh):
    placed = (P(("group", "band"), None, None, None), P(), P(), P(), P(), P(), P(), P(), P())
    return jax.shard_map(
        body,
        mesh=mesh,
        in_specs=placed,
        out_specs=P("group", "band", None, None, None),
        check_vma=False,
    )
```

time: 158 us -> 138 us (0.87)
  starting transfers between devices: 67.2 us -> 44.3 us
  waiting for transfers between devices: 33.7 us -> 55.1 us
  Pallas kernels: 45.8 us -> 27.9 us
    ppermute x14 -> x11, waiting for transfers between devices: 10.4 us -> 31.6 us  [to_chip(): return lax.ppermute(value, 'group', pairs) if hop or flip else value]
    ppermute x14 -> x11, starting transfers between devices: 31.6 us -> 13.7 us  [to_chip(): return lax.ppermute(value, 'group', pairs) if hop or flip else value]
    pallas_call x2, Pallas kernels: 41.7 us -> 24.2 us  [attention(): pl.pallas_call(functools.partial(attention_kernel, slots), out_shape=jax....]
    all_to_all x2, starting transfers between devices: 18.4 us -> 13.2 us  [body(): lax.all_to_all(refined, 'band', split_axis=0, concat_axis=0, tiled=True)]
    conv_general_dilated x1 -> x2, matrix products: 4.75 us -> 4.52 us  [conv_rows(): lax.conv_general_dilated(normed, conv_weight, (1, 1), ((1 - above, 1 - be...]
  transfers between devices with their start and end apart: 18 -> 15, of which waited for: 6 -> 11; matrix products, arithmetic and copies ran while one was open for 2% -> 3% of each run, Pallas kernels for 28% -> 19%
where the time goes in v2:
time: 138 us; the launch traced here: 137 us
  waiting for transfers between devices  55.1 us (40%)
  starting transfers between devices  44.3 us (32%)
  Pallas kernels  27.9 us (20%)
  matrix products  4.52 us (3%)
  other arithmetic  2.58 us (2%)
  local copies, waits for them, and re-layouts  2.2 us (2%)
    ppermute x11, waiting for transfers between devices, to_chip(): return lax.ppermute(value, 'group', pairs) if hop or flip else value  31.6 us
    pallas_call x2, Pallas kernels, attention(): pl.pallas_call(functools.partial(attention_kernel, slots), out_shape=jax....  24.2 us
    all_to_all x2, starting transfers between devices, body(): lax.all_to_all(hidden, 'band', split_axis=0, concat_axis=0, tiled=True)  17.4 us
    all_to_all x2, waiting for transfers between devices, body(): lax.all_to_all(hidden, 'band', split_axis=0, concat_axis=0, tiled=True)  15.9 us
    ppermute x11, starting transfers between devices, to_chip(): return lax.ppermute(value, 'group', pairs) if hop or flip else value  13.7 us
    all_to_all x2, starting transfers between devices, body(): lax.all_to_all(refined, 'band', split_axis=0, concat_axis=0, tiled=True)  13.2 us
    all_to_all x2, waiting for transfers between devices, body(): lax.all_to_all(refined, 'band', split_axis=0, concat_axis=0, tiled=True)  7.53 us
    conv_general_dilated x2, matrix products, conv_rows(): lax.conv_general_dilated(normed, conv_weight, (1, 1), ((1 - above, 1 - be...  4.52 us
  transfers between devices with their start and end apart: 15, of which 11 were waited for; matrix products, arithmetic and copies ran while one was open for 3% of the time, Pallas kernels for 19%

profile of v2, /device:TPU:1, one launch (start us, length us, event | category | flops | bytes accessed | tf_op | source)
XLA Modules:
  0.0 137.0 jit_solution(16138224364027258291)
XLA Ops:
  0.0 1.5 %fusion.10 = (bf16[8,17,16,128]{3,2,1,0:T(8,128)(2,1)S(1)}, bf16[8,17,16,128]{3,2,1,0:T(8,128)(2,1)S(1)}) fusion(bf16[8,32,16,128]{3,2,1,0:T(8,128)(2,1)} %param.9), kind=kLoop, calls=%fused_computation.42 | loop fusion | bytes 2228224 | tf_op jit(solution)/shard_map/slice | solution.py:157
  2.5 2.3 %fusion = bf16[8,16,16,128]{3,0,2,1:T(8,128)(2,1)} fusion(bf16[3,3,128,128]{3,2,1,0:T(8,128)(2,1)S(1)} %copy-done, f32[8,17,16,128]{3,0,2,1:T(8,128)S(1)} %get-tuple-element.37, f32[8,17,16]{0,2,1:T(8,128)S(1)} %add_rsqrt_fusion.1), kind=kOutput, calls=%fused_computation.2 | convolution fusion | flops 568950784 | bytes 3121152 | tf_op jit(solution)/shard_map/conv_general_dilated | solution.py:159
  4.8 12.2 %all-to-all-start = ((bf16[32,64,128]{2,1,0:T(8,128)(2,1)}), bf16[32,64,128]{2,1,0:T(8,128)(2,1)S(1)}, u32[]{:S(2)}, u32[]{:S(2)}) async-start(bf16[32,64,128]{2,1,0:T(8,128)(2,1)} %bitcast.14), calls=%async_computation | async-start | bytes 1048576 | tf_op jit(solution)/shard_map/all_to_all | solution.py:269
  17.7 2.2 %fusion.1 = bf16[8,16,16,128]{3,0,2,1:T(8,128)(2,1)} fusion(bf16[3,3,128,128]{3,2,1,0:T(8,128)(2,1)S(1)} %copy-done, f32[8,17,16,128]{3,0,2,1:T(8,128)S(1)} %get-tuple-element.36, f32[8,17,16]{0,2,1:T(8,128)S(1)} %add_rsqrt_fusion), kind=kOutput, calls=%fused_computation.3 | convolution fusion | flops 568950784 | bytes 3121152 | tf_op jit(solution)/shard_map/conv_general_dilated | solution.py:159
  20.0 13.2 %all-to-all-done.x_ref = bf16[32,64,128]{2,1,0:T(8,128)(2,1)S(1)} async-done(((bf16[32,64,128]{2,1,0:T(8,128)(2,1)}), bf16[32,64,128]{2,1,0:T(8,128)(2,1)S(1)}, u32[]{:S(2)}, u32[]{:S(2)}) %all-to-all-start) | async-done | bytes 524320 | tf_op jit(solution)/shard_map/all_to_all | solution.py:269
  33.2 5.2 %all-to-all-start.2 = ((bf16[32,64,128]{2,1,0:T(8,128)(2,1)}), bf16[32,64,128]{2,1,0:T(8,128)(2,1)S(1)}, u32[]{:S(2)}, u32[]{:S(2)}) async-start(bf16[32,64,128]{2,1,0:T(8,128)(2,1)} %bitcast.21), calls=%async_computation.2 | async-start | bytes 1048576 | tf_op jit(solution)/shard_map/all_to_all | solution.py:269
  38.7 12.1 %pool_attention.2 = bf16[32,12,8,128]{3,2,1,0:T(8,128)(2,1)} custom-call(s32[4]{0:T(128)S(1)} %bitcast_subtract_fusion.1.starts, s32[4]{0:T(128)S(1)} %bitcast.38, bf16[32,64,128]{2,1,0:T(8,128)(2,1)S(1)} %all-to-all-done.x_ref, bf16[128,256]{1,0:T(8,128)(2,1)S(1)} %pad_maximum_fusion.2.wqv_ref, bf16[128,128]{1,0:T(8,128)(2,1)S(1)} %bitcast.35, ...), custom_call_target="tpu_custom_call" | custom-call | flops 2097152000 | bytes 4194304 | tf_op jit(solution)/shard_map/pool_attention/pallas_call | solution.py:129
  50.8 2.7 %all-to-all-done.2.x_ref = bf16[32,64,128]{2,1,0:T(8,128)(2,1)S(1)} async-done(((bf16[32,64,128]{2,1,0:T(8,128)(2,1)}), bf16[32,64,128]{2,1,0:T(8,128)(2,1)S(1)}, u32[]{:S(2)}, u32[]{:S(2)}) %all-to-all-start.2) | async-done | bytes 524320 | tf_op jit(solution)/shard_map/all_to_all | solution.py:269
  53.5 6.5 %all-to-all-start.1 = ((bf16[32,12,8,128]{3,2,1,0:T(8,128)(2,1)}), bf16[32,12,8,128]{3,2,1,0:T(8,128)(2,1)S(1)}, u32[]{:S(2)}, u32[]{:S(2)}) async-start(bf16[32,12,8,128]{3,2,1,0:T(8,128)(2,1)} %pool_attention.2), calls=%async_computation.1 | async-start | bytes 1572864 | tf_op jit(solution)/shard_map/all_to_all | solution.py:271
  60.0 12.1 %pool_attention.3 = bf16[32,12,8,128]{3,2,1,0:T(8,128)(2,1)} custom-call(s32[4]{0:T(128)S(1)} %bitcast_subtract_fusion.1.starts, s32[4]{0:T(128)S(1)} %bitcast.39, bf16[32,64,128]{2,1,0:T(8,128)(2,1)S(1)} %all-to-all-done.2.x_ref, bf16[128,256]{1,0:T(8,128)(2,1)S(1)} %pad_maximum_fusion.2.wqv_ref, bf16[128,128]{1,0:T(8,128)(2,1)S(1)} %bitcast.36, ...), custom_call_target="tpu_custom_call" | custom-call | flops 2097152000 | bytes 4194304 | tf_op jit(solution)/shard_map/pool_attention/pallas_call | solution.py:129
  72.2 7.5 %all-to-all-done.1.y_ref = bf16[32,12,8,128]{3,2,1,0:T(8,128)(2,1)S(1)} async-done(((bf16[32,12,8,128]{3,2,1,0:T(8,128)(2,1)}), bf16[32,12,8,128]{3,2,1,0:T(8,128)(2,1)S(1)}, u32[]{:S(2)}, u32[]{:S(2)}) %all-to-all-start.1) | async-done | bytes 786464 | tf_op jit(solution)/shard_map/all_to_all | solution.py:271
  79.7 6.7 %all-to-all-start.3 = ((bf16[32,12,8,128]{3,2,1,0:T(8,128)(2,1)}), bf16[32,12,8,128]{3,2,1,0:T(8,128)(2,1)S(1)}, u32[]{:S(2)}, u32[]{:S(2)}) async-start(bf16[32,12,8,128]{3,2,1,0:T(8,128)(2,1)} %pool_attention.3), calls=%async_computation.3 | async-start | bytes 1572864 | tf_op jit(solution)/shard_map/all_to_all | solution.py:271
  89.1 2.5 %collective-permute-start.1 = (bf16[2,3,256,128]{3,2,1,0:T(8,128)(2,1)S(1)}, bf16[2,3,256,128]{3,2,1,0:T(8,128)(2,1)S(1)}, u32[]{:S(2)}, u32[]{:S(2)}) collective-permute-start(bf16[2,3,256,128]{3,2,1,0:T(8,128)(2,1)S(1)} %get-tuple-element.19), channel_id=1, source_target_pairs={{0,128},{32,160},{64,192},{96,224},{128,0},{160,32},{192,64},{224,... | collective-permute-start | bytes 1179656 | tf_op jit(solution)/shard_map/ppermute | solution.py:237
  92.7 4.4 %collective-permute-done.refs_1_ = bf16[2,3,256,128]{3,2,1,0:T(8,128)(2,1)S(1)} collective-permute-done((bf16[2,3,256,128]{3,2,1,0:T(8,128)(2,1)S(1)}, bf16[2,3,256,128]{3,2,1,0:T(8,128)(2,1)S(1)}, u32[]{:S(2)}, u32[]{:S(2)}) %collective-permute-start) | collective-permute-done | bytes 393248 | tf_op jit(solution)/shard_map/ppermute | solution.py:237
  97.1 9.4 %collective-permute-done.1.refs_2_ = bf16[2,3,256,128]{3,2,1,0:T(8,128)(2,1)S(1)} collective-permute-done((bf16[2,3,256,128]{3,2,1,0:T(8,128)(2,1)S(1)}, bf16[2,3,256,128]{3,2,1,0:T(8,128)(2,1)S(1)}, u32[]{:S(2)}, u32[]{:S(2)}) %collective-permute-start.1) | collective-permute-done | bytes 393248 | tf_op jit(solution)/shard_map/ppermute | solution.py:237
  109.0 2.1 %collective-permute-start.3 = (bf16[4,3,256,128]{3,2,1,0:T(8,128)(2,1)}, bf16[4,3,256,128]{3,2,1,0:T(8,128)(2,1)S(1)}, u32[]{:S(2)}, u32[]{:S(2)}) collective-permute-start(bf16[4,3,256,128]{3,2,1,0:T(8,128)(2,1)} %pad_maximum_fusion), channel_id=1, source_target_pairs={{0,32},{32,0},{64,96},{96,64},{128,160},{160,128},{192,224},{224,1... | collective-permute-start | bytes 2359304 | tf_op jit(solution)/shard_map/ppermute | solution.py:237
  113.1 1.6 %collective-permute-start.6 = (bf16[1,3,256,128]{3,2,1,0:T(8,128)(2,1)S(1)}, bf16[1,3,256,128]{3,2,1,0:T(8,128)(2,1)S(1)}, u32[]{:S(2)}, u32[]{:S(2)}) collective-permute-start(bf16[1,3,256,128]{3,2,1,0:T(8,128)(2,1)S(1)} %get-tuple-element.24), channel_id=1, source_target_pairs={{0,96},{32,64},{64,160},{96,128},{128,224},{160,192},{192,32},{224... | collective-permute-start | bytes 589832 | tf_op jit(solution)/shard_map/ppermute | solution.py:237
  114.7 1.8 %collective-permute-start.7 = (bf16[1,3,256,128]{3,2,1,0:T(8,128)(2,1)S(1)}, bf16[1,3,256,128]{3,2,1,0:T(8,128)(2,1)S(1)}, u32[]{:S(2)}, u32[]{:S(2)}) collective-permute-start(bf16[1,3,256,128]{3,2,1,0:T(8,128)(2,1)S(1)} %get-tuple-element.25), channel_id=1, source_target_pairs={{0,128},{32,160},{64,192},{96,224},{128,0},{160,32},{192,64},{224,... | collective-permute-start | bytes 589832 | tf_op jit(solution)/shard_map/ppermute | solution.py:237
  117.7 1.7 %collective-permute-done.5.refs_7_ = bf16[1,3,256,128]{3,2,1,0:T(8,128)(2,1)S(1)} collective-permute-done((bf16[1,3,256,128]{3,2,1,0:T(8,128)(2,1)S(1)}, bf16[1,3,256,128]{3,2,1,0:T(8,128)(2,1)S(1)}, u32[]{:S(2)}, u32[]{:S(2)}) %collective-permute-start.5) | collective-permute-done | bytes 196640 | tf_op jit(solution)/shard_map/ppermute | solution.py:237
  120.1 4.5 %collective-permute-done.6.refs_8_ = bf16[1,3,256,128]{3,2,1,0:T(8,128)(2,1)S(1)} collective-permute-done((bf16[1,3,256,128]{3,2,1,0:T(8,128)(2,1)S(1)}, bf16[1,3,256,128]{3,2,1,0:T(8,128)(2,1)S(1)}, u32[]{:S(2)}, u32[]{:S(2)}) %collective-permute-start.6) | collective-permute-done | bytes 196640 | tf_op jit(solution)/shard_map/ppermute | solution.py:237
  124.6 3.6 %collective-permute-done.7.refs_9_ = bf16[1,3,256,128]{3,2,1,0:T(8,128)(2,1)S(1)} collective-permute-done((bf16[1,3,256,128]{3,2,1,0:T(8,128)(2,1)S(1)}, bf16[1,3,256,128]{3,2,1,0:T(8,128)(2,1)S(1)}, u32[]{:S(2)}, u32[]{:S(2)}) %collective-permute-start.7) | collective-permute-done | bytes 196640 | tf_op jit(solution)/shard_map/ppermute | solution.py:237
  128.2 4.8 %collective-permute-done.8.refs_10_ = bf16[1,3,256,128]{3,2,1,0:T(8,128)(2,1)S(1)} collective-permute-done((bf16[1,3,256,128]{3,2,1,0:T(8,128)(2,1)S(1)}, bf16[1,3,256,128]{3,2,1,0:T(8,128)(2,1)S(1)}, u32[]{:S(2)}, u32[]{:S(2)}) %collective-permute-start.8) | collective-permute-done | bytes 196640 | tf_op jit(solution)/shard_map/ppermute | solution.py:237
  133.0 1.8 %collective-permute-done.10.refs_12_ = bf16[1,3,256,128]{3,2,1,0:T(8,128)(2,1)S(1)} collective-permute-done((bf16[1,3,256,128]{3,2,1,0:T(8,128)(2,1)S(1)}, bf16[1,3,256,128]{3,2,1,0:T(8,128)(2,1)S(1)}, u32[]{:S(2)}, u32[]{:S(2)}) %collective-permute-start.10) | collective-permute-done | bytes 196640 | tf_op jit(solution)/shard_map/ppermute | solution.py:237
  134.8 2.0 %place_slots.1 = bf16[24,512,128]{2,1,0:T(8,128)(2,1)} custom-call(s32[1]{0:T(128)} %bitcast.me_ref, bf16[2,3,256,128]{3,2,1,0:T(8,128)(2,1)S(1)} %get-tuple-element.17.refs_0_, bf16[2,3,256,128]{3,2,1,0:T(8,128)(2,1)S(1)} %collective-permute-done.refs_1_, bf16[2,3,256,128]{3,2,1,0:T(8,128)(2,1)S(1)} %collective-permute-done.1.refs_2_, ...), custom_call_target="tpu_custom_call" | custom-call | bytes 6291456 | tf_op jit(solution)/shard_map/place_slots/pallas_call | solution.py:219
  (60 shorter events, 12.0 us)
Async XLA Ops:
  0.0 2.5 %copy-start = (bf16[3,3,128,128]{3,2,1,0:T(8,128)(2,1)S(1)}, bf16[3,3,128,128]{3,2,1,0:T(8,128)(2,1)}, u32[]{:S(2)}) copy-start(bf16[3,3,128,128]{3,2,1,0:T(8,128)(2,1)} %param.12) | copy-start | bytes 884740
  2.5 14.5 %copy-start.7 = (s32[8,4]{0,1:T(4,128)S(1)}, s32[8,4]{0,1:T(4,128)}, u32[]{:S(2)}) copy-start(s32[8,4]{0,1:T(4,128)} %param.10) | copy-start | bytes 388
  4.8 12.9 %copy-start.5 = (bf16[128,384]{1,0:T(8,128)(2,1)S(1)}, bf16[128,384]{1,0:T(8,128)(2,1)}, u32[]{:S(2)}) copy-start(bf16[128,384]{1,0:T(8,128)(2,1)} %param.13) | copy-start | bytes 294916
  4.8 28.5 %all-to-all-start = ((bf16[32,64,128]{2,1,0:T(8,128)(2,1)}), bf16[32,64,128]{2,1,0:T(8,128)(2,1)S(1)}, u32[]{:S(2)}, u32[]{:S(2)}) async-start(bf16[32,64,128]{2,1,0:T(8,128)(2,1)} %bitcast.14), calls=%async_computation | async-start | bytes 1048576 | tf_op jit(solution)/shard_map/all_to_all | solution.py:269
  20.0 18.7 %copy-start.1 = (bf16[128,512]{1,0:T(8,128)(2,1)S(1)}, bf16[128,512]{1,0:T(8,128)(2,1)}, u32[]{:S(2)}) copy-start(bf16[128,512]{1,0:T(8,128)(2,1)} %wup_ref.3) | copy-start | bytes 393220
  20.0 18.7 %copy-start.2 = (bf16[512,128]{1,0:T(8,128)(2,1)S(1)}, bf16[512,128]{1,0:T(8,128)(2,1)}, u32[]{:S(2)}) copy-start(bf16[512,128]{1,0:T(8,128)(2,1)} %wdown_ref.3) | copy-start | bytes 393220
  20.0 18.7 %copy-start.3 = (bf16[128,128]{1,0:T(8,128)(2,1)S(1)}, bf16[128,128]{1,0:T(8,128)(2,1)}, u32[]{:S(2)}) copy-start(bf16[128,128]{1,0:T(8,128)(2,1)} %wout_ref.3) | copy-start | bytes 98308
  20.0 18.7 %copy-start.4 = (f32[128]{0:T(128)S(1)}, f32[128]{0:T(128)}, u32[]{:S(2)}) copy-start(f32[128]{0:T(128)} %param.14) | copy-start | bytes 1540
  33.2 20.3 %all-to-all-start.2 = ((bf16[32,64,128]{2,1,0:T(8,128)(2,1)}), bf16[32,64,128]{2,1,0:T(8,128)(2,1)S(1)}, u32[]{:S(2)}, u32[]{:S(2)}) async-start(bf16[32,64,128]{2,1,0:T(8,128)(2,1)} %bitcast.21), calls=%async_computation.2 | async-start | bytes 1048576 | tf_op jit(solution)/shard_map/all_to_all | solution.py:269
  53.5 26.2 %all-to-all-start.1 = ((bf16[32,12,8,128]{3,2,1,0:T(8,128)(2,1)}), bf16[32,12,8,128]{3,2,1,0:T(8,128)(2,1)S(1)}, u32[]{:S(2)}, u32[]{:S(2)}) async-start(bf16[32,12,8,128]{3,2,1,0:T(8,128)(2,1)} %pool_attention.2), calls=%async_computation.1 | async-start | bytes 1572864 | tf_op jit(solution)/shard_map/all_to_all | solution.py:271
  72.2 14.3 %copy-start.6 = (s32[8,4]{0,1:T(4,128)S(1)}, s32[8,4]{0,1:T(4,128)}, u32[]{:S(2)}) copy-start(s32[8,4]{0,1:T(4,128)} %param.11) | copy-start | bytes 388
  79.7 31.4 %all-to-all-start.3 = ((bf16[32,12,8,128]{3,2,1,0:T(8,128)(2,1)}), bf16[32,12,8,128]{3,2,1,0:T(8,128)(2,1)S(1)}, u32[]{:S(2)}, u32[]{:S(2)}) async-start(bf16[32,12,8,128]{3,2,1,0:T(8,128)(2,1)} %pool_attention.3), calls=%async_computation.3 | async-start | bytes 1572864 | tf_op jit(solution)/shard_map/all_to_all | solution.py:271
  87.7 9.5 %collective-permute-start = (bf16[2,3,256,128]{3,2,1,0:T(8,128)(2,1)S(1)}, bf16[2,3,256,128]{3,2,1,0:T(8,128)(2,1)S(1)}, u32[]{:S(2)}, u32[]{:S(2)}) collective-permute-start(bf16[2,3,256,128]{3,2,1,0:T(8,128)(2,1)S(1)} %get-tuple-element.18), channel_id=1, source_target_pairs={{0,64},{32,96},{64,128},{96,160},{128,192},{160,224},{192,0},{224,... | collective-permute-start | bytes 1179656 | tf_op jit(solution)/shard_map/ppermute | solution.py:237
  89.1 17.4 %collective-permute-start.1 = (bf16[2,3,256,128]{3,2,1,0:T(8,128)(2,1)S(1)}, bf16[2,3,256,128]{3,2,1,0:T(8,128)(2,1)S(1)}, u32[]{:S(2)}, u32[]{:S(2)}) collective-permute-start(bf16[2,3,256,128]{3,2,1,0:T(8,128)(2,1)S(1)} %get-tuple-element.19), channel_id=1, source_target_pairs={{0,128},{32,160},{64,192},{96,224},{128,0},{160,32},{192,64},{224,... | collective-permute-start | bytes 1179656 | tf_op jit(solution)/shard_map/ppermute | solution.py:237
  91.6 16.4 %collective-permute-start.2 = (bf16[2,3,256,128]{3,2,1,0:T(8,128)(2,1)S(1)}, bf16[2,3,256,128]{3,2,1,0:T(8,128)(2,1)S(1)}, u32[]{:S(2)}, u32[]{:S(2)}) collective-permute-start(bf16[2,3,256,128]{3,2,1,0:T(8,128)(2,1)S(1)} %get-tuple-element.20), channel_id=1, source_target_pairs={{0,192},{32,224},{64,0},{96,32},{128,64},{160,96},{192,128},{224,1... | collective-permute-start | bytes 1179656 | tf_op jit(solution)/shard_map/ppermute | solution.py:237
  109.0 25.8 %collective-permute-start.3 = (bf16[4,3,256,128]{3,2,1,0:T(8,128)(2,1)}, bf16[4,3,256,128]{3,2,1,0:T(8,128)(2,1)S(1)}, u32[]{:S(2)}, u32[]{:S(2)}) collective-permute-start(bf16[4,3,256,128]{3,2,1,0:T(8,128)(2,1)} %pad_maximum_fusion), channel_id=1, source_target_pairs={{0,32},{32,0},{64,96},{96,64},{128,160},{160,128},{192,224},{224,1... | collective-permute-start | bytes 2359304 | tf_op jit(solution)/shard_map/ppermute | solution.py:237
  111.9 4.6 %collective-permute-start.4 = (bf16[1,3,256,128]{3,2,1,0:T(8,128)(2,1)S(1)}, bf16[1,3,256,128]{3,2,1,0:T(8,128)(2,1)S(1)}, u32[]{:S(2)}, u32[]{:S(2)}) collective-permute-start(bf16[1,3,256,128]{3,2,1,0:T(8,128)(2,1)S(1)} %get-tuple-element.22), channel_id=1, source_target_pairs={{0,32},{32,0},{64,96},{96,64},{128,160},{160,128},{192,224},{224,1... | collective-permute-start | bytes 589832 | tf_op jit(solution)/shard_map/ppermute | solution.py:237
  112.0 7.3 %collective-permute-start.5 = (bf16[1,3,256,128]{3,2,1,0:T(8,128)(2,1)S(1)}, bf16[1,3,256,128]{3,2,1,0:T(8,128)(2,1)S(1)}, u32[]{:S(2)}, u32[]{:S(2)}) collective-permute-start(bf16[1,3,256,128]{3,2,1,0:T(8,128)(2,1)S(1)} %get-tuple-element.23), channel_id=1, source_target_pairs={{0,64},{32,96},{64,128},{96,160},{128,192},{160,224},{192,0},{224,... | collective-permute-start | bytes 589832 | tf_op jit(solution)/shard_map/ppermute | solution.py:237
  113.1 11.4 %collective-permute-start.6 = (bf16[1,3,256,128]{3,2,1,0:T(8,128)(2,1)S(1)}, bf16[1,3,256,128]{3,2,1,0:T(8,128)(2,1)S(1)}, u32[]{:S(2)}, u32[]{:S(2)}) collective-permute-start(bf16[1,3,256,128]{3,2,1,0:T(8,128)(2,1)S(1)} %get-tuple-element.24), channel_id=1, source_target_pairs={{0,96},{32,64},{64,160},{96,128},{128,224},{160,192},{192,32},{224... | collective-permute-start | bytes 589832 | tf_op jit(solution)/shard_map/ppermute | solution.py:237
  114.7 13.5 %collective-permute-start.7 = (bf16[1,3,256,128]{3,2,1,0:T(8,128)(2,1)S(1)}, bf16[1,3,256,128]{3,2,1,0:T(8,128)(2,1)S(1)}, u32[]{:S(2)}, u32[]{:S(2)}) collective-permute-start(bf16[1,3,256,128]{3,2,1,0:T(8,128)(2,1)S(1)} %get-tuple-element.25), channel_id=1, source_target_pairs={{0,128},{32,160},{64,192},{96,224},{128,0},{160,32},{192,64},{224,... | collective-permute-start | bytes 589832 | tf_op jit(solution)/shard_map/ppermute | solution.py:237
  116.5 16.5 %collective-permute-start.8 = (bf16[1,3,256,128]{3,2,1,0:T(8,128)(2,1)S(1)}, bf16[1,3,256,128]{3,2,1,0:T(8,128)(2,1)S(1)}, u32[]{:S(2)}, u32[]{:S(2)}) collective-permute-start(bf16[1,3,256,128]{3,2,1,0:T(8,128)(2,1)S(1)} %get-tuple-element.26), channel_id=1, source_target_pairs={{0,160},{32,128},{64,224},{96,192},{128,32},{160,0},{192,96},{224,... | collective-permute-start | bytes 589832 | tf_op jit(solution)/shard_map/ppermute | solution.py:237
  119.4 13.7 %collective-permute-start.9 = (bf16[1,3,256,128]{3,2,1,0:T(8,128)(2,1)S(1)}, bf16[1,3,256,128]{3,2,1,0:T(8,128)(2,1)S(1)}, u32[]{:S(2)}, u32[]{:S(2)}) collective-permute-start(bf16[1,3,256,128]{3,2,1,0:T(8,128)(2,1)S(1)} %get-tuple-element.27), channel_id=1, source_target_pairs={{0,192},{32,224},{64,0},{96,32},{128,64},{160,96},{192,128},{224,1... | collective-permute-start | bytes 589832 | tf_op jit(solution)/shard_map/ppermute | solution.py:237
  124.6 10.3 %collective-permute-start.10 = (bf16[1,3,256,128]{3,2,1,0:T(8,128)(2,1)S(1)}, bf16[1,3,256,128]{3,2,1,0:T(8,128)(2,1)S(1)}, u32[]{:S(2)}, u32[]{:S(2)}) collective-permute-start(bf16[1,3,256,128]{3,2,1,0:T(8,128)(2,1)S(1)} %get-tuple-element.28), channel_id=1, source_target_pairs={{0,224},{32,192},{64,32},{96,0},{128,96},{160,64},{192,160},{224,1... | collective-permute-start | bytes 589832 | tf_op jit(solution)/shard_map/ppermute | solution.py:237

commit v3 on v2

--- a/solution.py
+++ b/solution.py
@@ -262,8 +262,10 @@
     clip_of_aim = jnp.max(jnp.where(hit, clip_index[None, :], -1), axis=1)
 
     pieces, entries = [], []
+    latents, to_swap = base_latents, []
     for chunk in range(CHUNKS):
-        hidden = conv_rows(base_latents, conv_weight, chunk * chunk_rows, chunk_rows)
+        hidden = conv_rows(latents, conv_weight, chunk * chunk_rows, chunk_rows)
+        latents, hidden = lax.optimization_barrier((latents, hidden))
         hidden = hidden.reshape(frames_dev, chunk_rows * tile_cols, channels).transpose(1, 0, 2)
         hidden = hidden.reshape(bands, px * frames_dev, channels)
         pencil = lax.all_to_all(hidden, "band", split_axis=0, concat_axis=0, tiled=True)
@@ -273,14 +275,17 @@
             packed = pack(
                 arrived, clip_of_aim, slots, [[2 * hop, 2 * hop + 1] for hop in range(chips)]
             )
-            landed = [to_chip(slab, hop, 0, groups) for hop, slab in enumerate(packed)]
-            swapped = to_chip(jnp.stack([slab[1] for slab in landed]), 0, 1, groups)
-            for hop, slab in enumerate(landed):
-                entries += [(len(pieces), 0, chunk, hop, 0), (chips, hop, chunk, hop, 1)]
-                pieces.append(slab)
-            pieces.append(swapped)
+            for hop, slab in enumerate(packed):
+                landed = to_chip(slab, hop, 0, groups)
+                entries.append((len(pieces), 0, chunk, hop, 0))
+                pieces.append(landed)
+                to_swap.append((landed, chunk, hop))
         else:
             packed = pack(arrived, clip_of_aim, slots, [[i] for i in range(groups)])
+            packed, landed = lax.optimization_barrier((packed, [slab for slab, _, _ in to_swap]))
+            swapped = to_chip(jnp.stack([slab[1] for slab in landed]), 0, 1, groups)
+            entries += [(len(pieces), at, of, hop, 1) for at, (_, of, hop) in enumerate(to_swap)]
+            pieces.append(swapped)
             for (hop, flip), slab in zip(aim_list, packed):
                 entries.append((len(pieces), 0, chunk, hop, flip))
                 pieces.append(to_chip(slab, hop, flip, groups))

time: 138 us -> 137 us (level)
  waiting for transfers between devices: 55.1 us -> 50.5 us
  starting transfers between devices: 44.3 us -> 47.1 us
    ppermute x11, waiting for transfers between devices: 31.6 us -> 16.1 us  [to_chip(): return lax.ppermute(value, 'group', pairs) if hop or flip else value]
    all_to_all x2, waiting for transfers between devices: 7.53 us -> 20.3 us  [body(): lax.all_to_all(refined, 'band', split_axis=0, concat_axis=0, tiled=True)]
    ppermute x11, starting transfers between devices: 13.7 us -> 16.2 us  [to_chip(): return lax.ppermute(value, 'group', pairs) if hop or flip else value]
    all_to_all x2, waiting for transfers between devices: 15.9 us -> 14 us  [body(): lax.all_to_all(hidden, 'band', split_axis=0, concat_axis=0, tiled=True)]
  transfers between devices with their start and end apart: 15 -> 15, of which waited for: 11 -> 11; matrix products, arithmetic and copies ran while one was open for 3% -> 4% of each run, Pallas kernels for 19% -> 19%
where the time goes in v3:
time: 137 us; the launch traced here: 136 us
  waiting for transfers between devices  50.5 us (37%)
  starting transfers between devices  47.1 us (34%)
  Pallas kernels  28.5 us (21%)
  matrix products  4.52 us (3%)
  local copies, waits for them, and re-layouts  3.2 us (2%)
  other arithmetic  1.74 us (1%)
    pallas_call x2, Pallas kernels, attention(): pl.pallas_call(functools.partial(attention_kernel, slots), out_shape=jax....  24.2 us
    all_to_all x2, waiting for transfers between devices, body(): lax.all_to_all(refined, 'band', split_axis=0, concat_axis=0, tiled=True)  20.3 us
    all_to_all x2, starting transfers between devices, body(): lax.all_to_all(hidden, 'band', split_axis=0, concat_axis=0, tiled=True)  17.4 us
    ppermute x11, starting transfers between devices, to_chip(): return lax.ppermute(value, 'group', pairs) if hop or flip else value  16.2 us
    ppermute x11, waiting for transfers between devices, to_chip(): return lax.ppermute(value, 'group', pairs) if hop or flip else value  16.1 us
    all_to_all x2, waiting for transfers between devices, body(): lax.all_to_all(hidden, 'band', split_axis=0, concat_axis=0, tiled=True)  14 us
    all_to_all x2, starting transfers between devices, body(): lax.all_to_all(refined, 'band', split_axis=0, concat_axis=0, tiled=True)  13.5 us
    conv_general_dilated x2, matrix products, conv_rows(): lax.conv_general_dilated(normed, conv_weight, (1, 1), ((1 - above, 1 - be...  4.52 us
  transfers between devices with their start and end apart: 15, of which 11 were waited for; matrix products, arithmetic and copies ran while one was open for 4% of the time, Pallas kernels for 19%

profile of v3, /device:TPU:1, one launch (start us, length us, event | category | flops | bytes accessed | tf_op | source)
XLA Modules:
  0.0 136.1 jit_solution(3631177063356771982)
XLA Ops:
  1.7 2.3 %fusion = bf16[8,16,16,128]{3,0,2,1:T(8,128)(2,1)} fusion(bf16[3,3,128,128]{3,2,1,0:T(8,128)(2,1)S(1)} %copy-done, f32[8,17,16,128]{3,0,2,1:T(8,128)S(1)} %copy_convert_fusion, f32[8,17,16]{0,2,1:T(8,128)S(1)} %add_rsqrt_fusion.1), kind=kOutput, calls=%fused_computation.2 | convolution fusion | flops 568950784 | bytes 3121152 | tf_op jit(solution)/shard_map/conv_general_dilated | solution.py:159
  4.0 12.2 %all-to-all-start = ((bf16[32,64,128]{2,1,0:T(8,128)(2,1)}), bf16[32,64,128]{2,1,0:T(8,128)(2,1)S(1)}, u32[]{:S(2)}, u32[]{:S(2)}) async-start(bf16[32,64,128]{2,1,0:T(8,128)(2,1)} %bitcast.14), calls=%async_computation | async-start | bytes 1048576 | tf_op jit(solution)/shard_map/all_to_all | solution.py:271
  18.5 2.2 %fusion.1 = bf16[8,16,16,128]{3,0,2,1:T(8,128)(2,1)} fusion(bf16[3,3,128,128]{3,2,1,0:T(8,128)(2,1)S(1)} %copy-done, f32[8,17,16,128]{3,0,2,1:T(8,128)S(1)} %slice_convert_fusion, f32[8,17,16]{0,2,1:T(8,128)S(1)} %add_rsqrt_fusion), kind=kOutput, calls=%fused_computation.3 | convolution fusion | flops 568950784 | bytes 3121152 | tf_op jit(solution)/shard_map/conv_general_dilated | solution.py:159
  21.1 11.3 %all-to-all-done.x_ref = bf16[32,64,128]{2,1,0:T(8,128)(2,1)S(1)} async-done(((bf16[32,64,128]{2,1,0:T(8,128)(2,1)}), bf16[32,64,128]{2,1,0:T(8,128)(2,1)S(1)}, u32[]{:S(2)}, u32[]{:S(2)}) %all-to-all-start) | async-done | bytes 524320 | tf_op jit(solution)/shard_map/all_to_all | solution.py:271
  32.4 5.2 %all-to-all-start.2 = ((bf16[32,64,128]{2,1,0:T(8,128)(2,1)}), bf16[32,64,128]{2,1,0:T(8,128)(2,1)S(1)}, u32[]{:S(2)}, u32[]{:S(2)}) async-start(bf16[32,64,128]{2,1,0:T(8,128)(2,1)} %bitcast.21), calls=%async_computation.2 | async-start | bytes 1048576 | tf_op jit(solution)/shard_map/all_to_all | solution.py:271
  37.9 12.1 %pool_attention.2 = bf16[32,12,8,128]{3,2,1,0:T(8,128)(2,1)} custom-call(s32[4]{0:T(128)S(1)} %bitcast_subtract_fusion.1.starts, s32[4]{0:T(128)S(1)} %bitcast.38, bf16[32,64,128]{2,1,0:T(8,128)(2,1)S(1)} %all-to-all-done.x_ref, bf16[128,256]{1,0:T(8,128)(2,1)S(1)} %pad_maximum_fusion.2.wqv_ref, bf16[128,128]{1,0:T(8,128)(2,1)S(1)} %bitcast.35, ...), custom_call_target="tpu_custom_call" | custom-call | flops 2097152000 | bytes 4194304 | tf_op jit(solution)/shard_map/pool_attention/pallas_call | solution.py:129
  50.0 2.7 %all-to-all-done.2.x_ref = bf16[32,64,128]{2,1,0:T(8,128)(2,1)S(1)} async-done(((bf16[32,64,128]{2,1,0:T(8,128)(2,1)}), bf16[32,64,128]{2,1,0:T(8,128)(2,1)S(1)}, u32[]{:S(2)}, u32[]{:S(2)}) %all-to-all-start.2) | async-done | bytes 524320 | tf_op jit(solution)/shard_map/all_to_all | solution.py:271
  52.7 6.7 %all-to-all-start.1 = ((bf16[32,12,8,128]{3,2,1,0:T(8,128)(2,1)}), bf16[32,12,8,128]{3,2,1,0:T(8,128)(2,1)S(1)}, u32[]{:S(2)}, u32[]{:S(2)}) async-start(bf16[32,12,8,128]{3,2,1,0:T(8,128)(2,1)} %pool_attention.2), calls=%async_computation.1 | async-start | bytes 1572864 | tf_op jit(solution)/shard_map/all_to_all | solution.py:273
  59.4 12.1 %pool_attention.3 = bf16[32,12,8,128]{3,2,1,0:T(8,128)(2,1)} custom-call(s32[4]{0:T(128)S(1)} %bitcast_subtract_fusion.1.starts, s32[4]{0:T(128)S(1)} %bitcast.39, bf16[32,64,128]{2,1,0:T(8,128)(2,1)S(1)} %all-to-all-done.2.x_ref, bf16[128,256]{1,0:T(8,128)(2,1)S(1)} %pad_maximum_fusion.2.wqv_ref, bf16[128,128]{1,0:T(8,128)(2,1)S(1)} %bitcast.36, ...), custom_call_target="tpu_custom_call" | custom-call | flops 2097152000 | bytes 4194304 | tf_op jit(solution)/shard_map/pool_attention/pallas_call | solution.py:129
  71.5 7.3 %all-to-all-done.1.y_ref = bf16[32,12,8,128]{3,2,1,0:T(8,128)(2,1)S(1)} async-done(((bf16[32,12,8,128]{3,2,1,0:T(8,128)(2,1)}), bf16[32,12,8,128]{3,2,1,0:T(8,128)(2,1)S(1)}, u32[]{:S(2)}, u32[]{:S(2)}) %all-to-all-start.1) | async-done | bytes 786464 | tf_op jit(solution)/shard_map/all_to_all | solution.py:273
  78.8 6.7 %all-to-all-start.3 = ((bf16[32,12,8,128]{3,2,1,0:T(8,128)(2,1)}), bf16[32,12,8,128]{3,2,1,0:T(8,128)(2,1)S(1)}, u32[]{:S(2)}, u32[]{:S(2)}) async-start(bf16[32,12,8,128]{3,2,1,0:T(8,128)(2,1)} %pool_attention.3), calls=%async_computation.3 | async-start | bytes 1572864 | tf_op jit(solution)/shard_map/all_to_all | solution.py:273
  86.0 1.5 %pack_slots.2 = (bf16[2,3,256,128]{3,2,1,0:T(8,128)(2,1)S(1)}, bf16[2,3,256,128]{3,2,1,0:T(8,128)(2,1)}, bf16[2,3,256,128]{3,2,1,0:T(8,128)(2,1)S(1)}, bf16[2,3,256,128]{3,2,1,0:T(8,128)(2,1)S(1)}) custom-call(s32[8]{0:T(128)S(1)} %select_reduce_fusion.clip_ref, bf16[32,12,8,128]{3,2,1,0:T(8,128)(2,1)S(1)} %all-to-all-done.1.y_ref), custom_call_target="tpu_custom_call" | custom-call | bytes 2097152 | tf_op jit(solution)/shard_map/pack_slots/pallas_call | solution.py:184
  88.7 2.5 %collective-permute-start.1 = (bf16[2,3,256,128]{3,2,1,0:T(8,128)(2,1)S(1)}, bf16[2,3,256,128]{3,2,1,0:T(8,128)(2,1)S(1)}, u32[]{:S(2)}, u32[]{:S(2)}) collective-permute-start(bf16[2,3,256,128]{3,2,1,0:T(8,128)(2,1)S(1)} %get-tuple-element.35), channel_id=1, source_target_pairs={{0,128},{32,160},{64,192},{96,224},{128,0},{160,32},{192,64},{224,... | collective-permute-start | bytes 1179656 | tf_op jit(solution)/shard_map/ppermute | solution.py:237
  92.3 13.0 %all-to-all-done.3.y_ref = bf16[32,12,8,128]{3,2,1,0:T(8,128)(2,1)S(1)} async-done(((bf16[32,12,8,128]{3,2,1,0:T(8,128)(2,1)}), bf16[32,12,8,128]{3,2,1,0:T(8,128)(2,1)S(1)}, u32[]{:S(2)}, u32[]{:S(2)}) %all-to-all-start.3) | async-done | bytes 786464 | tf_op jit(solution)/shard_map/all_to_all | solution.py:273
  107.7 3.1 %collective-permute-start.3 = (bf16[4,3,256,128]{3,2,1,0:T(8,128)(2,1)S(1)}, bf16[4,3,256,128]{3,2,1,0:T(8,128)(2,1)S(1)}, u32[]{:S(2)}, u32[]{:S(2)}) collective-permute-start(bf16[4,3,256,128]{3,2,1,0:T(8,128)(2,1)S(1)} %pad_maximum_fusion), channel_id=1, source_target_pairs={{0,32},{32,0},{64,96},{96,64},{128,160},{160,128},{192,224},{224,1... | collective-permute-start | bytes 2359304 | tf_op jit(solution)/shard_map/ppermute | solution.py:237
  112.2 1.8 %collective-permute-start.6 = (bf16[1,3,256,128]{3,2,1,0:T(8,128)(2,1)S(1)}, bf16[1,3,256,128]{3,2,1,0:T(8,128)(2,1)S(1)}, u32[]{:S(2)}, u32[]{:S(2)}) collective-permute-start(bf16[1,3,256,128]{3,2,1,0:T(8,128)(2,1)S(1)} %get-tuple-element.54), channel_id=1, source_target_pairs={{0,96},{32,64},{64,160},{96,128},{128,224},{160,192},{192,32},{224... | collective-permute-start | bytes 589832 | tf_op jit(solution)/shard_map/ppermute | solution.py:237
  113.9 1.4 %collective-permute-start.7 = (bf16[1,3,256,128]{3,2,1,0:T(8,128)(2,1)S(1)}, bf16[1,3,256,128]{3,2,1,0:T(8,128)(2,1)S(1)}, u32[]{:S(2)}, u32[]{:S(2)}) collective-permute-start(bf16[1,3,256,128]{3,2,1,0:T(8,128)(2,1)S(1)} %get-tuple-element.55), channel_id=1, source_target_pairs={{0,128},{32,160},{64,192},{96,224},{128,0},{160,32},{192,64},{224,... | collective-permute-start | bytes 589832 | tf_op jit(solution)/shard_map/ppermute | solution.py:237
  115.4 1.5 %collective-permute-start.8 = (bf16[1,3,256,128]{3,2,1,0:T(8,128)(2,1)S(1)}, bf16[1,3,256,128]{3,2,1,0:T(8,128)(2,1)S(1)}, u32[]{:S(2)}, u32[]{:S(2)}) collective-permute-start(bf16[1,3,256,128]{3,2,1,0:T(8,128)(2,1)S(1)} %get-tuple-element.56), channel_id=1, source_target_pairs={{0,160},{32,128},{64,224},{96,192},{128,32},{160,0},{192,96},{224,... | collective-permute-start | bytes 589832 | tf_op jit(solution)/shard_map/ppermute | solution.py:237
  116.9 1.3 collective-permute-done.5.refs_7_
  119.5 3.5 %collective-permute-done.6.refs_8_ = bf16[1,3,256,128]{3,2,1,0:T(8,128)(2,1)S(1)} collective-permute-done((bf16[1,3,256,128]{3,2,1,0:T(8,128)(2,1)S(1)}, bf16[1,3,256,128]{3,2,1,0:T(8,128)(2,1)S(1)}, u32[]{:S(2)}, u32[]{:S(2)}) %collective-permute-start.6) | collective-permute-done | bytes 196640 | tf_op jit(solution)/shard_map/ppermute | solution.py:237
  124.0 3.6 %collective-permute-done.7.refs_9_ = bf16[1,3,256,128]{3,2,1,0:T(8,128)(2,1)S(1)} collective-permute-done((bf16[1,3,256,128]{3,2,1,0:T(8,128)(2,1)S(1)}, bf16[1,3,256,128]{3,2,1,0:T(8,128)(2,1)S(1)}, u32[]{:S(2)}, u32[]{:S(2)}) %collective-permute-start.7) | collective-permute-done | bytes 196640 | tf_op jit(solution)/shard_map/ppermute | solution.py:237
  127.6 4.8 %collective-permute-done.8.refs_10_ = bf16[1,3,256,128]{3,2,1,0:T(8,128)(2,1)S(1)} collective-permute-done((bf16[1,3,256,128]{3,2,1,0:T(8,128)(2,1)S(1)}, bf16[1,3,256,128]{3,2,1,0:T(8,128)(2,1)S(1)}, u32[]{:S(2)}, u32[]{:S(2)}) %collective-permute-start.8) | collective-permute-done | bytes 196640 | tf_op jit(solution)/shard_map/ppermute | solution.py:237
  132.4 1.4 %collective-permute-done.10.refs_12_ = bf16[1,3,256,128]{3,2,1,0:T(8,128)(2,1)S(1)} collective-permute-done((bf16[1,3,256,128]{3,2,1,0:T(8,128)(2,1)S(1)}, bf16[1,3,256,128]{3,2,1,0:T(8,128)(2,1)S(1)}, u32[]{:S(2)}, u32[]{:S(2)}) %collective-permute-start.10) | collective-permute-done | bytes 196640 | tf_op jit(solution)/shard_map/ppermute | solution.py:237
  133.9 2.0 %place_slots.1 = bf16[24,512,128]{2,1,0:T(8,128)(2,1)} custom-call(s32[1]{0:T(128)} %bitcast.me_ref, bf16[2,3,256,128]{3,2,1,0:T(8,128)(2,1)S(1)} %get-tuple-element.47.refs_0_, bf16[2,3,256,128]{3,2,1,0:T(8,128)(2,1)S(1)} %collective-permute-done.refs_1_, bf16[2,3,256,128]{3,2,1,0:T(8,128)(2,1)S(1)} %collective-permute-done.1.refs_2_, ...), custom_call_target="tpu_custom_call" | custom-call | bytes 6291456 | tf_op jit(solution)/shard_map/place_slots/pallas_call | solution.py:219
  (65 shorter events, 13.1 us)
Async XLA Ops:
  0.0 1.7 %copy-start = (bf16[3,3,128,128]{3,2,1,0:T(8,128)(2,1)S(1)}, bf16[3,3,128,128]{3,2,1,0:T(8,128)(2,1)}, u32[]{:S(2)}) copy-start(bf16[3,3,128,128]{3,2,1,0:T(8,128)(2,1)} %param.12) | copy-start | bytes 884740
  4.0 12.2 %copy-start.5 = (bf16[8,32,16,128]{3,2,1,0:T(8,128)(2,1)S(1)}, bf16[8,32,16,128]{3,2,1,0:T(8,128)(2,1)}, u32[]{:S(2)}) copy-start(bf16[8,32,16,128]{3,2,1,0:T(8,128)(2,1)} %param.9) | copy-start | bytes 3145732
  4.0 28.5 %all-to-all-start = ((bf16[32,64,128]{2,1,0:T(8,128)(2,1)}), bf16[32,64,128]{2,1,0:T(8,128)(2,1)S(1)}, u32[]{:S(2)}, u32[]{:S(2)}) async-start(bf16[32,64,128]{2,1,0:T(8,128)(2,1)} %bitcast.14), calls=%async_computation | async-start | bytes 1048576 | tf_op jit(solution)/shard_map/all_to_all | solution.py:271
  17.4 0.7 copy-start.8
  18.4 2.6 %copy-start.6 = (bf16[128,384]{1,0:T(8,128)(2,1)S(1)}, bf16[128,384]{1,0:T(8,128)(2,1)}, u32[]{:S(2)}) copy-start(bf16[128,384]{1,0:T(8,128)(2,1)} %param.13) | copy-start | bytes 294916
  20.7 17.2 %copy-start.1 = (bf16[128,512]{1,0:T(8,128)(2,1)S(1)}, bf16[128,512]{1,0:T(8,128)(2,1)}, u32[]{:S(2)}) copy-start(bf16[128,512]{1,0:T(8,128)(2,1)} %wup_ref.3) | copy-start | bytes 393220
  20.7 17.2 %copy-start.2 = (bf16[512,128]{1,0:T(8,128)(2,1)S(1)}, bf16[512,128]{1,0:T(8,128)(2,1)}, u32[]{:S(2)}) copy-start(bf16[512,128]{1,0:T(8,128)(2,1)} %wdown_ref.3) | copy-start | bytes 393220
  20.7 17.2 %copy-start.3 = (bf16[128,128]{1,0:T(8,128)(2,1)S(1)}, bf16[128,128]{1,0:T(8,128)(2,1)}, u32[]{:S(2)}) copy-start(bf16[128,128]{1,0:T(8,128)(2,1)} %wout_ref.3) | copy-start | bytes 98308
  20.7 17.2 %copy-start.4 = (f32[128]{0:T(128)S(1)}, f32[128]{0:T(128)}, u32[]{:S(2)}) copy-start(f32[128]{0:T(128)} %param.14) | copy-start | bytes 1540
  32.4 20.3 %all-to-all-start.2 = ((bf16[32,64,128]{2,1,0:T(8,128)(2,1)}), bf16[32,64,128]{2,1,0:T(8,128)(2,1)S(1)}, u32[]{:S(2)}, u32[]{:S(2)}) async-start(bf16[32,64,128]{2,1,0:T(8,128)(2,1)} %bitcast.21), calls=%async_computation.2 | async-start | bytes 1048576 | tf_op jit(solution)/shard_map/all_to_all | solution.py:271
  52.7 26.2 %all-to-all-start.1 = ((bf16[32,12,8,128]{3,2,1,0:T(8,128)(2,1)}), bf16[32,12,8,128]{3,2,1,0:T(8,128)(2,1)S(1)}, u32[]{:S(2)}, u32[]{:S(2)}) async-start(bf16[32,12,8,128]{3,2,1,0:T(8,128)(2,1)} %pool_attention.2), calls=%async_computation.1 | async-start | bytes 1572864 | tf_op jit(solution)/shard_map/all_to_all | solution.py:273
  71.5 14.1 %copy-start.7 = (s32[8,4]{0,1:T(4,128)S(1)}, s32[8,4]{0,1:T(4,128)}, u32[]{:S(2)}) copy-start(s32[8,4]{0,1:T(4,128)} %param.11) | copy-start | bytes 388
  78.8 26.4 %all-to-all-start.3 = ((bf16[32,12,8,128]{3,2,1,0:T(8,128)(2,1)}), bf16[32,12,8,128]{3,2,1,0:T(8,128)(2,1)S(1)}, u32[]{:S(2)}, u32[]{:S(2)}) async-start(bf16[32,12,8,128]{3,2,1,0:T(8,128)(2,1)} %pool_attention.3), calls=%async_computation.3 | async-start | bytes 1572864 | tf_op jit(solution)/shard_map/all_to_all | solution.py:273
  87.5 18.6 %collective-permute-start = (bf16[2,3,256,128]{3,2,1,0:T(8,128)(2,1)}, bf16[2,3,256,128]{3,2,1,0:T(8,128)(2,1)S(1)}, u32[]{:S(2)}, u32[]{:S(2)}) collective-permute-start(bf16[2,3,256,128]{3,2,1,0:T(8,128)(2,1)} %get-tuple-element.34), channel_id=1, source_target_pairs={{0,64},{32,96},{64,128},{96,160},{128,192},{160,224},{192,0},{224,... | collective-permute-start | bytes 1179656 | tf_op jit(solution)/shard_map/ppermute | solution.py:237
  88.7 17.6 %collective-permute-start.1 = (bf16[2,3,256,128]{3,2,1,0:T(8,128)(2,1)S(1)}, bf16[2,3,256,128]{3,2,1,0:T(8,128)(2,1)S(1)}, u32[]{:S(2)}, u32[]{:S(2)}) collective-permute-start(bf16[2,3,256,128]{3,2,1,0:T(8,128)(2,1)S(1)} %get-tuple-element.35), channel_id=1, source_target_pairs={{0,128},{32,160},{64,192},{96,224},{128,0},{160,32},{192,64},{224,... | collective-permute-start | bytes 1179656 | tf_op jit(solution)/shard_map/ppermute | solution.py:237
  91.1 16.4 %collective-permute-start.2 = (bf16[2,3,256,128]{3,2,1,0:T(8,128)(2,1)S(1)}, bf16[2,3,256,128]{3,2,1,0:T(8,128)(2,1)S(1)}, u32[]{:S(2)}, u32[]{:S(2)}) collective-permute-start(bf16[2,3,256,128]{3,2,1,0:T(8,128)(2,1)S(1)} %get-tuple-element.36), channel_id=1, source_target_pairs={{0,192},{32,224},{64,0},{96,32},{128,64},{160,96},{192,128},{224,1... | collective-permute-start | bytes 1179656 | tf_op jit(solution)/shard_map/ppermute | solution.py:237
  107.7 26.1 %collective-permute-start.3 = (bf16[4,3,256,128]{3,2,1,0:T(8,128)(2,1)S(1)}, bf16[4,3,256,128]{3,2,1,0:T(8,128)(2,1)S(1)}, u32[]{:S(2)}, u32[]{:S(2)}) collective-permute-start(bf16[4,3,256,128]{3,2,1,0:T(8,128)(2,1)S(1)} %pad_maximum_fusion), channel_id=1, source_target_pairs={{0,32},{32,0},{64,96},{96,64},{128,160},{160,128},{192,224},{224,1... | collective-permute-start | bytes 2359304 | tf_op jit(solution)/shard_map/ppermute | solution.py:237
  110.8 4.5 %collective-permute-start.4 = (bf16[1,3,256,128]{3,2,1,0:T(8,128)(2,1)S(1)}, bf16[1,3,256,128]{3,2,1,0:T(8,128)(2,1)S(1)}, u32[]{:S(2)}, u32[]{:S(2)}) collective-permute-start(bf16[1,3,256,128]{3,2,1,0:T(8,128)(2,1)S(1)} %get-tuple-element.52), channel_id=1, source_target_pairs={{0,32},{32,0},{64,96},{96,64},{128,160},{160,128},{192,224},{224,1... | collective-permute-start | bytes 589832 | tf_op jit(solution)/shard_map/ppermute | solution.py:237
  110.9 7.3 %collective-permute-start.5 = (bf16[1,3,256,128]{3,2,1,0:T(8,128)(2,1)S(1)}, bf16[1,3,256,128]{3,2,1,0:T(8,128)(2,1)S(1)}, u32[]{:S(2)}, u32[]{:S(2)}) collective-permute-start(bf16[1,3,256,128]{3,2,1,0:T(8,128)(2,1)S(1)} %get-tuple-element.53), channel_id=1, source_target_pairs={{0,64},{32,96},{64,128},{96,160},{128,192},{160,224},{192,0},{224,... | collective-permute-start | bytes 589832 | tf_op jit(solution)/shard_map/ppermute | solution.py:237
  112.2 10.8 %collective-permute-start.6 = (bf16[1,3,256,128]{3,2,1,0:T(8,128)(2,1)S(1)}, bf16[1,3,256,128]{3,2,1,0:T(8,128)(2,1)S(1)}, u32[]{:S(2)}, u32[]{:S(2)}) collective-permute-start(bf16[1,3,256,128]{3,2,1,0:T(8,128)(2,1)S(1)} %get-tuple-element.54), channel_id=1, source_target_pairs={{0,96},{32,64},{64,160},{96,128},{128,224},{160,192},{192,32},{224... | collective-permute-start | bytes 589832 | tf_op jit(solution)/shard_map/ppermute | solution.py:237
  113.9 13.7 %collective-permute-start.7 = (bf16[1,3,256,128]{3,2,1,0:T(8,128)(2,1)S(1)}, bf16[1,3,256,128]{3,2,1,0:T(8,128)(2,1)S(1)}, u32[]{:S(2)}, u32[]{:S(2)}) collective-permute-start(bf16[1,3,256,128]{3,2,1,0:T(8,128)(2,1)S(1)} %get-tuple-element.55), channel_id=1, source_target_pairs={{0,128},{32,160},{64,192},{96,224},{128,0},{160,32},{192,64},{224,... | collective-permute-start | bytes 589832 | tf_op jit(solution)/shard_map/ppermute | solution.py:237
  115.4 17.0 %collective-permute-start.8 = (bf16[1,3,256,128]{3,2,1,0:T(8,128)(2,1)S(1)}, bf16[1,3,256,128]{3,2,1,0:T(8,128)(2,1)S(1)}, u32[]{:S(2)}, u32[]{:S(2)}) collective-permute-start(bf16[1,3,256,128]{3,2,1,0:T(8,128)(2,1)S(1)} %get-tuple-element.56), channel_id=1, source_target_pairs={{0,160},{32,128},{64,224},{96,192},{128,32},{160,0},{192,96},{224,... | collective-permute-start | bytes 589832 | tf_op jit(solution)/shard_map/ppermute | solution.py:237
  118.2 14.2 %collective-permute-start.9 = (bf16[1,3,256,128]{3,2,1,0:T(8,128)(2,1)S(1)}, bf16[1,3,256,128]{3,2,1,0:T(8,128)(2,1)S(1)}, u32[]{:S(2)}, u32[]{:S(2)}) collective-permute-start(bf16[1,3,256,128]{3,2,1,0:T(8,128)(2,1)S(1)} %get-tuple-element.57), channel_id=1, source_target_pairs={{0,192},{32,224},{64,0},{96,32},{128,64},{160,96},{192,128},{224,1... | collective-permute-start | bytes 589832 | tf_op jit(solution)/shard_map/ppermute | solution.py:237
  123.0 10.9 %collective-permute-start.10 = (bf16[1,3,256,128]{3,2,1,0:T(8,128)(2,1)S(1)}, bf16[1,3,256,128]{3,2,1,0:T(8,128)(2,1)S(1)}, u32[]{:S(2)}, u32[]{:S(2)}) collective-permute-start(bf16[1,3,256,128]{3,2,1,0:T(8,128)(2,1)S(1)} %get-tuple-element.58), channel_id=1, source_target_pairs={{0,224},{32,192},{64,32},{96,0},{128,96},{160,64},{192,160},{224,1... | collective-permute-start | bytes 589832 | tf_op jit(solution)/shard_map/ppermute | solution.py:237

commit v4 on v3

--- a/solution.py
+++ b/solution.py
@@ -286,9 +286,9 @@
             swapped = to_chip(jnp.stack([slab[1] for slab in landed]), 0, 1, groups)
             entries += [(len(pieces), at, of, hop, 1) for at, (_, of, hop) in enumerate(to_swap)]
             pieces.append(swapped)
-            for (hop, flip), slab in zip(aim_list, packed):
+            for hop, flip in ((2, 0), (1, 0), (3, 0), (2, 1), (1, 1), (3, 1), (0, 1), (0, 0)):
                 entries.append((len(pieces), 0, chunk, hop, flip))
-                pieces.append(to_chip(slab, hop, flip, groups))
+                pieces.append(to_chip(packed[aim_list.index((hop, flip))], hop, flip, groups))
     placed = place(pieces, entries, me, groups, pixels)
     return placed.reshape(1, slots * groups, tile_rows, tile_cols, channels)
 

time: 137 us -> 135 us (0.985)
  waiting for transfers between devices: 50.5 us -> 48.2 us
    ppermute x11, waiting for transfers between devices: 16.1 us -> 13.9 us  [to_chip(): return lax.ppermute(value, 'group', pairs) if hop or flip else value]
  transfers between devices with their start and end apart: 15 -> 15, of which waited for: 11 -> 10; matrix products, arithmetic and copies ran while one was open for 4% -> 4% of each run, Pallas kernels for 19% -> 20%
where the time goes in v4:
time: 135 us; the launch traced here: 134 us
  waiting for transfers between devices  48.2 us (36%)
  starting transfers between devices  47.4 us (35%)
  Pallas kernels  28.5 us (21%)
  matrix products  4.52 us (3%)
  local copies, waits for them, and re-layouts  3.2 us (2%)
  other arithmetic  1.74 us (1%)
    pallas_call x2, Pallas kernels, attention(): pl.pallas_call(functools.partial(attention_kernel, slots), out_shape=jax....  24.2 us
    all_to_all x2, waiting for transfers between devices, body(): lax.all_to_all(refined, 'band', split_axis=0, concat_axis=0, tiled=True)  20.3 us
    all_to_all x2, starting transfers between devices, body(): lax.all_to_all(hidden, 'band', split_axis=0, concat_axis=0, tiled=True)  17.4 us
    ppermute x11, starting transfers between devices, to_chip(): return lax.ppermute(value, 'group', pairs) if hop or flip else value  16.6 us
    all_to_all x2, waiting for transfers between devices, body(): lax.all_to_all(hidden, 'band', split_axis=0, concat_axis=0, tiled=True)  14 us
    ppermute x11, waiting for transfers between devices, to_chip(): return lax.ppermute(value, 'group', pairs) if hop or flip else value  13.9 us
    all_to_all x2, starting transfers between devices, body(): lax.all_to_all(refined, 'band', split_axis=0, concat_axis=0, tiled=True)  13.5 us
    conv_general_dilated x2, matrix products, conv_rows(): lax.conv_general_dilated(normed, conv_weight, (1, 1), ((1 - above, 1 - be...  4.52 us
  transfers between devices with their start and end apart: 15, of which 10 were waited for; matrix products, arithmetic and copies ran while one was open for 4% of the time, Pallas kernels for 20%

profile of v4, /device:TPU:1, one launch (start us, length us, event | category | flops | bytes accessed | tf_op | source)
XLA Modules:
  0.0 134.2 jit_solution(12870726915576923240)
XLA Ops:
  1.7 2.3 %fusion = bf16[8,16,16,128]{3,0,2,1:T(8,128)(2,1)} fusion(bf16[3,3,128,128]{3,2,1,0:T(8,128)(2,1)S(1)} %copy-done, f32[8,17,16,128]{3,0,2,1:T(8,128)S(1)} %copy_convert_fusion, f32[8,17,16]{0,2,1:T(8,128)S(1)} %add_rsqrt_fusion.1), kind=kOutput, calls=%fused_computation.2 | convolution fusion | flops 568950784 | bytes 3121152 | tf_op jit(solution)/shard_map/conv_general_dilated | solution.py:159
  4.0 12.2 %all-to-all-start = ((bf16[32,64,128]{2,1,0:T(8,128)(2,1)}), bf16[32,64,128]{2,1,0:T(8,128)(2,1)S(1)}, u32[]{:S(2)}, u32[]{:S(2)}) async-start(bf16[32,64,128]{2,1,0:T(8,128)(2,1)} %bitcast.14), calls=%async_computation | async-start | bytes 1048576 | tf_op jit(solution)/shard_map/all_to_all | solution.py:271
  18.5 2.2 %fusion.1 = bf16[8,16,16,128]{3,0,2,1:T(8,128)(2,1)} fusion(bf16[3,3,128,128]{3,2,1,0:T(8,128)(2,1)S(1)} %copy-done, f32[8,17,16,128]{3,0,2,1:T(8,128)S(1)} %slice_convert_fusion, f32[8,17,16]{0,2,1:T(8,128)S(1)} %add_rsqrt_fusion), kind=kOutput, calls=%fused_computation.3 | convolution fusion | flops 568950784 | bytes 3121152 | tf_op jit(solution)/shard_map/conv_general_dilated | solution.py:159
  21.1 11.3 %all-to-all-done.x_ref = bf16[32,64,128]{2,1,0:T(8,128)(2,1)S(1)} async-done(((bf16[32,64,128]{2,1,0:T(8,128)(2,1)}), bf16[32,64,128]{2,1,0:T(8,128)(2,1)S(1)}, u32[]{:S(2)}, u32[]{:S(2)}) %all-to-all-start) | async-done | bytes 524320 | tf_op jit(solution)/shard_map/all_to_all | solution.py:271
  32.4 5.2 %all-to-all-start.2 = ((bf16[32,64,128]{2,1,0:T(8,128)(2,1)}), bf16[32,64,128]{2,1,0:T(8,128)(2,1)S(1)}, u32[]{:S(2)}, u32[]{:S(2)}) async-start(bf16[32,64,128]{2,1,0:T(8,128)(2,1)} %bitcast.21), calls=%async_computation.2 | async-start | bytes 1048576 | tf_op jit(solution)/shard_map/all_to_all | solution.py:271
  37.9 12.1 %pool_attention.2 = bf16[32,12,8,128]{3,2,1,0:T(8,128)(2,1)} custom-call(s32[4]{0:T(128)S(1)} %bitcast_subtract_fusion.1.starts, s32[4]{0:T(128)S(1)} %bitcast.38, bf16[32,64,128]{2,1,0:T(8,128)(2,1)S(1)} %all-to-all-done.x_ref, bf16[128,256]{1,0:T(8,128)(2,1)S(1)} %pad_maximum_fusion.2.wqv_ref, bf16[128,128]{1,0:T(8,128)(2,1)S(1)} %bitcast.35, ...), custom_call_target="tpu_custom_call" | custom-call | flops 2097152000 | bytes 4194304 | tf_op jit(solution)/shard_map/pool_attention/pallas_call | solution.py:129
  50.0 2.7 %all-to-all-done.2.x_ref = bf16[32,64,128]{2,1,0:T(8,128)(2,1)S(1)} async-done(((bf16[32,64,128]{2,1,0:T(8,128)(2,1)}), bf16[32,64,128]{2,1,0:T(8,128)(2,1)S(1)}, u32[]{:S(2)}, u32[]{:S(2)}) %all-to-all-start.2) | async-done | bytes 524320 | tf_op jit(solution)/shard_map/all_to_all | solution.py:271
  52.7 6.7 %all-to-all-start.1 = ((bf16[32,12,8,128]{3,2,1,0:T(8,128)(2,1)}), bf16[32,12,8,128]{3,2,1,0:T(8,128)(2,1)S(1)}, u32[]{:S(2)}, u32[]{:S(2)}) async-start(bf16[32,12,8,128]{3,2,1,0:T(8,128)(2,1)} %pool_attention.2), calls=%async_computation.1 | async-start | bytes 1572864 | tf_op jit(solution)/shard_map/all_to_all | solution.py:273
  59.4 12.1 %pool_attention.3 = bf16[32,12,8,128]{3,2,1,0:T(8,128)(2,1)} custom-call(s32[4]{0:T(128)S(1)} %bitcast_subtract_fusion.1.starts, s32[4]{0:T(128)S(1)} %bitcast.39, bf16[32,64,128]{2,1,0:T(8,128)(2,1)S(1)} %all-to-all-done.2.x_ref, bf16[128,256]{1,0:T(8,128)(2,1)S(1)} %pad_maximum_fusion.2.wqv_ref, bf16[128,128]{1,0:T(8,128)(2,1)S(1)} %bitcast.36, ...), custom_call_target="tpu_custom_call" | custom-call | flops 2097152000 | bytes 4194304 | tf_op jit(solution)/shard_map/pool_attention/pallas_call | solution.py:129
  71.5 7.3 %all-to-all-done.1.y_ref = bf16[32,12,8,128]{3,2,1,0:T(8,128)(2,1)S(1)} async-done(((bf16[32,12,8,128]{3,2,1,0:T(8,128)(2,1)}), bf16[32,12,8,128]{3,2,1,0:T(8,128)(2,1)S(1)}, u32[]{:S(2)}, u32[]{:S(2)}) %all-to-all-start.1) | async-done | bytes 786464 | tf_op jit(solution)/shard_map/all_to_all | solution.py:273
  78.8 6.7 %all-to-all-start.3 = ((bf16[32,12,8,128]{3,2,1,0:T(8,128)(2,1)}), bf16[32,12,8,128]{3,2,1,0:T(8,128)(2,1)S(1)}, u32[]{:S(2)}, u32[]{:S(2)}) async-start(bf16[32,12,8,128]{3,2,1,0:T(8,128)(2,1)} %pool_attention.3), calls=%async_computation.3 | async-start | bytes 1572864 | tf_op jit(solution)/shard_map/all_to_all | solution.py:273
  86.0 1.5 %pack_slots.2 = (bf16[2,3,256,128]{3,2,1,0:T(8,128)(2,1)S(1)}, bf16[2,3,256,128]{3,2,1,0:T(8,128)(2,1)}, bf16[2,3,256,128]{3,2,1,0:T(8,128)(2,1)S(1)}, bf16[2,3,256,128]{3,2,1,0:T(8,128)(2,1)S(1)}) custom-call(s32[8]{0:T(128)S(1)} %select_reduce_fusion.clip_ref, bf16[32,12,8,128]{3,2,1,0:T(8,128)(2,1)S(1)} %all-to-all-done.1.y_ref), custom_call_target="tpu_custom_call" | custom-call | bytes 2097152 | tf_op jit(solution)/shard_map/pack_slots/pallas_call | solution.py:184
  88.7 2.5 %collective-permute-start.1 = (bf16[2,3,256,128]{3,2,1,0:T(8,128)(2,1)S(1)}, bf16[2,3,256,128]{3,2,1,0:T(8,128)(2,1)S(1)}, u32[]{:S(2)}, u32[]{:S(2)}) collective-permute-start(bf16[2,3,256,128]{3,2,1,0:T(8,128)(2,1)S(1)} %get-tuple-element.35), channel_id=1, source_target_pairs={{0,128},{32,160},{64,192},{96,224},{128,0},{160,32},{192,64},{224,... | collective-permute-start | bytes 1179656 | tf_op jit(solution)/shard_map/ppermute | solution.py:237
  92.3 13.0 %all-to-all-done.3.y_ref = bf16[32,12,8,128]{3,2,1,0:T(8,128)(2,1)S(1)} async-done(((bf16[32,12,8,128]{3,2,1,0:T(8,128)(2,1)}), bf16[32,12,8,128]{3,2,1,0:T(8,128)(2,1)S(1)}, u32[]{:S(2)}, u32[]{:S(2)}) %all-to-all-start.3) | async-done | bytes 786464 | tf_op jit(solution)/shard_map/all_to_all | solution.py:273
  106.3 1.2 collective-permute-done.2.refs_3_
  107.7 3.1 %collective-permute-start.3 = (bf16[4,3,256,128]{3,2,1,0:T(8,128)(2,1)S(1)}, bf16[4,3,256,128]{3,2,1,0:T(8,128)(2,1)S(1)}, u32[]{:S(2)}, u32[]{:S(2)}) collective-permute-start(bf16[4,3,256,128]{3,2,1,0:T(8,128)(2,1)S(1)} %pad_maximum_fusion), channel_id=1, source_target_pairs={{0,32},{32,0},{64,96},{96,64},{128,160},{160,128},{192,224},{224,1... | collective-permute-start | bytes 2359304 | tf_op jit(solution)/shard_map/ppermute | solution.py:237
  110.8 2.8 %collective-permute-start.4 = (bf16[1,3,256,128]{3,2,1,0:T(8,128)(2,1)S(1)}, bf16[1,3,256,128]{3,2,1,0:T(8,128)(2,1)S(1)}, u32[]{:S(2)}, u32[]{:S(2)}) collective-permute-start(bf16[1,3,256,128]{3,2,1,0:T(8,128)(2,1)S(1)} %get-tuple-element.51), channel_id=1, source_target_pairs={{0,128},{32,160},{64,192},{96,224},{128,0},{160,32},{192,64},{224,... | collective-permute-start | bytes 589832 | tf_op jit(solution)/shard_map/ppermute | solution.py:237
  113.9 2.4 %collective-permute-start.6 = (bf16[1,3,256,128]{3,2,1,0:T(8,128)(2,1)S(1)}, bf16[1,3,256,128]{3,2,1,0:T(8,128)(2,1)S(1)}, u32[]{:S(2)}, u32[]{:S(2)}) collective-permute-start(bf16[1,3,256,128]{3,2,1,0:T(8,128)(2,1)S(1)} %get-tuple-element.53), channel_id=1, source_target_pairs={{0,192},{32,224},{64,0},{96,32},{128,64},{160,96},{192,128},{224,1... | collective-permute-start | bytes 589832 | tf_op jit(solution)/shard_map/ppermute | solution.py:237
  116.3 2.5 %collective-permute-done.4.refs_5_ = bf16[1,3,256,128]{3,2,1,0:T(8,128)(2,1)S(1)} collective-permute-done((bf16[1,3,256,128]{3,2,1,0:T(8,128)(2,1)S(1)}, bf16[1,3,256,128]{3,2,1,0:T(8,128)(2,1)S(1)}, u32[]{:S(2)}, u32[]{:S(2)}) %collective-permute-start.4) | collective-permute-done | bytes 196640 | tf_op jit(solution)/shard_map/ppermute | solution.py:237
  118.8 2.5 %collective-permute-start.8 = (bf16[1,3,256,128]{3,2,1,0:T(8,128)(2,1)S(1)}, bf16[1,3,256,128]{3,2,1,0:T(8,128)(2,1)S(1)}, u32[]{:S(2)}, u32[]{:S(2)}) collective-permute-start(bf16[1,3,256,128]{3,2,1,0:T(8,128)(2,1)S(1)} %get-tuple-element.55), channel_id=1, source_target_pairs={{0,96},{32,64},{64,160},{96,128},{128,224},{160,192},{192,32},{224... | collective-permute-start | bytes 589832 | tf_op jit(solution)/shard_map/ppermute | solution.py:237
  121.3 2.5 %collective-permute-done.5.refs_6_ = bf16[1,3,256,128]{3,2,1,0:T(8,128)(2,1)S(1)} collective-permute-done((bf16[1,3,256,128]{3,2,1,0:T(8,128)(2,1)S(1)}, bf16[1,3,256,128]{3,2,1,0:T(8,128)(2,1)S(1)}, u32[]{:S(2)}, u32[]{:S(2)}) %collective-permute-start.5) | collective-permute-done | bytes 196640 | tf_op jit(solution)/shard_map/ppermute | solution.py:237
  124.5 3.4 %collective-permute-done.7.refs_8_ = bf16[1,3,256,128]{3,2,1,0:T(8,128)(2,1)S(1)} collective-permute-done((bf16[1,3,256,128]{3,2,1,0:T(8,128)(2,1)S(1)}, bf16[1,3,256,128]{3,2,1,0:T(8,128)(2,1)S(1)}, u32[]{:S(2)}, u32[]{:S(2)}) %collective-permute-start.7) | collective-permute-done | bytes 196640 | tf_op jit(solution)/shard_map/ppermute | solution.py:237
  127.9 4.0 %collective-permute-done.8.refs_9_ = bf16[1,3,256,128]{3,2,1,0:T(8,128)(2,1)S(1)} collective-permute-done((bf16[1,3,256,128]{3,2,1,0:T(8,128)(2,1)S(1)}, bf16[1,3,256,128]{3,2,1,0:T(8,128)(2,1)S(1)}, u32[]{:S(2)}, u32[]{:S(2)}) %collective-permute-start.8) | collective-permute-done | bytes 196640 | tf_op jit(solution)/shard_map/ppermute | solution.py:237
  131.9 2.1 %place_slots.1 = bf16[24,512,128]{2,1,0:T(8,128)(2,1)} custom-call(s32[1]{0:T(128)} %bitcast.me_ref, bf16[2,3,256,128]{3,2,1,0:T(8,128)(2,1)S(1)} %get-tuple-element.47.refs_0_, bf16[2,3,256,128]{3,2,1,0:T(8,128)(2,1)S(1)} %collective-permute-done.refs_1_, bf16[2,3,256,128]{3,2,1,0:T(8,128)(2,1)S(1)} %collective-permute-done.1.refs_2_, ...), custom_call_target="tpu_custom_call" | custom-call | bytes 6291456 | tf_op jit(solution)/shard_map/place_slots/pallas_call | solution.py:219
  (65 shorter events, 9.4 us)
Async XLA Ops:
  0.0 1.7 %copy-start = (bf16[3,3,128,128]{3,2,1,0:T(8,128)(2,1)S(1)}, bf16[3,3,128,128]{3,2,1,0:T(8,128)(2,1)}, u32[]{:S(2)}) copy-start(bf16[3,3,128,128]{3,2,1,0:T(8,128)(2,1)} %param.12) | copy-start | bytes 884740
  4.0 12.2 %copy-start.5 = (bf16[8,32,16,128]{3,2,1,0:T(8,128)(2,1)S(1)}, bf16[8,32,16,128]{3,2,1,0:T(8,128)(2,1)}, u32[]{:S(2)}) copy-start(bf16[8,32,16,128]{3,2,1,0:T(8,128)(2,1)} %param.9) | copy-start | bytes 3145732
  4.0 28.5 %all-to-all-start = ((bf16[32,64,128]{2,1,0:T(8,128)(2,1)}), bf16[32,64,128]{2,1,0:T(8,128)(2,1)S(1)}, u32[]{:S(2)}, u32[]{:S(2)}) async-start(bf16[32,64,128]{2,1,0:T(8,128)(2,1)} %bitcast.14), calls=%async_computation | async-start | bytes 1048576 | tf_op jit(solution)/shard_map/all_to_all | solution.py:271
  17.4 0.7 copy-start.8
  18.4 2.6 %copy-start.6 = (bf16[128,384]{1,0:T(8,128)(2,1)S(1)}, bf16[128,384]{1,0:T(8,128)(2,1)}, u32[]{:S(2)}) copy-start(bf16[128,384]{1,0:T(8,128)(2,1)} %param.13) | copy-start | bytes 294916
  20.7 17.2 %copy-start.1 = (bf16[128,512]{1,0:T(8,128)(2,1)S(1)}, bf16[128,512]{1,0:T(8,128)(2,1)}, u32[]{:S(2)}) copy-start(bf16[128,512]{1,0:T(8,128)(2,1)} %wup_ref.3) | copy-start | bytes 393220
  20.7 17.2 %copy-start.2 = (bf16[512,128]{1,0:T(8,128)(2,1)S(1)}, bf16[512,128]{1,0:T(8,128)(2,1)}, u32[]{:S(2)}) copy-start(bf16[512,128]{1,0:T(8,128)(2,1)} %wdown_ref.3) | copy-start | bytes 393220
  20.7 17.2 %copy-start.3 = (bf16[128,128]{1,0:T(8,128)(2,1)S(1)}, bf16[128,128]{1,0:T(8,128)(2,1)}, u32[]{:S(2)}) copy-start(bf16[128,128]{1,0:T(8,128)(2,1)} %wout_ref.3) | copy-start | bytes 98308
  20.7 17.2 %copy-start.4 = (f32[128]{0:T(128)S(1)}, f32[128]{0:T(128)}, u32[]{:S(2)}) copy-start(f32[128]{0:T(128)} %param.14) | copy-start | bytes 1540
  32.4 20.3 %all-to-all-start.2 = ((bf16[32,64,128]{2,1,0:T(8,128)(2,1)}), bf16[32,64,128]{2,1,0:T(8,128)(2,1)S(1)}, u32[]{:S(2)}, u32[]{:S(2)}) async-start(bf16[32,64,128]{2,1,0:T(8,128)(2,1)} %bitcast.21), calls=%async_computation.2 | async-start | bytes 1048576 | tf_op jit(solution)/shard_map/all_to_all | solution.py:271
  52.7 26.2 %all-to-all-start.1 = ((bf16[32,12,8,128]{3,2,1,0:T(8,128)(2,1)}), bf16[32,12,8,128]{3,2,1,0:T(8,128)(2,1)S(1)}, u32[]{:S(2)}, u32[]{:S(2)}) async-start(bf16[32,12,8,128]{3,2,1,0:T(8,128)(2,1)} %pool_attention.2), calls=%async_computation.1 | async-start | bytes 1572864 | tf_op jit(solution)/shard_map/all_to_all | solution.py:273
  71.5 14.1 %copy-start.7 = (s32[8,4]{0,1:T(4,128)S(1)}, s32[8,4]{0,1:T(4,128)}, u32[]{:S(2)}) copy-start(s32[8,4]{0,1:T(4,128)} %param.11) | copy-start | bytes 388
  78.8 26.4 %all-to-all-start.3 = ((bf16[32,12,8,128]{3,2,1,0:T(8,128)(2,1)}), bf16[32,12,8,128]{3,2,1,0:T(8,128)(2,1)S(1)}, u32[]{:S(2)}, u32[]{:S(2)}) async-start(bf16[32,12,8,128]{3,2,1,0:T(8,128)(2,1)} %pool_attention.3), calls=%async_computation.3 | async-start | bytes 1572864 | tf_op jit(solution)/shard_map/all_to_all | solution.py:273
  87.5 18.6 %collective-permute-start = (bf16[2,3,256,128]{3,2,1,0:T(8,128)(2,1)}, bf16[2,3,256,128]{3,2,1,0:T(8,128)(2,1)S(1)}, u32[]{:S(2)}, u32[]{:S(2)}) collective-permute-start(bf16[2,3,256,128]{3,2,1,0:T(8,128)(2,1)} %get-tuple-element.34), channel_id=1, source_target_pairs={{0,64},{32,96},{64,128},{96,160},{128,192},{160,224},{192,0},{224,... | collective-permute-start | bytes 1179656 | tf_op jit(solution)/shard_map/ppermute | solution.py:237
  88.7 17.6 %collective-permute-start.1 = (bf16[2,3,256,128]{3,2,1,0:T(8,128)(2,1)S(1)}, bf16[2,3,256,128]{3,2,1,0:T(8,128)(2,1)S(1)}, u32[]{:S(2)}, u32[]{:S(2)}) collective-permute-start(bf16[2,3,256,128]{3,2,1,0:T(8,128)(2,1)S(1)} %get-tuple-element.35), channel_id=1, source_target_pairs={{0,128},{32,160},{64,192},{96,224},{128,0},{160,32},{192,64},{224,... | collective-permute-start | bytes 1179656 | tf_op jit(solution)/shard_map/ppermute | solution.py:237
  91.1 16.4 %collective-permute-start.2 = (bf16[2,3,256,128]{3,2,1,0:T(8,128)(2,1)S(1)}, bf16[2,3,256,128]{3,2,1,0:T(8,128)(2,1)S(1)}, u32[]{:S(2)}, u32[]{:S(2)}) collective-permute-start(bf16[2,3,256,128]{3,2,1,0:T(8,128)(2,1)S(1)} %get-tuple-element.36), channel_id=1, source_target_pairs={{0,192},{32,224},{64,0},{96,32},{128,64},{160,96},{192,128},{224,1... | collective-permute-start | bytes 1179656 | tf_op jit(solution)/shard_map/ppermute | solution.py:237
  107.7 24.2 %collective-permute-start.3 = (bf16[4,3,256,128]{3,2,1,0:T(8,128)(2,1)S(1)}, bf16[4,3,256,128]{3,2,1,0:T(8,128)(2,1)S(1)}, u32[]{:S(2)}, u32[]{:S(2)}) collective-permute-start(bf16[4,3,256,128]{3,2,1,0:T(8,128)(2,1)S(1)} %pad_maximum_fusion), channel_id=1, source_target_pairs={{0,32},{32,0},{64,96},{96,64},{128,160},{160,128},{192,224},{224,1... | collective-permute-start | bytes 2359304 | tf_op jit(solution)/shard_map/ppermute | solution.py:237
  110.8 8.0 %collective-permute-start.4 = (bf16[1,3,256,128]{3,2,1,0:T(8,128)(2,1)S(1)}, bf16[1,3,256,128]{3,2,1,0:T(8,128)(2,1)S(1)}, u32[]{:S(2)}, u32[]{:S(2)}) collective-permute-start(bf16[1,3,256,128]{3,2,1,0:T(8,128)(2,1)S(1)} %get-tuple-element.51), channel_id=1, source_target_pairs={{0,128},{32,160},{64,192},{96,224},{128,0},{160,32},{192,64},{224,... | collective-permute-start | bytes 589832 | tf_op jit(solution)/shard_map/ppermute | solution.py:237
  113.6 10.2 %collective-permute-start.5 = (bf16[1,3,256,128]{3,2,1,0:T(8,128)(2,1)S(1)}, bf16[1,3,256,128]{3,2,1,0:T(8,128)(2,1)S(1)}, u32[]{:S(2)}, u32[]{:S(2)}) collective-permute-start(bf16[1,3,256,128]{3,2,1,0:T(8,128)(2,1)S(1)} %get-tuple-element.52), channel_id=1, source_target_pairs={{0,64},{32,96},{64,128},{96,160},{128,192},{160,224},{192,0},{224,... | collective-permute-start | bytes 589832 | tf_op jit(solution)/shard_map/ppermute | solution.py:237
  113.9 10.6 %collective-permute-start.6 = (bf16[1,3,256,128]{3,2,1,0:T(8,128)(2,1)S(1)}, bf16[1,3,256,128]{3,2,1,0:T(8,128)(2,1)S(1)}, u32[]{:S(2)}, u32[]{:S(2)}) collective-permute-start(bf16[1,3,256,128]{3,2,1,0:T(8,128)(2,1)S(1)} %get-tuple-element.53), channel_id=1, source_target_pairs={{0,192},{32,224},{64,0},{96,32},{128,64},{160,96},{192,128},{224,1... | collective-permute-start | bytes 589832 | tf_op jit(solution)/shard_map/ppermute | solution.py:237
  116.3 11.7 %collective-permute-start.7 = (bf16[1,3,256,128]{3,2,1,0:T(8,128)(2,1)S(1)}, bf16[1,3,256,128]{3,2,1,0:T(8,128)(2,1)S(1)}, u32[]{:S(2)}, u32[]{:S(2)}) collective-permute-start(bf16[1,3,256,128]{3,2,1,0:T(8,128)(2,1)S(1)} %get-tuple-element.54), channel_id=1, source_target_pairs={{0,160},{32,128},{64,224},{96,192},{128,32},{160,0},{192,96},{224,... | collective-permute-start | bytes 589832 | tf_op jit(solution)/shard_map/ppermute | solution.py:237
  118.8 13.1 %collective-permute-start.8 = (bf16[1,3,256,128]{3,2,1,0:T(8,128)(2,1)S(1)}, bf16[1,3,256,128]{3,2,1,0:T(8,128)(2,1)S(1)}, u32[]{:S(2)}, u32[]{:S(2)}) collective-permute-start(bf16[1,3,256,128]{3,2,1,0:T(8,128)(2,1)S(1)} %get-tuple-element.55), channel_id=1, source_target_pairs={{0,96},{32,64},{64,160},{96,128},{128,224},{160,192},{192,32},{224... | collective-permute-start | bytes 589832 | tf_op jit(solution)/shard_map/ppermute | solution.py:237
  123.8 8.1 %collective-permute-start.9 = (bf16[1,3,256,128]{3,2,1,0:T(8,128)(2,1)S(1)}, bf16[1,3,256,128]{3,2,1,0:T(8,128)(2,1)S(1)}, u32[]{:S(2)}, u32[]{:S(2)}) collective-permute-start(bf16[1,3,256,128]{3,2,1,0:T(8,128)(2,1)S(1)} %get-tuple-element.56), channel_id=1, source_target_pairs={{0,224},{32,192},{64,32},{96,0},{128,96},{160,64},{192,160},{224,1... | collective-permute-start | bytes 589832 | tf_op jit(solution)/shard_map/ppermute | solution.py:237
  124.5 7.4 %collective-permute-start.10 = (bf16[1,3,256,128]{3,2,1,0:T(8,128)(2,1)S(1)}, bf16[1,3,256,128]{3,2,1,0:T(8,128)(2,1)S(1)}, u32[]{:S(2)}, u32[]{:S(2)}) collective-permute-start(bf16[1,3,256,128]{3,2,1,0:T(8,128)(2,1)S(1)} %get-tuple-element.57), channel_id=1, source_target_pairs={{0,32},{32,0},{64,96},{96,64},{128,160},{160,128},{192,224},{224,1... | collective-permute-start | bytes 589832 | tf_op jit(solution)/shard_map/ppermute | solution.py:237

commit v5 on v4

--- a/solution.py
+++ b/solution.py
@@ -193,7 +193,7 @@
 
 
 def place_kernel(groups, slots, entries, me_ref, *refs):
-    pieces, out_ref, sem = refs[:-2], refs[-2], refs[-1]
+    pieces, out_ref, sem = refs, refs[-2], refs[-1]
     chip, core = me_ref[0] // 2, lax.rem(me_ref[0], 2)
     copies = []
     for piece, at, chunk, hop, flip in entries:
@@ -213,19 +213,21 @@
         copy.wait()
 
 
-def place(pieces, entries, me, groups, pixels):
+def place(pieces, entries, me, groups, pixels, onto=None):
     slots = pieces[0].shape[1]
-    vmem = pl.BlockSpec(memory_space=pltpu.VMEM)
+    vmem, anywhere = pl.BlockSpec(memory_space=pltpu.VMEM), pl.BlockSpec(memory_space=pl.ANY)
+    more = [] if onto is None else [onto]
     return pl.pallas_call(
         functools.partial(place_kernel, groups, slots, entries),
         out_shape=jax.ShapeDtypeStruct((slots * groups, pixels, C), BF),
-        in_specs=[pl.BlockSpec(memory_space=pltpu.SMEM)] + [vmem] * len(pieces),
-        out_specs=pl.BlockSpec(memory_space=pl.ANY),
+        in_specs=[pl.BlockSpec(memory_space=pltpu.SMEM)] + [vmem] * len(pieces) + [anywhere] * len(more),
+        out_specs=anywhere,
+        input_output_aliases={1 + len(pieces): 0} if more else {},
         scratch_shapes=[pltpu.SemaphoreType.DMA((len(entries) * slots,))],
         compiler_params=pltpu.CompilerParams(vmem_limit_bytes=32 * 2**20),
-        cost_estimate=pl.CostEstimate(flops=0, bytes_accessed=6 * 2**20, transcendentals=0),
+        cost_estimate=pl.CostEstimate(flops=0, bytes_accessed=3 * 2**20, transcendentals=0),
         name="place_slots",
-    )(me[None], *pieces)
+    )(me[None], *pieces, *more)
 
 
 def to_chip(value, hop, flip, groups):
@@ -286,10 +288,12 @@
             swapped = to_chip(jnp.stack([slab[1] for slab in landed]), 0, 1, groups)
             entries += [(len(pieces), at, of, hop, 1) for at, (_, of, hop) in enumerate(to_swap)]
             pieces.append(swapped)
+            placed = place(pieces, entries, me, groups, pixels)
+            pieces, entries = [], []
             for hop, flip in ((2, 0), (1, 0), (3, 0), (2, 1), (1, 1), (3, 1), (0, 1), (0, 0)):
                 entries.append((len(pieces), 0, chunk, hop, flip))
                 pieces.append(to_chip(packed[aim_list.index((hop, flip))], hop, flip, groups))
-    placed = place(pieces, entries, me, groups, pixels)
+    placed = place(pieces, entries, me, groups, pixels, placed)
     return placed.reshape(1, slots * groups, tile_rows, tile_cols, channels)
 
 

time: 135 us -> 134 us (level)
  transfers between devices with their start and end apart: 15 -> 15, of which waited for: 10 -> 10; matrix products, arithmetic and copies ran while one was open for 4% -> 4% of each run, Pallas kernels for 20% -> 21%
where the time goes in v5:
time: 134 us; the launch traced here: 133 us
  starting transfers between devices  47.4 us (35%)
  waiting for transfers between devices  46.9 us (35%)
  Pallas kernels  29.1 us (22%)
  matrix products  4.52 us (3%)
  local copies, waits for them, and re-layouts  3.2 us (2%)
  other arithmetic  1.74 us (1%)
    pallas_call x2, Pallas kernels, attention(): pl.pallas_call(functools.partial(attention_kernel, slots), out_shape=jax....  24.2 us
    all_to_all x2, waiting for transfers between devices, body(): lax.all_to_all(refined, 'band', split_axis=0, concat_axis=0, tiled=True)  20.3 us
    all_to_all x2, starting transfers between devices, body(): lax.all_to_all(hidden, 'band', split_axis=0, concat_axis=0, tiled=True)  17.4 us
    ppermute x11, starting transfers between devices, to_chip(): return lax.ppermute(value, 'group', pairs) if hop or flip else value  16.6 us
    all_to_all x2, waiting for transfers between devices, body(): lax.all_to_all(hidden, 'band', split_axis=0, concat_axis=0, tiled=True)  14 us
    all_to_all x2, starting transfers between devices, body(): lax.all_to_all(refined, 'band', split_axis=0, concat_axis=0, tiled=True)  13.5 us
    ppermute x11, waiting for transfers between devices, to_chip(): return lax.ppermute(value, 'group', pairs) if hop or flip else value  12.5 us
    conv_general_dilated x2, matrix products, conv_rows(): lax.conv_general_dilated(normed, conv_weight, (1, 1), ((1 - above, 1 - be...  4.52 us
  transfers between devices with their start and end apart: 15, of which 10 were waited for; matrix products, arithmetic and copies ran while one was open for 4% of the time, Pallas kernels for 21%

profile of v5, /device:TPU:1, one launch (start us, length us, event | category | flops | bytes accessed | tf_op | source)
XLA Modules:
  0.0 133.4 jit_solution(14074228168143552307)
XLA Ops:
  1.7 2.3 %fusion = bf16[8,16,16,128]{3,0,2,1:T(8,128)(2,1)} fusion(bf16[3,3,128,128]{3,2,1,0:T(8,128)(2,1)S(1)} %copy-done, f32[8,17,16,128]{3,0,2,1:T(8,128)S(1)} %copy_convert_fusion, f32[8,17,16]{0,2,1:T(8,128)S(1)} %add_rsqrt_fusion.1), kind=kOutput, calls=%fused_computation.2 | convolution fusion | flops 568950784 | bytes 3121152 | tf_op jit(solution)/shard_map/conv_general_dilated | solution.py:159
  4.0 12.2 %all-to-all-start.2 = ((bf16[32,64,128]{2,1,0:T(8,128)(2,1)}), bf16[32,64,128]{2,1,0:T(8,128)(2,1)S(1)}, u32[]{:S(2)}, u32[]{:S(2)}) async-start(bf16[32,64,128]{2,1,0:T(8,128)(2,1)} %bitcast.21), calls=%async_computation.2 | async-start | bytes 1048576 | tf_op jit(solution)/shard_map/all_to_all | solution.py:273
  18.5 2.2 %fusion.1 = bf16[8,16,16,128]{3,0,2,1:T(8,128)(2,1)} fusion(bf16[3,3,128,128]{3,2,1,0:T(8,128)(2,1)S(1)} %copy-done, f32[8,17,16,128]{3,0,2,1:T(8,128)S(1)} %slice_convert_fusion, f32[8,17,16]{0,2,1:T(8,128)S(1)} %add_rsqrt_fusion), kind=kOutput, calls=%fused_computation.3 | convolution fusion | flops 568950784 | bytes 3121152 | tf_op jit(solution)/shard_map/conv_general_dilated | solution.py:159
  21.1 11.4 %all-to-all-done.2.x_ref = bf16[32,64,128]{2,1,0:T(8,128)(2,1)S(1)} async-done(((bf16[32,64,128]{2,1,0:T(8,128)(2,1)}), bf16[32,64,128]{2,1,0:T(8,128)(2,1)S(1)}, u32[]{:S(2)}, u32[]{:S(2)}) %all-to-all-start.2) | async-done | bytes 524320 | tf_op jit(solution)/shard_map/all_to_all | solution.py:273
  32.4 5.2 %all-to-all-start = ((bf16[32,64,128]{2,1,0:T(8,128)(2,1)}), bf16[32,64,128]{2,1,0:T(8,128)(2,1)S(1)}, u32[]{:S(2)}, u32[]{:S(2)}) async-start(bf16[32,64,128]{2,1,0:T(8,128)(2,1)} %bitcast.14), calls=%async_computation | async-start | bytes 1048576 | tf_op jit(solution)/shard_map/all_to_all | solution.py:273
  37.9 12.1 %pool_attention.3 = bf16[32,12,8,128]{3,2,1,0:T(8,128)(2,1)} custom-call(s32[4]{0:T(128)S(1)} %bitcast_subtract_fusion.1.starts, s32[4]{0:T(128)S(1)} %bitcast.38, bf16[32,64,128]{2,1,0:T(8,128)(2,1)S(1)} %all-to-all-done.2.x_ref, bf16[128,256]{1,0:T(8,128)(2,1)S(1)} %pad_maximum_fusion.2.wqv_ref, bf16[128,128]{1,0:T(8,128)(2,1)S(1)} %bitcast.35, ...), custom_call_target="tpu_custom_call" | custom-call | flops 2097152000 | bytes 4194304 | tf_op jit(solution)/shard_map/pool_attention/pallas_call | solution.py:129
  50.0 2.7 %all-to-all-done.x_ref = bf16[32,64,128]{2,1,0:T(8,128)(2,1)S(1)} async-done(((bf16[32,64,128]{2,1,0:T(8,128)(2,1)}), bf16[32,64,128]{2,1,0:T(8,128)(2,1)S(1)}, u32[]{:S(2)}, u32[]{:S(2)}) %all-to-all-start) | async-done | bytes 524320 | tf_op jit(solution)/shard_map/all_to_all | solution.py:273
  52.7 6.7 %all-to-all-start.3 = ((bf16[32,12,8,128]{3,2,1,0:T(8,128)(2,1)}), bf16[32,12,8,128]{3,2,1,0:T(8,128)(2,1)S(1)}, u32[]{:S(2)}, u32[]{:S(2)}) async-start(bf16[32,12,8,128]{3,2,1,0:T(8,128)(2,1)} %pool_attention.3), calls=%async_computation.3 | async-start | bytes 1572864 | tf_op jit(solution)/shard_map/all_to_all | solution.py:275
  59.4 12.1 %pool_attention.2 = bf16[32,12,8,128]{3,2,1,0:T(8,128)(2,1)} custom-call(s32[4]{0:T(128)S(1)} %bitcast_subtract_fusion.1.starts, s32[4]{0:T(128)S(1)} %bitcast.39, bf16[32,64,128]{2,1,0:T(8,128)(2,1)S(1)} %all-to-all-done.x_ref, bf16[128,256]{1,0:T(8,128)(2,1)S(1)} %pad_maximum_fusion.2.wqv_ref, bf16[128,128]{1,0:T(8,128)(2,1)S(1)} %bitcast.36, ...), custom_call_target="tpu_custom_call" | custom-call | flops 2097152000 | bytes 4194304 | tf_op jit(solution)/shard_map/pool_attention/pallas_call | solution.py:129
  71.5 7.3 %all-to-all-done.3.y_ref = bf16[32,12,8,128]{3,2,1,0:T(8,128)(2,1)S(1)} async-done(((bf16[32,12,8,128]{3,2,1,0:T(8,128)(2,1)}), bf16[32,12,8,128]{3,2,1,0:T(8,128)(2,1)S(1)}, u32[]{:S(2)}, u32[]{:S(2)}) %all-to-all-start.3) | async-done | bytes 786464 | tf_op jit(solution)/shard_map/all_to_all | solution.py:275
  78.9 6.7 %all-to-all-start.1 = ((bf16[32,12,8,128]{3,2,1,0:T(8,128)(2,1)}), bf16[32,12,8,128]{3,2,1,0:T(8,128)(2,1)S(1)}, u32[]{:S(2)}, u32[]{:S(2)}) async-start(bf16[32,12,8,128]{3,2,1,0:T(8,128)(2,1)} %pool_attention.2), calls=%async_computation.1 | async-start | bytes 1572864 | tf_op jit(solution)/shard_map/all_to_all | solution.py:275
  86.0 1.5 %pack_slots.3 = (bf16[2,3,256,128]{3,2,1,0:T(8,128)(2,1)S(1)}, bf16[2,3,256,128]{3,2,1,0:T(8,128)(2,1)}, bf16[2,3,256,128]{3,2,1,0:T(8,128)(2,1)S(1)}, bf16[2,3,256,128]{3,2,1,0:T(8,128)(2,1)S(1)}) custom-call(s32[8]{0:T(128)S(1)} %select_reduce_fusion.clip_ref, bf16[32,12,8,128]{3,2,1,0:T(8,128)(2,1)S(1)} %all-to-all-done.3.y_ref), custom_call_target="tpu_custom_call" | custom-call | bytes 2097152 | tf_op jit(solution)/shard_map/pack_slots/pallas_call | solution.py:184
  88.7 2.5 %collective-permute-start.1 = (bf16[2,3,256,128]{3,2,1,0:T(8,128)(2,1)S(1)}, bf16[2,3,256,128]{3,2,1,0:T(8,128)(2,1)S(1)}, u32[]{:S(2)}, u32[]{:S(2)}) collective-permute-start(bf16[2,3,256,128]{3,2,1,0:T(8,128)(2,1)S(1)} %get-tuple-element.45), channel_id=1, source_target_pairs={{0,128},{32,160},{64,192},{96,224},{128,0},{160,32},{192,64},{224,... | collective-permute-start | bytes 1179656 | tf_op jit(solution)/shard_map/ppermute | solution.py:239
  92.3 13.0 %all-to-all-done.1.y_ref = bf16[32,12,8,128]{3,2,1,0:T(8,128)(2,1)S(1)} async-done(((bf16[32,12,8,128]{3,2,1,0:T(8,128)(2,1)}), bf16[32,12,8,128]{3,2,1,0:T(8,128)(2,1)S(1)}, u32[]{:S(2)}, u32[]{:S(2)}) %all-to-all-start.1) | async-done | bytes 786464 | tf_op jit(solution)/shard_map/all_to_all | solution.py:275
  107.8 3.1 %collective-permute-start.10 = (bf16[4,3,256,128]{3,2,1,0:T(8,128)(2,1)S(1)}, bf16[4,3,256,128]{3,2,1,0:T(8,128)(2,1)S(1)}, u32[]{:S(2)}, u32[]{:S(2)}) collective-permute-start(bf16[4,3,256,128]{3,2,1,0:T(8,128)(2,1)S(1)} %pad_maximum_fusion), channel_id=1, source_target_pairs={{0,32},{32,0},{64,96},{96,64},{128,160},{160,128},{192,224},{224,1... | collective-permute-start | bytes 2359304 | tf_op jit(solution)/shard_map/ppermute | solution.py:239
  110.9 2.8 %collective-permute-start.3 = (bf16[1,3,256,128]{3,2,1,0:T(8,128)(2,1)S(1)}, bf16[1,3,256,128]{3,2,1,0:T(8,128)(2,1)S(1)}, u32[]{:S(2)}, u32[]{:S(2)}) collective-permute-start(bf16[1,3,256,128]{3,2,1,0:T(8,128)(2,1)S(1)} %get-tuple-element.47), channel_id=1, source_target_pairs={{0,128},{32,160},{64,192},{96,224},{128,0},{160,32},{192,64},{224,... | collective-permute-start | bytes 589832 | tf_op jit(solution)/shard_map/ppermute | solution.py:239
  113.9 2.4 %collective-permute-start.5 = (bf16[1,3,256,128]{3,2,1,0:T(8,128)(2,1)S(1)}, bf16[1,3,256,128]{3,2,1,0:T(8,128)(2,1)S(1)}, u32[]{:S(2)}, u32[]{:S(2)}) collective-permute-start(bf16[1,3,256,128]{3,2,1,0:T(8,128)(2,1)S(1)} %get-tuple-element.49), channel_id=1, source_target_pairs={{0,192},{32,224},{64,0},{96,32},{128,64},{160,96},{192,128},{224,1... | collective-permute-start | bytes 589832 | tf_op jit(solution)/shard_map/ppermute | solution.py:239
  116.3 2.5 %collective-permute-done.3.refs_0_ = bf16[1,3,256,128]{3,2,1,0:T(8,128)(2,1)S(1)} collective-permute-done((bf16[1,3,256,128]{3,2,1,0:T(8,128)(2,1)S(1)}, bf16[1,3,256,128]{3,2,1,0:T(8,128)(2,1)S(1)}, u32[]{:S(2)}, u32[]{:S(2)}) %collective-permute-start.3) | collective-permute-done | bytes 196640 | tf_op jit(solution)/shard_map/ppermute | solution.py:239
  118.8 2.5 %collective-permute-start.7 = (bf16[1,3,256,128]{3,2,1,0:T(8,128)(2,1)S(1)}, bf16[1,3,256,128]{3,2,1,0:T(8,128)(2,1)S(1)}, u32[]{:S(2)}, u32[]{:S(2)}) collective-permute-start(bf16[1,3,256,128]{3,2,1,0:T(8,128)(2,1)S(1)} %get-tuple-element.51), channel_id=1, source_target_pairs={{0,96},{32,64},{64,160},{96,128},{128,224},{160,192},{192,32},{224... | collective-permute-start | bytes 589832 | tf_op jit(solution)/shard_map/ppermute | solution.py:239
  121.3 2.5 %collective-permute-done.4.refs_1_ = bf16[1,3,256,128]{3,2,1,0:T(8,128)(2,1)S(1)} collective-permute-done((bf16[1,3,256,128]{3,2,1,0:T(8,128)(2,1)S(1)}, bf16[1,3,256,128]{3,2,1,0:T(8,128)(2,1)S(1)}, u32[]{:S(2)}, u32[]{:S(2)}) %collective-permute-start.4) | collective-permute-done | bytes 196640 | tf_op jit(solution)/shard_map/ppermute | solution.py:239
  124.6 1.3 place_slots.2.refs_8_
  125.9 2.0 %collective-permute-done.6.refs_3_ = bf16[1,3,256,128]{3,2,1,0:T(8,128)(2,1)S(1)} collective-permute-done((bf16[1,3,256,128]{3,2,1,0:T(8,128)(2,1)S(1)}, bf16[1,3,256,128]{3,2,1,0:T(8,128)(2,1)S(1)}, u32[]{:S(2)}, u32[]{:S(2)}) %collective-permute-start.6) | collective-permute-done | bytes 196640 | tf_op jit(solution)/shard_map/ppermute | solution.py:239
  128.0 4.0 %collective-permute-done.7.refs_4_ = bf16[1,3,256,128]{3,2,1,0:T(8,128)(2,1)S(1)} collective-permute-done((bf16[1,3,256,128]{3,2,1,0:T(8,128)(2,1)S(1)}, bf16[1,3,256,128]{3,2,1,0:T(8,128)(2,1)S(1)}, u32[]{:S(2)}, u32[]{:S(2)}) %collective-permute-start.7) | collective-permute-done | bytes 196640 | tf_op jit(solution)/shard_map/ppermute | solution.py:239
  132.0 1.3 place_slots.3
  (66 shorter events, 10.6 us)
Async XLA Ops:
  0.0 1.7 %copy-start = (bf16[3,3,128,128]{3,2,1,0:T(8,128)(2,1)S(1)}, bf16[3,3,128,128]{3,2,1,0:T(8,128)(2,1)}, u32[]{:S(2)}) copy-start(bf16[3,3,128,128]{3,2,1,0:T(8,128)(2,1)} %param.12) | copy-start | bytes 884740
  4.0 12.2 %copy-start.5 = (bf16[8,32,16,128]{3,2,1,0:T(8,128)(2,1)S(1)}, bf16[8,32,16,128]{3,2,1,0:T(8,128)(2,1)}, u32[]{:S(2)}) copy-start(bf16[8,32,16,128]{3,2,1,0:T(8,128)(2,1)} %param.9) | copy-start | bytes 3145732
  4.0 28.5 %all-to-all-start.2 = ((bf16[32,64,128]{2,1,0:T(8,128)(2,1)}), bf16[32,64,128]{2,1,0:T(8,128)(2,1)S(1)}, u32[]{:S(2)}, u32[]{:S(2)}) async-start(bf16[32,64,128]{2,1,0:T(8,128)(2,1)} %bitcast.21), calls=%async_computation.2 | async-start | bytes 1048576 | tf_op jit(solution)/shard_map/all_to_all | solution.py:273
  17.4 0.7 copy-start.8
  18.4 2.6 %copy-start.6 = (bf16[128,384]{1,0:T(8,128)(2,1)S(1)}, bf16[128,384]{1,0:T(8,128)(2,1)}, u32[]{:S(2)}) copy-start(bf16[128,384]{1,0:T(8,128)(2,1)} %param.13) | copy-start | bytes 294916
  20.7 17.2 %copy-start.1 = (bf16[128,512]{1,0:T(8,128)(2,1)S(1)}, bf16[128,512]{1,0:T(8,128)(2,1)}, u32[]{:S(2)}) copy-start(bf16[128,512]{1,0:T(8,128)(2,1)} %wup_ref.3) | copy-start | bytes 393220
  20.7 17.2 %copy-start.2 = (bf16[512,128]{1,0:T(8,128)(2,1)S(1)}, bf16[512,128]{1,0:T(8,128)(2,1)}, u32[]{:S(2)}) copy-start(bf16[512,128]{1,0:T(8,128)(2,1)} %wdown_ref.3) | copy-start | bytes 393220
  20.7 17.2 %copy-start.3 = (bf16[128,128]{1,0:T(8,128)(2,1)S(1)}, bf16[128,128]{1,0:T(8,128)(2,1)}, u32[]{:S(2)}) copy-start(bf16[128,128]{1,0:T(8,128)(2,1)} %wout_ref.3) | copy-start | bytes 98308
  20.7 17.2 %copy-start.4 = (f32[128]{0:T(128)S(1)}, f32[128]{0:T(128)}, u32[]{:S(2)}) copy-start(f32[128]{0:T(128)} %param.14) | copy-start | bytes 1540
  32.4 20.3 %all-to-all-start = ((bf16[32,64,128]{2,1,0:T(8,128)(2,1)}), bf16[32,64,128]{2,1,0:T(8,128)(2,1)S(1)}, u32[]{:S(2)}, u32[]{:S(2)}) async-start(bf16[32,64,128]{2,1,0:T(8,128)(2,1)} %bitcast.14), calls=%async_computation | async-start | bytes 1048576 | tf_op jit(solution)/shard_map/all_to_all | solution.py:273
  52.7 26.2 %all-to-all-start.3 = ((bf16[32,12,8,128]{3,2,1,0:T(8,128)(2,1)}), bf16[32,12,8,128]{3,2,1,0:T(8,128)(2,1)S(1)}, u32[]{:S(2)}, u32[]{:S(2)}) async-start(bf16[32,12,8,128]{3,2,1,0:T(8,128)(2,1)} %pool_attention.3), calls=%async_computation.3 | async-start | bytes 1572864 | tf_op jit(solution)/shard_map/all_to_all | solution.py:275
  71.5 14.2 %copy-start.7 = (s32[8,4]{0,1:T(4,128)S(1)}, s32[8,4]{0,1:T(4,128)}, u32[]{:S(2)}) copy-start(s32[8,4]{0,1:T(4,128)} %param.11) | copy-start | bytes 388
  78.9 26.4 %all-to-all-start.1 = ((bf16[32,12,8,128]{3,2,1,0:T(8,128)(2,1)}), bf16[32,12,8,128]{3,2,1,0:T(8,128)(2,1)S(1)}, u32[]{:S(2)}, u32[]{:S(2)}) async-start(bf16[32,12,8,128]{3,2,1,0:T(8,128)(2,1)} %pool_attention.2), calls=%async_computation.1 | async-start | bytes 1572864 | tf_op jit(solution)/shard_map/all_to_all | solution.py:275
  87.5 18.6 %collective-permute-start = (bf16[2,3,256,128]{3,2,1,0:T(8,128)(2,1)}, bf16[2,3,256,128]{3,2,1,0:T(8,128)(2,1)S(1)}, u32[]{:S(2)}, u32[]{:S(2)}) collective-permute-start(bf16[2,3,256,128]{3,2,1,0:T(8,128)(2,1)} %get-tuple-element.44), channel_id=1, source_target_pairs={{0,64},{32,96},{64,128},{96,160},{128,192},{160,224},{192,0},{224,... | collective-permute-start | bytes 1179656 | tf_op jit(solution)/shard_map/ppermute | solution.py:239
  88.7 17.6 %collective-permute-start.1 = (bf16[2,3,256,128]{3,2,1,0:T(8,128)(2,1)S(1)}, bf16[2,3,256,128]{3,2,1,0:T(8,128)(2,1)S(1)}, u32[]{:S(2)}, u32[]{:S(2)}) collective-permute-start(bf16[2,3,256,128]{3,2,1,0:T(8,128)(2,1)S(1)} %get-tuple-element.45), channel_id=1, source_target_pairs={{0,128},{32,160},{64,192},{96,224},{128,0},{160,32},{192,64},{224,... | collective-permute-start | bytes 1179656 | tf_op jit(solution)/shard_map/ppermute | solution.py:239
  91.1 16.4 %collective-permute-start.2 = (bf16[2,3,256,128]{3,2,1,0:T(8,128)(2,1)S(1)}, bf16[2,3,256,128]{3,2,1,0:T(8,128)(2,1)S(1)}, u32[]{:S(2)}, u32[]{:S(2)}) collective-permute-start(bf16[2,3,256,128]{3,2,1,0:T(8,128)(2,1)S(1)} %get-tuple-element.46), channel_id=1, source_target_pairs={{0,192},{32,224},{64,0},{96,32},{128,64},{160,96},{192,128},{224,1... | collective-permute-start | bytes 1179656 | tf_op jit(solution)/shard_map/ppermute | solution.py:239
  107.8 16.8 %collective-permute-start.10 = (bf16[4,3,256,128]{3,2,1,0:T(8,128)(2,1)S(1)}, bf16[4,3,256,128]{3,2,1,0:T(8,128)(2,1)S(1)}, u32[]{:S(2)}, u32[]{:S(2)}) collective-permute-start(bf16[4,3,256,128]{3,2,1,0:T(8,128)(2,1)S(1)} %pad_maximum_fusion), channel_id=1, source_target_pairs={{0,32},{32,0},{64,96},{96,64},{128,160},{160,128},{192,224},{224,1... | collective-permute-start | bytes 2359304 | tf_op jit(solution)/shard_map/ppermute | solution.py:239
  110.9 8.0 %collective-permute-start.3 = (bf16[1,3,256,128]{3,2,1,0:T(8,128)(2,1)S(1)}, bf16[1,3,256,128]{3,2,1,0:T(8,128)(2,1)S(1)}, u32[]{:S(2)}, u32[]{:S(2)}) collective-permute-start(bf16[1,3,256,128]{3,2,1,0:T(8,128)(2,1)S(1)} %get-tuple-element.47), channel_id=1, source_target_pairs={{0,128},{32,160},{64,192},{96,224},{128,0},{160,32},{192,64},{224,... | collective-permute-start | bytes 589832 | tf_op jit(solution)/shard_map/ppermute | solution.py:239
  113.6 10.2 %collective-permute-start.4 = (bf16[1,3,256,128]{3,2,1,0:T(8,128)(2,1)S(1)}, bf16[1,3,256,128]{3,2,1,0:T(8,128)(2,1)S(1)}, u32[]{:S(2)}, u32[]{:S(2)}) collective-permute-start(bf16[1,3,256,128]{3,2,1,0:T(8,128)(2,1)S(1)} %get-tuple-element.48), channel_id=1, source_target_pairs={{0,64},{32,96},{64,128},{96,160},{128,192},{160,224},{192,0},{224,... | collective-permute-start | bytes 589832 | tf_op jit(solution)/shard_map/ppermute | solution.py:239
  113.9 12.0 %collective-permute-start.5 = (bf16[1,3,256,128]{3,2,1,0:T(8,128)(2,1)S(1)}, bf16[1,3,256,128]{3,2,1,0:T(8,128)(2,1)S(1)}, u32[]{:S(2)}, u32[]{:S(2)}) collective-permute-start(bf16[1,3,256,128]{3,2,1,0:T(8,128)(2,1)S(1)} %get-tuple-element.49), channel_id=1, source_target_pairs={{0,192},{32,224},{64,0},{96,32},{128,64},{160,96},{192,128},{224,1... | collective-permute-start | bytes 589832 | tf_op jit(solution)/shard_map/ppermute | solution.py:239
  116.3 11.7 %collective-permute-start.6 = (bf16[1,3,256,128]{3,2,1,0:T(8,128)(2,1)S(1)}, bf16[1,3,256,128]{3,2,1,0:T(8,128)(2,1)S(1)}, u32[]{:S(2)}, u32[]{:S(2)}) collective-permute-start(bf16[1,3,256,128]{3,2,1,0:T(8,128)(2,1)S(1)} %get-tuple-element.50), channel_id=1, source_target_pairs={{0,160},{32,128},{64,224},{96,192},{128,32},{160,0},{192,96},{224,... | collective-permute-start | bytes 589832 | tf_op jit(solution)/shard_map/ppermute | solution.py:239
  118.8 13.1 %collective-permute-start.7 = (bf16[1,3,256,128]{3,2,1,0:T(8,128)(2,1)S(1)}, bf16[1,3,256,128]{3,2,1,0:T(8,128)(2,1)S(1)}, u32[]{:S(2)}, u32[]{:S(2)}) collective-permute-start(bf16[1,3,256,128]{3,2,1,0:T(8,128)(2,1)S(1)} %get-tuple-element.51), channel_id=1, source_target_pairs={{0,96},{32,64},{64,160},{96,128},{128,224},{160,192},{192,32},{224... | collective-permute-start | bytes 589832 | tf_op jit(solution)/shard_map/ppermute | solution.py:239
  123.8 8.1 %collective-permute-start.8 = (bf16[1,3,256,128]{3,2,1,0:T(8,128)(2,1)S(1)}, bf16[1,3,256,128]{3,2,1,0:T(8,128)(2,1)S(1)}, u32[]{:S(2)}, u32[]{:S(2)}) collective-permute-start(bf16[1,3,256,128]{3,2,1,0:T(8,128)(2,1)S(1)} %get-tuple-element.52), channel_id=1, source_target_pairs={{0,224},{32,192},{64,32},{96,0},{128,96},{160,64},{192,160},{224,1... | collective-permute-start | bytes 589832 | tf_op jit(solution)/shard_map/ppermute | solution.py:239
  124.6 7.4 %collective-permute-start.9 = (bf16[1,3,256,128]{3,2,1,0:T(8,128)(2,1)S(1)}, bf16[1,3,256,128]{3,2,1,0:T(8,128)(2,1)S(1)}, u32[]{:S(2)}, u32[]{:S(2)}) collective-permute-start(bf16[1,3,256,128]{3,2,1,0:T(8,128)(2,1)S(1)} %get-tuple-element.53), channel_id=1, source_target_pairs={{0,32},{32,0},{64,96},{96,64},{128,160},{160,128},{192,224},{224,1... | collective-permute-start | bytes 589832 | tf_op jit(solution)/shard_map/ppermute | solution.py:239
